TPU v7x, 128 devices: a whole 4x4x4 slice. The times are simulated.
128 devices in a mesh: fsdp: 16 (over x, z_lo, core), ctx: 4 (over y), tp: 2 (over z_hi).
Axes of the slice: x: 4, y: 4, z: 4 (z_hi: 2, z_lo: 2; z = z_hi * 2 + z_lo), core: 2. Of those that a mesh axis runs over, the one named last changes fastest.
Arguments:
- tokens_in: bfloat16 [8192, 2048], P(('fsdp', 'ctx')), may hold values from -16 to 16
- documents: int32 [16, 512], P('fsdp'), may hold values from 0 to 126, as said below
- routes: int32 [8192, 6], P(('fsdp', 'ctx')), may hold values from 0 to 63, all different within a row; in each aligned block of 128 rows (0 to 127, 128 to 255, ...) at most 16 rows name the same one
- attn_gain: bfloat16 [2048], P(('fsdp', 'ctx')), may hold values from 0.5 to 1.5
- query_weight: bfloat16 [2048, 3072], P(('fsdp', 'ctx'), 'tp'), may hold values from -0.125 to 0.125
- latent_down: bfloat16 [2048, 576], P(('fsdp', 'ctx')), may hold values from -0.125 to 0.125
- latent_gain: bfloat16 [512], P(('fsdp', 'ctx')), may hold values from 0.5 to 1.5
- latent_up: bfloat16 [512, 4096], P(('fsdp', 'ctx'), 'tp'), may hold values from -0.25 to 0.25
- output_weight: bfloat16 [2048, 2048], P('tp', ('fsdp', 'ctx')), may hold values from -1.5 to 1.5
- ffn_gain: bfloat16 [2048], P(('fsdp', 'ctx')), may hold values from 0.5 to 1.5
- router: bfloat16 [2048, 64], P(('fsdp', 'ctx')), may hold values from -0.0625 to 0.0625
- shared_gate: bfloat16 [2048, 2816], P(('fsdp', 'ctx'), 'tp'), may hold values from -0.125 to 0.125
- shared_up: bfloat16 [2048, 2816], P(('fsdp', 'ctx'), 'tp'), may hold values from -0.125 to 0.125
- shared_down: bfloat16 [2816, 2048], P('tp', ('fsdp', 'ctx')), may hold values from -0.109375 to 0.109375
- expert_gate: bfloat16 [64, 2048, 1408], P(('fsdp', 'ctx'), None, 'tp'), may hold values from -0.125 to 0.125
- expert_up: bfloat16 [64, 2048, 1408], P(('fsdp', 'ctx'), None, 'tp'), may hold values from -0.125 to 0.125
- expert_down: bfloat16 [64, 1408, 2048], P(('fsdp', 'ctx'), 'tp'), may hold values from -4 to 4
- cotangent: bfloat16 [8192, 2048], P(('fsdp', 'ctx')), may hold values from -16 to 16
Outputs:
- layer_out: bfloat16 [8192, 2048], P(('fsdp', 'ctx'))
- input_grad: float32 [8192, 2048], P(('fsdp', 'ctx'))
- attn_gain_grad: float32 [2048], P(('fsdp', 'ctx'))
- query_weight_grad: float32 [2048, 3072], P(('fsdp', 'ctx'), 'tp')
- latent_down_grad: float32 [2048, 576], P(('fsdp', 'ctx'))
- latent_gain_grad: float32 [512], P(('fsdp', 'ctx'))
- latent_up_grad: float32 [512, 4096], P(('fsdp', 'ctx'), 'tp')
- output_weight_grad: float32 [2048, 2048], P('tp', ('fsdp', 'ctx'))
- ffn_gain_grad: float32 [2048], P(('fsdp', 'ctx'))
- router_grad: float32 [2048, 64], P(('fsdp', 'ctx'))
- shared_gate_grad: float32 [2048, 2816], P(('fsdp', 'ctx'), 'tp')
- shared_up_grad: float32 [2048, 2816], P(('fsdp', 'ctx'), 'tp')
- shared_down_grad: float32 [2816, 2048], P('tp', ('fsdp', 'ctx'))
- expert_gate_grad: float32 [64, 2048, 1408], P(('fsdp', 'ctx'), None, 'tp')
- expert_up_grad: float32 [64, 2048, 1408], P(('fsdp', 'ctx'), None, 'tp')
- expert_down_grad: float32 [64, 1408, 2048], P(('fsdp', 'ctx'), 'tp')
Inputs may be any that keep to these rules, and one draw needn't show every extreme that they name: `routes`: each row names 6 different experts; within each aligned block of 128 rows (the rows of one device) no expert is named more than 16 times, and in some block an expert is named exactly 16 times. `documents`: document numbers start at 0 in each row and never fall along it; each row has one document of 386 positions that begins before position 127, and every other position is a document of its own.
All inputs are finite; a program needn't handle non-finite values.
Results may differ from a plain program's by a relative error of at most 0.02.
Values may be sent and summed in bfloat16 or wider, within the bound.
No kernel may reach another device: no remote copies, remote signals or barrier semaphores. Data moves between devices by JAX's collectives and lax.ppermute only.
A program may use at most 256 MiB of HBM per device.

v0:
```python
import jax
import jax.numpy as jnp
from jax import lax
from jax.sharding import PartitionSpec as P

NOPE = 128
ROPE = 64
VDIM = 128
LATENT = 512


epsilon = 1e-06


def product(left, right):
    return jnp.dot(left, right, preferred_element_type=jnp.float32)


def rope_tables(positions, half_width):
    freq_steps = jnp.arange(half_width, dtype=jnp.float32)
    inverse = 10000.0 ** (-freq_steps / half_width)
    angles = positions.astype(jnp.float32)[:, None] * inverse[None, :]
    return (jnp.cos(angles), jnp.sin(angles))


def rotate(values, cosine_table, sine_table):
    half_width = values.shape[-1] // 2
    leading = values[..., :half_width]
    trailing = values[..., half_width:]
    return jnp.concatenate(
        [
            leading * cosine_table - trailing * sine_table,
            trailing * cosine_table + leading * sine_table,
        ],
        axis=-1,
    )


def doc_positions(doc_row):
    places = jnp.arange(doc_row.shape[0], dtype=jnp.int32)
    starts = jnp.concatenate([jnp.ones((1,), bool), doc_row[1:] != doc_row[:-1]])
    begins = lax.cummax(jnp.where(starts, places, 0), axis=0)
    return places - begins


def norm_back(gradient, normed, inverse, gain_vec):
    scaled = gradient * gain_vec
    return inverse * (scaled - normed * jnp.mean(scaled * normed, axis=1, keepdims=True))


def silu_parts(gate_lin):
    sigmoid_val = jax.nn.sigmoid(gate_lin)
    return (gate_lin * sigmoid_val, sigmoid_val * (1.0 + gate_lin * (1.0 - sigmoid_val)))


def shards(
    tokens_in,
    documents,
    routes,
    attn_gain,
    query_weight,
    latent_down,
    latent_gain,
    latent_up,
    output_weight,
    ffn_gain,
    router,
    shared_gate,
    shared_up,
    shared_down,
    expert_gate,
    expert_up,
    expert_down,
    cotangent,
):
    n_ctx = lax.axis_size("ctx")
    ctx_index = lax.axis_index("ctx")
    row_count = tokens_in.shape[0]
    width = tokens_in.shape[1]
    length = documents.shape[1]
    head_width = NOPE + ROPE
    heads_here = query_weight.shape[1] // head_width
    group_heads = heads_here // n_ctx
    score_scale = head_width ** (-0.5)
    top_count = routes.shape[1]
    gathered = (
        lax.all_gather(query_weight, ("fsdp", "ctx"), axis=0, tiled=True),
        lax.all_gather(latent_down, ("fsdp", "ctx"), axis=0, tiled=True),
        lax.all_gather(latent_up, ("fsdp", "ctx"), axis=0, tiled=True),
        lax.all_gather(output_weight, ("fsdp", "ctx"), axis=1, tiled=True),
        lax.all_gather(attn_gain, ("fsdp", "ctx"), axis=0, tiled=True),
        lax.all_gather(latent_gain, ("fsdp", "ctx"), axis=0, tiled=True),
    )
    query_all, down_all, up_all, out_all, gain_one, gain_lat = gathered
    gain_one = gain_one.astype(jnp.float32)
    gain_lat = gain_lat.astype(jnp.float32)
    tokens_f = tokens_in.astype(jnp.float32)
    inverse_one = lax.rsqrt(jnp.mean(tokens_f * tokens_f, axis=1, keepdims=True) + epsilon)
    normed_one = tokens_f * inverse_one
    attn_in = (normed_one * gain_one).astype(jnp.bfloat16)
    doc_row = documents[0]
    positions_all = doc_positions(doc_row)
    local_pos = lax.dynamic_slice_in_dim(positions_all, ctx_index * row_count, row_count)
    cosine_table, sine_table = rope_tables(local_pos, ROPE // 2)
    query_lin = product(attn_in, query_all).reshape(row_count, heads_here, head_width)
    query_loc = jnp.concatenate(
        [
            query_lin[..., :NOPE],
            rotate(query_lin[..., NOPE:], cosine_table[:, None], sine_table[:, None]),
        ],
        axis=-1,
    ).astype(jnp.bfloat16)
    compressed = product(attn_in, down_all)
    latent = compressed[:, :LATENT]
    inverse_lat = lax.rsqrt(jnp.mean(latent * latent, axis=1, keepdims=True) + epsilon)
    latent_normed = latent * inverse_lat
    latent_in = (latent_normed * gain_lat).astype(jnp.bfloat16)
    key_rope = rotate(compressed[:, LATENT:], cosine_table, sine_table).astype(jnp.bfloat16)
    keys_values = (
        product(latent_in, up_all)
        .astype(jnp.bfloat16)
        .reshape(row_count, n_ctx, group_heads, NOPE + VDIM)
    )
    query_send = query_loc.reshape(row_count, n_ctx, group_heads * head_width)
    key_nope = keys_values[..., :NOPE].reshape(row_count, n_ctx, group_heads * NOPE)
    value_part = keys_values[..., NOPE:].reshape(row_count, n_ctx, group_heads * VDIM)
    rope_copy = jnp.broadcast_to(key_rope[:, None, :], (row_count, n_ctx, ROPE))
    kv_send = jnp.concatenate([key_nope, value_part, rope_copy], axis=2)
    query_recv, kv_recv = (
        lax.all_to_all(query_send, "ctx", split_axis=1, concat_axis=0, tiled=True),
        lax.all_to_all(kv_send, "ctx", split_axis=1, concat_axis=0, tiled=True),
    )
    query_full = query_recv.reshape(length, group_heads, head_width)
    nope_full = kv_recv[:, 0, : group_heads * NOPE].reshape(length, group_heads, NOPE)
    value_full = kv_recv[:, 0, group_heads * NOPE : group_heads * (NOPE + VDIM)].reshape(
        length, group_heads, VDIM
    )
    rope_full = kv_recv[:, 0, group_heads * (NOPE + VDIM) :]
    key_full = jnp.concatenate(
        [nope_full, jnp.broadcast_to(rope_full[:, None, :], (length, group_heads, ROPE))], axis=-1
    )
    places = jnp.arange(length, dtype=jnp.int32)
    same_doc = (doc_row[:, None] == doc_row[None, :]) & (places[None, :] <= places[:, None])

    def score_block():
        raw_scores = jnp.einsum(
            "qhd,khd->hqk", query_full, key_full, preferred_element_type=jnp.float32
        )
        return jnp.where(same_doc[None], raw_scores * score_scale, -1e30)

    scores = score_block()
    row_max = jnp.max(scores, axis=2, keepdims=True)
    log_total = row_max + jnp.log(jnp.sum(jnp.exp(scores - row_max), axis=2, keepdims=True))
    probs_low = jnp.exp(scores - log_total).astype(jnp.bfloat16)
    attended = jnp.einsum(
        "hqk,khd->qhd", probs_low, value_full, preferred_element_type=jnp.float32
    ).astype(jnp.bfloat16)
    attended_back = lax.all_to_all(
        attended.reshape(length, 1, group_heads * VDIM),
        "ctx",
        split_axis=0,
        concat_axis=1,
        tiled=True,
    )
    mixed_heads = attended_back.reshape(row_count, heads_here * VDIM)
    attn_out = lax.psum(product(mixed_heads, out_all), "tp")
    resid = tokens_f + attn_out
    gain_two, router_all, sgate_all, supper_all, sdown_all = (
        lax.all_gather(ffn_gain, ("fsdp", "ctx"), axis=0, tiled=True),
        lax.all_gather(router, ("fsdp", "ctx"), axis=0, tiled=True),
        lax.all_gather(shared_gate, ("fsdp", "ctx"), axis=0, tiled=True),
        lax.all_gather(shared_up, ("fsdp", "ctx"), axis=0, tiled=True),
        lax.all_gather(shared_down, ("fsdp", "ctx"), axis=1, tiled=True),
    )
    gain_two = gain_two.astype(jnp.float32)
    inverse_two = lax.rsqrt(jnp.mean(resid * resid, axis=1, keepdims=True) + epsilon)
    normed_two = resid * inverse_two
    ffn_in = (normed_two * gain_two).astype(jnp.bfloat16)
    experts_count = router_all.shape[1]
    router_probs = jax.nn.softmax(product(ffn_in, router_all), axis=1)
    chosen = routes[:, :, None] == jnp.arange(experts_count, dtype=jnp.int32)[None, None, :]
    gates = jnp.sum(jnp.where(chosen, router_probs[:, None, :], 0.0), axis=2)
    shared_glin = product(ffn_in, sgate_all)
    shared_ulin = product(ffn_in, supper_all)
    shared_silu, shared_slope = silu_parts(shared_glin)
    shared_act = (shared_silu * shared_ulin).astype(jnp.bfloat16)
    shared_part = product(shared_act, sdown_all)
    capacity = max(2, 4 * top_count * row_count // (3 * experts_count))
    pair_expert = routes.reshape(-1)
    onehot = (pair_expert[:, None] == jnp.arange(experts_count, dtype=jnp.int32)[None, :]).astype(
        jnp.int32
    )
    slot_index = jnp.sum(jnp.cumsum(onehot, axis=0) * onehot, axis=1) - 1
    destination = pair_expert * capacity + slot_index
    pair_token = jnp.arange(row_count * top_count, dtype=jnp.int32) // top_count
    source = jnp.zeros((experts_count * capacity,), jnp.int32).at[destination].set(pair_token)
    filled = jnp.zeros((experts_count * capacity,), bool).at[destination].set(True)
    slot_gate = (
        jnp.zeros((experts_count * capacity,), jnp.float32).at[destination].set(gates.reshape(-1))
    )
    grad_f = cotangent.astype(jnp.float32)
    send_rows = jnp.where(filled[:, None], ffn_in[source], jnp.zeros((), jnp.bfloat16)).reshape(
        experts_count, capacity, width
    )
    send_grads = (
        (slot_gate[:, None] * grad_f[source])
        .astype(jnp.bfloat16)
        .reshape(experts_count, capacity, width)
    )
    recv_rows, recv_grads = (
        lax.all_to_all(send_rows, ("fsdp", "ctx"), split_axis=0, concat_axis=0, tiled=True),
        lax.all_to_all(send_grads, ("fsdp", "ctx"), split_axis=0, concat_axis=0, tiled=True),
    )
    expert_rows = recv_rows.reshape(-1, width)
    expert_dout = recv_grads.reshape(-1, width)
    egate_w = expert_gate[0]
    eupper_w = expert_up[0]
    edown_w = expert_down[0]
    expert_glin = product(expert_rows, egate_w)
    expert_ulin = product(expert_rows, eupper_w)
    expert_silu, expert_slope = silu_parts(expert_glin)
    expert_act = (expert_silu * expert_ulin).astype(jnp.bfloat16)
    expert_piece = product(expert_act, edown_w).astype(jnp.bfloat16)
    expert_dact = product(expert_dout, edown_w.T)
    expert_dgate = (expert_dact * expert_ulin * expert_slope).astype(jnp.bfloat16)
    expert_dup = (expert_dact * expert_silu).astype(jnp.bfloat16)
    expert_drows = (product(expert_dgate, egate_w.T) + product(expert_dup, eupper_w.T)).astype(
        jnp.bfloat16
    )
    expert_down_grad = product(expert_act.T, expert_dout)[None]
    expert_gate_grad = product(expert_rows.T, expert_dgate)[None]
    expert_up_grad = product(expert_rows.T, expert_dup)[None]
    back_out, back_drows = (
        lax.all_to_all(
            expert_piece.reshape(experts_count, capacity, width),
            ("fsdp", "ctx"),
            split_axis=0,
            concat_axis=0,
            tiled=True,
        ),
        lax.all_to_all(
            expert_drows.reshape(experts_count, capacity, width),
            ("fsdp", "ctx"),
            split_axis=0,
            concat_axis=0,
            tiled=True,
        ),
    )
    pair_out = (
        back_out.reshape(-1, width)[destination]
        .reshape(row_count, top_count, width)
        .astype(jnp.float32)
    )
    routed_part = jnp.sum(gates[:, :, None] * pair_out, axis=1)
    gate_part = jnp.sum(grad_f[:, None, :] * pair_out, axis=2)
    routed_drows = jnp.sum(
        back_drows.reshape(-1, width)[destination]
        .reshape(row_count, top_count, width)
        .astype(jnp.float32),
        axis=1,
    )
    shared_dact = product(cotangent, sdown_all.T)
    shared_dgate = (shared_dact * shared_ulin * shared_slope).astype(jnp.bfloat16)
    shared_dup = (shared_dact * shared_silu).astype(jnp.bfloat16)
    shared_drows = product(shared_dgate, sgate_all.T) + product(shared_dup, supper_all.T)
    shared_down_grad = product(shared_act.T, cotangent)
    shared_gate_grad = product(ffn_in.T, shared_dgate)
    shared_up_grad = product(ffn_in.T, shared_dup)
    ffn_total, ffn_back, gate_back = (
        lax.psum((shared_part + routed_part).astype(jnp.bfloat16), "tp").astype(jnp.float32),
        lax.psum((shared_drows + routed_drows).astype(jnp.bfloat16), "tp").astype(jnp.float32),
        lax.psum(gate_part.astype(jnp.bfloat16), "tp").astype(jnp.float32),
    )
    layer_out = (resid + ffn_total).astype(jnp.bfloat16)
    prob_grad = jnp.sum(jnp.where(chosen, gate_back[:, :, None], 0.0), axis=1)
    logit_grad = (
        router_probs * (prob_grad - jnp.sum(router_probs * prob_grad, axis=1, keepdims=True))
    ).astype(jnp.bfloat16)
    ffn_in_grad = ffn_back + product(logit_grad, router_all.T)
    router_grad = product(ffn_in.T, logit_grad)
    ffn_gain_grad = jnp.sum(ffn_in_grad * normed_two, axis=0)
    resid_grad = grad_f + norm_back(ffn_in_grad, normed_two, inverse_two, gain_two)
    ffn_grads = (
        lax.psum_scatter(ffn_gain_grad, ("fsdp", "ctx"), scatter_dimension=0, tiled=True),
        lax.psum_scatter(router_grad, ("fsdp", "ctx"), scatter_dimension=0, tiled=True),
        lax.psum_scatter(shared_gate_grad, ("fsdp", "ctx"), scatter_dimension=0, tiled=True),
        lax.psum_scatter(shared_up_grad, ("fsdp", "ctx"), scatter_dimension=0, tiled=True),
        lax.psum_scatter(shared_down_grad, ("fsdp", "ctx"), scatter_dimension=1, tiled=True),
    )
    regathered = (
        lax.all_gather(query_weight, ("fsdp", "ctx"), axis=0, tiled=True),
        lax.all_gather(latent_down, ("fsdp", "ctx"), axis=0, tiled=True),
        lax.all_gather(latent_up, ("fsdp", "ctx"), axis=0, tiled=True),
        lax.all_gather(output_weight, ("fsdp", "ctx"), axis=1, tiled=True),
        lax.all_gather(attn_gain, ("fsdp", "ctx"), axis=0, tiled=True),
        lax.all_gather(latent_gain, ("fsdp", "ctx"), axis=0, tiled=True),
    )
    query_use, down_use, up_use, out_use, gain_one_use, gain_lat_use = regathered
    gain_one_use = gain_one_use.astype(jnp.float32)
    gain_lat_use = gain_lat_use.astype(jnp.float32)
    resid_low = resid_grad.astype(jnp.bfloat16)
    output_weight_grad = product(mixed_heads.T, resid_low)
    heads_grad = product(resid_low, out_use.T).astype(jnp.bfloat16)
    grad_recv = lax.all_to_all(
        heads_grad.reshape(row_count, n_ctx, group_heads * VDIM),
        "ctx",
        split_axis=1,
        concat_axis=0,
        tiled=True,
    )
    attended_grad = grad_recv.reshape(length, group_heads, VDIM)
    attn_probs = jnp.exp(score_block() - log_total)
    probs_again = attn_probs.astype(jnp.bfloat16)
    value_grad = jnp.einsum(
        "hqk,qhd->khd", probs_again, attended_grad, preferred_element_type=jnp.float32
    ).astype(jnp.bfloat16)
    probs_grad = jnp.einsum(
        "qhd,khd->hqk", attended_grad, value_full, preferred_element_type=jnp.float32
    )
    score_grad = (
        attn_probs
        * (probs_grad - jnp.sum(attn_probs * probs_grad, axis=2, keepdims=True))
        * score_scale
    ).astype(jnp.bfloat16)
    query_grad = jnp.einsum(
        "hqk,khd->qhd", score_grad, key_full, preferred_element_type=jnp.float32
    ).astype(jnp.bfloat16)
    key_grad = jnp.einsum(
        "hqk,qhd->khd", score_grad, query_full, preferred_element_type=jnp.float32
    )
    key_nope_grad = key_grad[..., :NOPE].astype(jnp.bfloat16).reshape(length, group_heads * NOPE)
    key_rope_grad = jnp.sum(key_grad[..., NOPE:], axis=1).astype(jnp.bfloat16)
    query_back = query_grad.reshape(length, 1, group_heads * head_width)
    kv_back = jnp.concatenate(
        [key_nope_grad, value_grad.reshape(length, group_heads * VDIM), key_rope_grad], axis=1
    ).reshape(length, 1, -1)
    query_got, kv_got = (
        lax.all_to_all(query_back, "ctx", split_axis=0, concat_axis=1, tiled=True),
        lax.all_to_all(kv_back, "ctx", split_axis=0, concat_axis=1, tiled=True),
    )
    query_heads_grad = query_got.reshape(row_count, heads_here, head_width).astype(jnp.float32)
    query_lin_grad = (
        jnp.concatenate(
            [
                query_heads_grad[..., :NOPE],
                rotate(query_heads_grad[..., NOPE:], cosine_table[:, None], -sine_table[:, None]),
            ],
            axis=-1,
        )
        .astype(jnp.bfloat16)
        .reshape(row_count, heads_here * head_width)
    )
    query_weight_grad = product(attn_in.T, query_lin_grad)
    attn_in_part = product(query_lin_grad, query_use.T)
    nope_got = kv_got[:, :, : group_heads * NOPE].reshape(row_count, n_ctx, group_heads, NOPE)
    value_got = kv_got[:, :, group_heads * NOPE : group_heads * (NOPE + VDIM)].reshape(
        row_count, n_ctx, group_heads, VDIM
    )
    kv_grad = jnp.concatenate([nope_got, value_got], axis=-1).reshape(
        row_count, heads_here * (NOPE + VDIM)
    )
    latent_up_grad = product(latent_in.T, kv_grad)
    latent_part = product(kv_grad, up_use.T)
    rope_part = rotate(
        jnp.sum(kv_got[:, :, group_heads * (NOPE + VDIM) :].astype(jnp.float32), axis=1),
        cosine_table,
        -sine_table,
    )
    attn_in_sum, latent_sum, rope_sum = (
        lax.psum(attn_in_part.astype(jnp.bfloat16), "tp").astype(jnp.float32),
        lax.psum(latent_part.astype(jnp.bfloat16), "tp").astype(jnp.float32),
        lax.psum(rope_part.astype(jnp.bfloat16), "tp").astype(jnp.float32),
    )
    latent_gain_grad = jnp.sum(latent_sum * latent_normed, axis=0)
    compressed_grad = jnp.concatenate(
        [norm_back(latent_sum, latent_normed, inverse_lat, gain_lat_use), rope_sum], axis=1
    ).astype(jnp.bfloat16)
    latent_down_grad = product(attn_in.T, compressed_grad)
    attn_in_grad = attn_in_sum + product(compressed_grad, down_use.T)
    attn_gain_grad = jnp.sum(attn_in_grad * normed_one, axis=0)
    input_grad = resid_grad + norm_back(attn_in_grad, normed_one, inverse_one, gain_one_use)
    attn_grads = (
        lax.psum_scatter(query_weight_grad, ("fsdp", "ctx"), scatter_dimension=0, tiled=True),
        lax.psum_scatter(latent_down_grad, ("fsdp", "ctx"), scatter_dimension=0, tiled=True),
        lax.psum_scatter(latent_up_grad, ("fsdp", "ctx"), scatter_dimension=0, tiled=True),
        lax.psum_scatter(output_weight_grad, ("fsdp", "ctx"), scatter_dimension=1, tiled=True),
        lax.psum_scatter(attn_gain_grad, ("fsdp", "ctx"), scatter_dimension=0, tiled=True),
        lax.psum_scatter(latent_gain_grad, ("fsdp", "ctx"), scatter_dimension=0, tiled=True),
    )
    return (
        layer_out,
        input_grad,
        attn_grads[4],
        attn_grads[0],
        attn_grads[1],
        attn_grads[5],
        attn_grads[2],
        attn_grads[3],
        ffn_grads[0],
        ffn_grads[1],
        ffn_grads[2],
        ffn_grads[3],
        ffn_grads[4],
        expert_gate_grad,
        expert_up_grad,
        expert_down_grad,
    )


def solution(mesh):
    in_specs = (
        P(("fsdp", "ctx"), None),
        P("fsdp", None),
        P(("fsdp", "ctx"), None),
        P(("fsdp", "ctx")),
        P(("fsdp", "ctx"), "tp"),
        P(("fsdp", "ctx"), None),
        P(("fsdp", "ctx")),
        P(("fsdp", "ctx"), "tp"),
        P("tp", ("fsdp", "ctx")),
        P(("fsdp", "ctx")),
        P(("fsdp", "ctx"), None),
        P(("fsdp", "ctx"), "tp"),
        P(("fsdp", "ctx"), "tp"),
        P("tp", ("fsdp", "ctx")),
        P(("fsdp", "ctx"), None, "tp"),
        P(("fsdp", "ctx"), None, "tp"),
        P(("fsdp", "ctx"), "tp", None),
        P(("fsdp", "ctx"), None),
    )
    out_specs = (
        P(("fsdp", "ctx"), None),
        P(("fsdp", "ctx"), None),
        P(("fsdp", "ctx")),
        P(("fsdp", "ctx"), "tp"),
        P(("fsdp", "ctx"), None),
        P(("fsdp", "ctx")),
        P(("fsdp", "ctx"), "tp"),
        P("tp", ("fsdp", "ctx")),
        P(("fsdp", "ctx")),
        P(("fsdp", "ctx"), None),
        P(("fsdp", "ctx"), "tp"),
        P(("fsdp", "ctx"), "tp"),
        P("tp", ("fsdp", "ctx")),
        P(("fsdp", "ctx"), None, "tp"),
        P(("fsdp", "ctx"), None, "tp"),
        P(("fsdp", "ctx"), "tp", None),
    )
    return jax.shard_map(shards, mesh=mesh, in_specs=in_specs, out_specs=out_specs, check_vma=False)
```

profile of v0, /device:TPU:1, one launch (start us, length us, event | category | flops | bytes accessed | tf_op | source)
XLA Modules:
  0.0 3942.0 jit_solution(235857281752153974)
XLA Ops:
  15.2 143.3 %all-reduce.7 = (bf16[2048]{0:T(1024)(128)(2,1)S(1)}, bf16[512]{0:T(512)(128)(2,1)S(1)}, bf16[2048]{0:T(1024)(128)(2,1)S(1)}) all-reduce(bf16[2048]{0:T(1024)(128)(2,1)S(1)} %dynamic-update-slice, bf16[512]{0:T(512)(128)(2,1)S(1)} %dynamic-update-slice.1, ...), channel_id=1, replica_groups=mesh['fsdp'=16,'ctx'=4,'tp'=2] {'fsdp','ctx'}, use_global_device_ids=true, to_apply=%add | all-reduce | flops 4608 | bytes 18432
  161.4 10.1 all-gather.8.cloned.1.call-done
  174.6 156.1 %all-gather.10.cloned.1.call-done = bf16[512,2048]{1,0:T(8,128)(2,1)} async-done(((bf16[8,2048]{1,0:T(8,128)(2,1)}), bf16[512,2048]{1,0:T(8,128)(2,1)}) %all-gather.10.cloned.1.call-update) | async-done | bytes 2097168 | tf_op jit(solution)/shard_map/all_gather | solution.py:89
  349.7 10.5 all-to-all-done
  362.1 134.9 %all-gather.12.cloned.1.call-done = bf16[2048,1536]{1,0:T(8,128)(2,1)} async-done(((bf16[32,1536]{1,0:T(8,128)(2,1)}), bf16[2048,1536]{1,0:T(8,128)(2,1)}) %all-gather.12.cloned.1.call-update) | async-done | bytes 6291472 | tf_op jit(solution)/shard_map/all_gather | solution.py:87
  531.9 10.9 all_to_all.110
  548.2 113.2 %all-gather.14.cloned.1.call-done = bf16[1024,2048]{0,1:T(8,128)(2,1)} async-done(((bf16[1024,32]{0,1:T(8,128)(2,1)}), bf16[1024,2048]{0,1:T(8,128)(2,1)}) %all-gather.14.cloned.1.call-update) | async-done | bytes 4194320 | tf_op jit(solution)/shard_map/all_gather | solution.py:90
  682.6 33.4 all-reduce.13.cloned.1.call-done
  739.4 10.2 gather_fusion.2
  749.7 169.9 %all_gather.49 = bf16[2048,64]{1,0:T(8,128)(2,1)S(1)} all-gather(bf16[32,64]{1,0:T(8,128)(2,1)S(1)} %copy-done.47), channel_id=1, replica_groups=mesh['fsdp'=16,'ctx'=4,'tp'=2] {'fsdp','ctx'}, dimensions={0}, use_global_device_ids=true | all-gather | bytes 266240 | tf_op jit(solution)/shard_map/all_gather | solution.py:170
  931.9 11.8 all-to-all-start.5
  943.8 11.1 all-gather.20.cloned.1.call-start
  969.8 29.8 all-to-all-done.5
  999.6 8.4 multiply_convert_fusion.1
  1017.0 8.4 all-to-all-start.6
  1031.8 47.8 %all-to-all-done.6 = bf16[64,16,2048]{2,1,0:T(8,128)(2,1)} async-done(((bf16[64,16,2048]{2,1,0:T(8,128)(2,1)}), bf16[64,16,2048]{2,1,0:T(8,128)(2,1)}, u32[]{:S(2)}, u32[]{:S(2)}) %all-to-all-start.6) | async-done | bytes 4194336 | tf_op jit(solution)/shard_map/all_to_all | solution.py:241
  1079.6 8.9 all-to-all-start.4
  1092.7 92.4 %all-gather.18.cloned.1.call-done = bf16[2048,1408]{1,0:T(8,128)(2,1)} async-done(((bf16[32,1408]{1,0:T(8,128)(2,1)}), bf16[2048,1408]{1,0:T(8,128)(2,1)}) %all-gather.18.cloned.1.call-update) | async-done | bytes 5767184 | tf_op jit(solution)/shard_map/all_gather | solution.py:172
  1189.6 165.6 %all-gather.20.cloned.1.call-done = bf16[1408,2048]{0,1:T(8,128)(2,1)} async-done(((bf16[1408,32]{0,1:T(8,128)(2,1)}), bf16[1408,2048]{0,1:T(8,128)(2,1)}) %all-gather.20.cloned.1.call-update) | async-done | bytes 5767184 | tf_op jit(solution)/shard_map/all_gather | solution.py:173
  1364.8 9.8 gather_fusion.3
  1392.7 9.8 gather_fusion.1
  1432.7 9.4 all_to_all.111
  1514.9 41.9 %all-reduce.17.cloned.1.call-done = (bf16[128,2048]{1,0:T(8,128)(2,1)}, bf16[128,2048]{1,0:T(8,128)(2,1)}, bf16[128,512]{0,1:T(8,128)(2,1)}) async-done(((bf16[128,2048]{1,0:T(8,128)(2,1)}, bf16[128,2048]{1,0:T(8,128)(2,1)}, bf16[128,512]{0,1:T(8,128)(2,1)}), (bf16[128,2048]{1,0:T(8,128)(2,1)}, bf16[128,2048]{1,0:T(8,128)(2,1)}, bf16[128,512]{0,1:T(8,128)(2,1)})) %all-reduce.17.cloned.1.call-update) | async-done | bytes 1179664 | tf_op jit(solution)/shard_map/psum | solution.py:270
  1597.7 8.4 convolution_bitcast_fusion.2
  1622.7 273.7 %all-reduce.6 = (f32[2048]{0:T(1024)S(1)}, f32[512]{0:T(512)S(1)}, f32[2048]{0:T(1024)S(1)}) all-reduce(f32[2048]{0:T(1024)S(1)} %get-tuple-element.20, f32[512]{0:T(512)S(1)} %get-tuple-element.22, f32[2048]{0:T(1024)S(1)} %get-tuple-element.18), channel_id=2, replica_groups=mesh['fsdp'=16,'ctx'=4,'tp'=2] {'fsdp','ctx'}, use_global_device_ids=true, to_apply=%region_35.36.clone | all-reduce | flops 4608 | bytes 36864
  1903.4 224.8 %reduce-scatter.13.cloned.1.call-done = f32[8,2048]{1,0:T(8,128)} async-done(((f32[512,2048]{1,0:T(8,128)}), f32[8,2048]{1,0:T(8,128)}) %reduce-scatter.13.cloned.1.call-update) | async-done | bytes 65552 | tf_op jit(solution)/shard_map/reduce_scatter | solution.py:385
  2128.2 291.6 %reduce-scatter.11.cloned.1.call-done = f32[32,576]{1,0:T(8,128)} async-done(((f32[2048,576]{1,0:T(8,128)}), f32[32,576]{1,0:T(8,128)}) %reduce-scatter.11.cloned.1.call-update) | async-done | bytes 73744 | tf_op jit(solution)/shard_map/reduce_scatter | solution.py:384
  2419.8 304.4 %reduce-scatter.19.cloned.1.call-done = f32[32,1408]{1,0:T(8,128)} async-done(((f32[2048,1408]{1,0:T(8,128)}), f32[32,1408]{1,0:T(8,128)}) %reduce-scatter.19.cloned.1.call-update) | async-done | bytes 180240 | tf_op jit(solution)/shard_map/reduce_scatter | solution.py:286
  2724.2 303.7 %reduce-scatter.21.cloned.1.call-done = f32[32,1408]{1,0:T(8,128)} async-done(((f32[2048,1408]{1,0:T(8,128)}), f32[32,1408]{1,0:T(8,128)}) %reduce-scatter.21.cloned.1.call-update) | async-done | bytes 180240 | tf_op jit(solution)/shard_map/reduce_scatter | solution.py:287
  3027.9 302.8 %reduce-scatter.23.cloned.1.call-done = f32[1408,32]{0,1:T(8,128)} async-done(((f32[1408,2048]{0,1:T(8,128)}), f32[1408,32]{0,1:T(8,128)}) %reduce-scatter.23.cloned.1.call-update) | async-done | bytes 180240 | tf_op jit(solution)/shard_map/reduce_scatter | solution.py:288
  3330.7 298.1 %reduce-scatter.15.cloned.1.call-done = f32[1024,32]{0,1:T(8,128)} async-done(((f32[1024,2048]{0,1:T(8,128)}), f32[1024,32]{0,1:T(8,128)}) %reduce-scatter.15.cloned.1.call-update) | async-done | bytes 131088 | tf_op jit(solution)/shard_map/reduce_scatter | solution.py:386
  3628.8 305.9 %reduce-scatter.9.cloned.1.call-done = f32[32,1536]{1,0:T(8,128)} async-done(((f32[2048,1536]{1,0:T(8,128)}), f32[32,1536]{1,0:T(8,128)}) %reduce-scatter.9.cloned.1.call-update) | async-done | bytes 196624 | tf_op jit(solution)/shard_map/reduce_scatter | solution.py:383
  (350 shorter events, 362.6 us)
Async XLA Ops:
  7.2 992.5 %copy-start = (bf16[1,704,2048]{2,1,0:T(8,128)(2,1)S(1)}, bf16[1,704,2048]{2,1,0:T(8,128)(2,1)}, u32[]{:S(2)}) copy-start(bf16[1,704,2048]{2,1,0:T(8,128)(2,1)} %param.34) | copy-start | bytes 8650756
  7.2 164.3 %all-gather.8.cloned.1.call-start = ((), (), s32[]{:S(2)}) async-start(), calls=%async_computation.18 | async-start | bytes 2662400 | tf_op jit(solution)/shard_map/all_gather | solution.py:88
  7.9 322.8 %all-gather.10.cloned.1.call-start = ((), (), s32[]{:S(2)}) async-start(), calls=%async_computation.19 | async-start | bytes 2129920 | tf_op jit(solution)/shard_map/all_gather | solution.py:89
  8.7 488.4 %all-gather.12.cloned.1.call-start = ((), (), s32[]{:S(2)}) async-start(), calls=%async_computation.20 | async-start | bytes 6389760 | tf_op jit(solution)/shard_map/all_gather | solution.py:87
  9.4 652.0 %all-gather.14.cloned.1.call-start = ((), (), s32[]{:S(2)}) async-start(), calls=%async_computation.21 | async-start | bytes 4259840 | tf_op jit(solution)/shard_map/all_gather | solution.py:90
  158.5 338.6 %copy-start.31 = (f32[2048]{0:T(1024)}, f32[2048]{0:T(1024)S(1)}, u32[]{:S(2)}) copy-start(f32[2048]{0:T(1024)S(1)} %convert_element_type.186) | copy-start | bytes 24580
  161.4 335.7 %copy-start.41 = (f32[128]{0:T(128)}, f32[128]{0:T(128)S(1)}, u32[]{:S(2)}) copy-start(f32[128]{0:T(128)S(1)} %add_rsqrt_fusion.2) | copy-start | bytes 1540
  344.6 15.6 all-to-all-start
  503.4 13.7 all-to-all-start.1
  508.2 207.8 %all-reduce.13.cloned.1.call-start = ((), (), s32[]{:S(2)}) async-start(), calls=%async_computation.22 | async-start | bytes 2097152 | tf_op jit(solution)/shard_map/psum | solution.py:166
  666.2 422.8 %all-gather.16.cloned.1.call-start = ((), (), s32[]{:S(2)}) async-start(), calls=%async_computation.23 | async-start | bytes 5857280 | tf_op jit(solution)/shard_map/all_gather | solution.py:171
  666.8 518.3 %all-gather.18.cloned.1.call-start = ((), (), s32[]{:S(2)}) async-start(), calls=%async_computation.24 | async-start | bytes 5857280 | tf_op jit(solution)/shard_map/all_gather | solution.py:172
  729.1 202.8 %all-to-all-start.3 = ((bf16[64,16,2048]{2,1,0:T(8,128)(2,1)}), bf16[64,16,2048]{2,1,0:T(8,128)(2,1)}, u32[]{:S(2)}, u32[]{:S(2)}) async-start(bf16[64,16,2048]{2,1,0:T(8,128)(2,1)} %broadcast_select_fusion), calls=%async_computation.3 | async-start | bytes 8388608 | tf_op jit(solution)/shard_map/all_to_all | solution.py:211
  931.9 67.7 %all-to-all-start.5 = ((bf16[64,16,2048]{2,1,0:T(8,128)(2,1)}), bf16[64,16,2048]{2,1,0:T(8,128)(2,1)}, u32[]{:S(2)}, u32[]{:S(2)}) async-start(bf16[64,16,2048]{2,1,0:T(8,128)(2,1)} %multiply_convert_fusion), calls=%async_computation.5 | async-start | bytes 8388608 | tf_op jit(solution)/shard_map/all_to_all | solution.py:212
  943.8 411.4 %all-gather.20.cloned.1.call-start = ((), (), s32[]{:S(2)}) async-start(), calls=%async_computation.25 | async-start | bytes 5857280 | tf_op jit(solution)/shard_map/all_gather | solution.py:173
  1017.0 62.6 %all-to-all-start.6 = ((bf16[64,16,2048]{2,1,0:T(8,128)(2,1)}), bf16[64,16,2048]{2,1,0:T(8,128)(2,1)}, u32[]{:S(2)}, u32[]{:S(2)}) async-start(bf16[64,16,2048]{2,1,0:T(8,128)(2,1)} %bitcast.180), calls=%async_computation.6 | async-start | bytes 8388608 | tf_op jit(solution)/shard_map/all_to_all | solution.py:241
  1079.6 313.1 %all-to-all-start.4 = ((bf16[64,16,2048]{2,1,0:T(8,128)(2,1)}), bf16[64,16,2048]{2,1,0:T(8,128)(2,1)}, u32[]{:S(2)}, u32[]{:S(2)}) async-start(bf16[64,16,2048]{2,1,0:T(8,128)(2,1)} %bitcast.179), calls=%async_computation.4 | async-start | bytes 8388608 | tf_op jit(solution)/shard_map/all_to_all | solution.py:234
  1088.5 340.7 %all-reduce.15.cloned.1.call-start = ((), (), s32[]{:S(2)}) async-start(), calls=%async_computation.26 | async-start | bytes 1048576 | tf_op jit(solution)/shard_map/psum | solution.py:271
  1092.7 262.5 %copy-start.17 = (bf16[128,2048]{1,0:T(8,128)(2,1)S(1)}, bf16[128,2048]{1,0:T(8,128)(2,1)}, u32[]{:S(2)}) copy-start(bf16[128,2048]{1,0:T(8,128)(2,1)} %param.35) | copy-start | bytes 1572868
  1459.6 15.5 all-to-all-start.8
  1475.1 13.1 all-to-all-start.9
  1479.3 77.6 %all-reduce.17.cloned.1.call-start = ((), (), s32[]{:S(2)}) async-start(), calls=%async_computation.35 | async-start | bytes 2359296 | tf_op jit(solution)/shard_map/psum | solution.py:270
  1503.5 399.9 %reduce-scatter.17.cloned.1.call-start = ((), (), s32[]{:S(2)}) async-start(), calls=%async_computation.31 | async-start | bytes 1064960 | tf_op jit(solution)/shard_map/reduce_scatter | solution.py:285
  1504.9 623.3 %reduce-scatter.13.cloned.1.call-start = ((), (), s32[]{:S(2)}) async-start(), calls=%async_computation.29 | async-start | bytes 4259840 | tf_op jit(solution)/shard_map/reduce_scatter | solution.py:385
  1508.1 911.7 %reduce-scatter.11.cloned.1.call-start = ((), (), s32[]{:S(2)}) async-start(), calls=%async_computation.28 | async-start | bytes 5324800 | tf_op jit(solution)/shard_map/reduce_scatter | solution.py:384
  1562.4 1161.9 %reduce-scatter.19.cloned.1.call-start = ((), (), s32[]{:S(2)}) async-start(), calls=%async_computation.32 | async-start | bytes 11714560 | tf_op jit(solution)/shard_map/reduce_scatter | solution.py:286
  1569.2 1458.7 %reduce-scatter.21.cloned.1.call-start = ((), (), s32[]{:S(2)}) async-start(), calls=%async_computation.33 | async-start | bytes 11714560 | tf_op jit(solution)/shard_map/reduce_scatter | solution.py:287
  1576.1 1754.6 %reduce-scatter.23.cloned.1.call-start = ((), (), s32[]{:S(2)}) async-start(), calls=%async_computation.34 | async-start | bytes 11714560 | tf_op jit(solution)/shard_map/reduce_scatter | solution.py:288
  1583.0 2045.7 %reduce-scatter.15.cloned.1.call-start = ((), (), s32[]{:S(2)}) async-start(), calls=%async_computation.30 | async-start | bytes 8519680 | tf_op jit(solution)/shard_map/reduce_scatter | solution.py:386
  1588.9 2345.8 %reduce-scatter.9.cloned.1.call-start = ((), (), s32[]{:S(2)}) async-start(), calls=%async_computation.27 | async-start | bytes 12779520 | tf_op jit(solution)/shard_map/reduce_scatter | solution.py:383
  1620.6 279.9 %copy-start.5 = (bf16[128,2048]{1,0:T(8,128)(2,1)S(1)}, bf16[128,2048]{1,0:T(8,128)(2,1)}, u32[]{:S(2)}) copy-start(bf16[128,2048]{1,0:T(8,128)(2,1)} %param.18) | copy-start | bytes 1572868
  1898.1 2036.6 %copy-start.1 = (bf16[1,704,2048]{2,1,0:T(8,128)(2,1)S(1)}, bf16[1,704,2048]{2,1,0:T(8,128)(2,1)}, u32[]{:S(2)}) copy-start(bf16[1,704,2048]{2,1,0:T(8,128)(2,1)} %param.34) | copy-start | bytes 8650756
  (59 other events, 1850.2 us)
Sparse Core Ops, SparseCore 0:
  9.7 161.6 all-gather.7
  173.1 157.5 all-gather.9
  332.4 164.5 all-gather.11
  498.6 162.7 all-gather.13
  666.3 49.6 all-reduce.12
  717.6 195.7 all-gather.15
  915.2 269.8 all-gather.17
  1186.8 168.2 all-gather.19
  1392.8 36.3 all-reduce.14
  1503.6 53.2 all-reduce.16
  1559.9 278.6 reduce-scatter.16
  1841.4 286.7 reduce-scatter.12
  2131.3 288.4 reduce-scatter.10
  2422.8 301.4 reduce-scatter.18
  2727.2 300.7 reduce-scatter.20
  3030.9 299.7 reduce-scatter.22
  3333.6 295.0 reduce-scatter.14
  3631.7 302.9 reduce-scatter.8
where the time goes:
time: 3960 us; the launch traced here: 3940 us
  waiting for transfers between devices  2880 us (73%)
  blocking collectives  619 us (16%)
  matrix products  171 us (4%)
  local copies, waits for them, and re-layouts  122 us (3%)
  starting transfers between devices  67.6 us (2%)
  other arithmetic  60.4 us (2%)
    unnamed x2, blocking collectives  417 us
    reduce_scatter x1, waiting for transfers between devices, shards(): lax.psum_scatter(query_weight_grad, ('fsdp', 'ctx'), scatter_dimension=0,...  306 us
    reduce_scatter x1, waiting for transfers between devices, shards(): lax.psum_scatter(shared_gate_grad, ('fsdp', 'ctx'), scatter_dimension=0,...  304 us
    reduce_scatter x1, waiting for transfers between devices, shards(): lax.psum_scatter(shared_up_grad, ('fsdp', 'ctx'), scatter_dimension=0, ti...  304 us
    reduce_scatter x1, waiting for transfers between devices, shards(): lax.psum_scatter(shared_down_grad, ('fsdp', 'ctx'), scatter_dimension=1,...  303 us
    reduce_scatter x1, waiting for transfers between devices, shards(): lax.psum_scatter(output_weight_grad, ('fsdp', 'ctx'), scatter_dimension=1...  298 us
    reduce_scatter x1, waiting for transfers between devices, shards(): lax.psum_scatter(latent_down_grad, ('fsdp', 'ctx'), scatter_dimension=0,...  292 us
    reduce_scatter x1, waiting for transfers between devices, shards(): lax.psum_scatter(latent_up_grad, ('fsdp', 'ctx'), scatter_dimension=0, ti...  225 us
  transfers between devices with their start and end apart: 26, of which 20 were waited for; matrix products, arithmetic and copies ran while one was open for 8% of the time, Pallas kernels for 0%

commit v1 on v0

v1 whole, which is shorter than its diff:
```python
import jax
import jax.numpy as jnp
from jax import lax
from jax.experimental import pallas as pl
from jax.experimental.pallas import tpu as pltpu
from jax.sharding import Mesh
from jax.sharding import PartitionSpec as P

NOPE = 128
ROPE = 64
VDIM = 128
LATENT = 512
HEAD = NOPE + ROPE
EPS = 1e-06
SCALE = HEAD ** (-0.5)
F32 = jnp.float32
BF16 = jnp.bfloat16


def dot(left, right, left_dim=1, right_dim=0):
    return lax.dot_general(
        left, right, (((left_dim,), (right_dim,)), ((), ())), preferred_element_type=F32
    )


def shift(values, axis, step):
    size = lax.axis_size(axis)
    return lax.ppermute(values, axis, [(j, (j + step) % size) for j in range(size)])


def put(buffer, piece, index, offset=0):
    start = (index, offset) + (0,) * (piece.ndim - 1)
    return lax.dynamic_update_slice(buffer, piece[None], start)


def pick(buffer, index):
    return lax.dynamic_index_in_dim(buffer, index, 0, keepdims=False)


def ring_gather(block, axis):
    me = lax.axis_index(axis)
    from_left = shift(block, axis, 1)
    from_right = shift(block, axis, -1)
    half = block.shape[0] // 2
    far_low = shift(from_left[:half], axis, 1)
    far_high = shift(from_right[half:], axis, -1)
    out = jnp.zeros((4,) + block.shape, block.dtype)
    out = put(out, block, me)
    out = put(out, from_left, (me + 3) % 4)
    out = put(out, from_right, (me + 1) % 4)
    out = put(out, far_low, (me + 2) % 4)
    return put(out, far_high, (me + 2) % 4, half)


def ring_scatter(parts, axis):
    me = lax.axis_index(axis)
    kind = parts.dtype
    far = pick(parts, (me + 2) % 4)
    right = pick(parts, (me + 1) % 4)
    left = pick(parts, (me + 3) % 4)
    half = far.shape[0] // 2
    low = shift(far[:half], axis, 1)
    high = shift(far[half:], axis, -1)
    right = jnp.concatenate(
        [(right[:half].astype(F32) + low.astype(F32)).astype(kind), right[half:]], axis=0
    )
    left = jnp.concatenate(
        [left[:half], (left[half:].astype(F32) + high.astype(F32)).astype(kind)], axis=0
    )
    got_left = shift(right, axis, 1)
    got_right = shift(left, axis, -1)
    total = pick(parts, me).astype(F32) + got_left.astype(F32) + got_right.astype(F32)
    return total.astype(kind)


def in_order(own, other, index):
    first = jnp.where(index == 0, own, other)
    second = jnp.where(index == 0, other, own)
    return jnp.stack([first, second])


def pair_gather(block, axis):
    return in_order(block, shift(block, axis, 1), lax.axis_index(axis))


def pair_scatter(parts, axis):
    me = lax.axis_index(axis)
    got = shift(pick(parts, 1 - me), axis, 1)
    return pick(parts, me).astype(F32) + got.astype(F32)


def gather_rows(halves):
    mine = lax.all_to_all(halves, "c", split_axis=0, concat_axis=0, tiled=True)
    pair = pair_gather(mine, "z")
    one = ring_gather(ring_gather(pair[:, 0], "x"), "y")
    two = ring_gather(ring_gather(pair[:, 1], "y"), "x")
    both = jnp.stack([one.transpose(1, 2, 0, 3, 4), two.transpose(0, 2, 1, 3, 4)], axis=2)
    return both.reshape(-1, halves.shape[-1])


def scatter_rows(partial):
    blocks = partial.reshape(4, 2, 2, 4, -1, partial.shape[-1])
    one, two = blocks[:, :, 0], blocks[:, :, 1]
    one = ring_scatter(ring_scatter(one.transpose(2, 0, 1, 3, 4), "y"), "x")
    two = ring_scatter(ring_scatter(two.transpose(0, 2, 1, 3, 4), "x"), "y")
    mine = pair_scatter(jnp.stack([one, two], axis=1), "z")
    return lax.all_to_all(mine, "c", split_axis=0, concat_axis=0, tiled=True)


def exchange(parts, axis):
    me = lax.axis_index(axis)
    out = jnp.zeros_like(parts)
    out = put(out, pick(parts, me), me)
    for step in (1, 2, 3):
        got = shift(pick(parts, (me + step) % 4), axis, step)
        out = put(out, got, (me + 4 - step) % 4)
    return out


def both_cores(block):
    pair = pair_gather(block, "c")
    return pair.reshape((-1,) + block.shape[1:])


def core_sum(partial):
    return pair_scatter_low(partial.reshape(2, -1, partial.shape[-1]))


def pair_scatter_low(parts):
    me = lax.axis_index("c")
    got = shift(pick(parts, 1 - me).astype(BF16), "c", 1)
    return pick(parts, me) + got.astype(F32)


def half_sum(partial):
    low = partial.astype(BF16)
    return low.astype(F32) + shift(low, "t", 1).astype(F32)


MSG = 1024
QR = 256
KV = 384
KR = 896


def head_lanes(rows, head):
    lane = lax.broadcasted_iota(jnp.int32, (rows, 128), 1)
    return jnp.where(((lane >> 5) & 1) == head, 1.0, 0.0).astype(F32)


def head_keys(msg_ref, head):
    rotated = msg_ref[:, :, KR:].reshape(512, 128).astype(F32) * head_lanes(512, head)
    plain = msg_ref[:, :, KV + head * 256 : KV + head * 256 + 128].reshape(512, 128)
    return jnp.concatenate([plain, rotated.astype(BF16)], axis=1)


def head_values(msg_ref, head):
    return msg_ref[:, :, KV + head * 256 + 128 : KV + head * 256 + 256].reshape(512, 128)


def block_probs(query, keys, row_ref, col_ref, block):
    count = (block + 1) * 128
    scores = dot(query, keys[:count], 1, 1) * SCALE
    rows = lax.broadcasted_iota(jnp.int32, (128, count), 0) + block * 128
    cols = lax.broadcasted_iota(jnp.int32, (128, count), 1)
    same = col_ref[block * 128 : count, :] == row_ref[:, :count]
    scores = jnp.where(same & (cols <= rows), scores, -1e30)
    powers = jnp.exp(scores - jnp.max(scores, axis=1, keepdims=True))
    return powers / jnp.sum(powers, axis=1, keepdims=True)


def block_query(msg_ref, head, block):
    return jnp.concatenate(
        [msg_ref[block, :, head * 128 : head * 128 + 128], msg_ref[block, :, QR:KV]], axis=1
    )


def forward_kernel(msg_ref, row_ref, col_ref, out_ref):
    for head in range(2):
        keys = head_keys(msg_ref, head)
        values = head_values(msg_ref, head)
        for block in range(4):
            query = block_query(msg_ref, head, block)
            probs = block_probs(query, keys, row_ref, col_ref, block)
            mixed = dot(probs.astype(BF16), values[: (block + 1) * 128])
            out_ref[block, :, head * 128 : head * 128 + 128] = mixed.astype(BF16)


def backward_kernel(msg_ref, grad_ref, row_ref, col_ref, out_ref, key_acc, value_acc):
    for head in range(2):
        keys = head_keys(msg_ref, head)
        values = head_values(msg_ref, head)
        key_acc[...] = jnp.zeros_like(key_acc)
        value_acc[...] = jnp.zeros_like(value_acc)
        lanes = head_lanes(128, head)
        for block in range(4):
            count = (block + 1) * 128
            query = block_query(msg_ref, head, block)
            probs = block_probs(query, keys, row_ref, col_ref, block)
            grad = grad_ref[block, :, head * 128 : head * 128 + 128]
            probs_grad = dot(grad, values[:count], 1, 1)
            inner = jnp.sum(probs * probs_grad, axis=1, keepdims=True)
            score_grad = (probs * (probs_grad - inner) * SCALE).astype(BF16)
            query_grad = dot(score_grad, keys[:count])
            out_ref[block, :, head * 128 : head * 128 + 128] = query_grad[:, :128].astype(BF16)
            turned = query_grad[:, 128:]
            if head == 1:
                turned = turned + out_ref[block, :, QR:KV].astype(F32)
            out_ref[block, :, QR:KV] = turned.astype(BF16)
            key_acc[:count] += dot(score_grad, query, 0, 0)
            value_acc[:count] += dot(probs.astype(BF16), grad, 0, 0)
        base = KV + head * 256
        for block in range(4):
            span = slice(block * 128, block * 128 + 128)
            out_ref[block, :, base : base + 128] = key_acc[span, :128].astype(BF16)
            out_ref[block, :, base + 128 : base + 256] = value_acc[span, :].astype(BF16)
            turned = key_acc[span, 128:] * lanes
            if head == 1:
                turned = turned + out_ref[block, :, KR:].astype(F32)
            out_ref[block, :, KR:] = turned.astype(BF16)


def vmem():
    return pl.BlockSpec(memory_space=pltpu.VMEM)


def attention_forward(msg, row, col):
    return pl.pallas_call(
        forward_kernel,
        out_shape=jax.ShapeDtypeStruct((4, 128, 256), BF16),
        in_specs=[vmem()] * 3,
        out_specs=vmem(),
        compiler_params=pltpu.CompilerParams(vmem_limit_bytes=32 * 1024 * 1024),
        cost_estimate=pl.CostEstimate(
            flops=400_000_000, bytes_accessed=1_400_000, transcendentals=400_000
        ),
    )(msg, row, col)


def attention_backward(msg, grad, row, col):
    return pl.pallas_call(
        backward_kernel,
        out_shape=jax.ShapeDtypeStruct((4, 128, MSG), BF16),
        in_specs=[vmem()] * 4,
        out_specs=vmem(),
        scratch_shapes=[pltpu.VMEM((512, 256), F32), pltpu.VMEM((512, 128), F32)],
        compiler_params=pltpu.CompilerParams(vmem_limit_bytes=32 * 1024 * 1024),
        cost_estimate=pl.CostEstimate(
            flops=1_000_000_000, bytes_accessed=2_600_000, transcendentals=400_000
        ),
    )(msg, grad, row, col)


def doc_positions(doc_row):
    places = jnp.arange(doc_row.shape[0], dtype=jnp.int32)
    starts = jnp.concatenate([jnp.ones((1,), bool), doc_row[1:] != doc_row[:-1]])
    begins = lax.cummax(jnp.where(starts, places, 0), axis=0)
    return places - begins


def swap_halves(values):
    rows, lanes = values.shape
    parts = values.reshape(rows, lanes // 128, 2, 64)
    return parts[:, :, ::-1].reshape(rows, lanes)


def rotate(values, cosine, sine):
    count = values.shape[1] // 128
    cosine = jnp.tile(cosine, (1, count))
    sine = jnp.tile(sine, (1, count))
    return values * cosine + swap_halves(values) * sine


def norm_back(scaled, normed, inverse):
    return inverse * (scaled - normed * jnp.mean(scaled * normed, axis=1, keepdims=True))


def silu_parts(lin):
    sig = jax.nn.sigmoid(lin)
    return lin * sig, sig * (1.0 + lin * (1.0 - sig))


def rms(values):
    return lax.rsqrt(jnp.mean(values * values, axis=1, keepdims=True) + EPS)


def shards(
    tokens_in,
    documents,
    routes,
    attn_gain,
    query_weight,
    latent_down,
    latent_gain,
    latent_up,
    output_weight,
    ffn_gain,
    router,
    shared_gate,
    shared_up,
    shared_down,
    expert_gate,
    expert_up,
    expert_down,
    cotangent,
):
    core = lax.axis_index("c")
    spot = lax.axis_index("y")
    expert = (lax.axis_index("x") * 4 + lax.axis_index("z") * 2 + core) * 4 + spot
    rows = tokens_in.shape[0]
    width = tokens_in.shape[1]
    experts_count = router.shape[1]
    capacity = 16
    every = ("x", "z", "c", "y")

    gain_col = attn_gain.astype(F32)[:, None]
    heads = query_weight.reshape(32, 2, 2, 2, HEAD)
    query_plain = heads[..., :NOPE].reshape(32, 2, 512)
    query_turn = (
        heads[..., NOPE:].reshape(32, 2, 2, 2, 2, 32).transpose(0, 1, 2, 4, 3, 5).reshape(32, 2, 256)
    )
    query_pack = jnp.concatenate([query_plain, query_turn], axis=2).transpose(1, 0, 2)
    up_pack = latent_up.reshape(8, 2, 4, 256).transpose(1, 0, 2, 3)
    up_scaled = (up_pack.astype(F32) * latent_gain.astype(F32)[None, :, None, None]).astype(BF16)
    out_pack = output_weight.reshape(2, 512, 32).transpose(0, 2, 1)
    gain_pad = jnp.pad(ffn_gain[:, None], ((0, 0), (0, 63)))
    attn_pack = jnp.concatenate(
        [
            (query_pack.astype(F32) * gain_col).astype(BF16),
            jnp.broadcast_to((latent_down.astype(F32) * gain_col).astype(BF16), (2, 32, 576)),
            jnp.broadcast_to(gain_pad, (2, 32, 64)),
            out_pack,
            up_scaled.reshape(2, 32, 256),
        ],
        axis=2,
    )
    attn_all = gather_rows(attn_pack)

    shared_pack = jnp.concatenate(
        [
            shared_gate.reshape(32, 2, 704),
            shared_up.reshape(32, 2, 704),
            shared_down.reshape(2, 704, 32).transpose(2, 0, 1),
            jnp.broadcast_to(router[:, None], (32, 2, 64)),
        ],
        axis=2,
    ).transpose(1, 0, 2)
    shared_pack, attn_all = lax.optimization_barrier((shared_pack, attn_all))
    shared_all = gather_rows(shared_pack)

    in_all = attn_all[:, :1408]
    out_all = attn_all[:, 1408:1920]
    up_all = attn_all[:, 1920:].reshape(LATENT, 1024)

    docs = both_cores(documents)
    positions = jax.vmap(doc_positions)(docs)
    local_pos = lax.dynamic_slice_in_dim(positions, spot * rows, rows, axis=1).reshape(-1)
    steps = jnp.arange(ROPE // 2, dtype=F32)
    angles = local_pos.astype(F32)[:, None] * (10000.0 ** (-steps / (ROPE // 2)))[None, :]
    cosine = jnp.tile(jnp.cos(angles), (1, 4))
    sine = jnp.sin(angles)
    sine = jnp.concatenate([-sine, -sine, sine, sine], axis=1)

    tokens_f = tokens_in.astype(F32)
    tokens_two = both_cores(tokens_in).astype(F32)
    normed_low = (tokens_two * rms(tokens_two)).astype(BF16)
    lin = dot(normed_low, in_all)
    query_turned = rotate(lin[:, 512:768], cosine, sine)
    latent = lin[:, 768:1280]
    inverse_lat = rms(latent)
    latent_normed = latent * inverse_lat
    latent_low = latent_normed.astype(BF16)
    key_u, key_w = lin[:, 1280:1312], lin[:, 1312:1344]
    key_turned = rotate(jnp.concatenate([key_u, key_u, key_w, key_w], axis=1), cosine, sine)
    keys_values = dot(latent_low, up_all)

    def messages(pair):
        span = slice(pair * 256, pair * 256 + 256)
        return jnp.concatenate(
            [
                lin[:, span],
                query_turned[:, pair * 128 : pair * 128 + 128],
                keys_values[:, pair * 512 : pair * 512 + 512],
                key_turned,
            ],
            axis=1,
        ).astype(BF16)

    sent = jnp.stack([messages(0), messages(1)]).reshape(2, 2, rows, MSG)
    sent = sent.transpose(1, 0, 2, 3).reshape(4, rows, MSG)
    msg = exchange(sent, "y")
    doc = pick(docs, spot // 2)
    doc_row, doc_col = doc[None, :], doc[:, None]
    mixed = attention_forward(msg, doc_row, doc_col)
    mixed_back = exchange(mixed, "y")
    attended = mixed_back.reshape(2, 2, rows, 256).transpose(0, 2, 1, 3).reshape(2 * rows, 512)
    resid = tokens_f + half_sum(core_sum(dot(attended, out_all, 1, 1)))

    gain_two = dot(
        (jnp.arange(64)[None, :] == 0).astype(BF16) * jnp.ones((8, 1), BF16),
        attn_all[:, 1344:1408],
        1,
        1,
    )[:1]
    inverse_two = rms(resid)
    normed_two = resid * inverse_two
    ffn_in = (normed_two * gain_two).astype(BF16)

    named = jnp.any(
        routes.T[None, :, :] == jnp.arange(experts_count, dtype=jnp.int32)[:, None, None], axis=1
    )
    before = jnp.arange(rows)[:, None] < jnp.arange(rows)[None, :]
    place = dot(named.astype(BF16), before.astype(BF16))
    slots = (
        named[:, None, :] & (place[:, None, :] == jnp.arange(capacity, dtype=F32)[None, :, None])
    ).astype(BF16)
    slots = slots.reshape(experts_count * capacity, rows)

    def to_experts(values):
        sent = dot(slots, values).astype(BF16).reshape(experts_count, capacity, width)
        got = lax.all_to_all(sent, every, split_axis=0, concat_axis=0, tiled=True)
        return got.reshape(-1, width)

    def from_experts(values):
        sent = values.reshape(experts_count, capacity, width)
        got = lax.all_to_all(sent, every, split_axis=0, concat_axis=0, tiled=True)
        return dot(slots, got.reshape(-1, width), 0, 0)

    gate_w, up_w, down_w = expert_gate[0], expert_up[0], expert_down[0]
    cot_sent, _ = lax.optimization_barrier((cotangent, attn_all))
    expert_cot = to_experts(cot_sent)
    expert_rows = to_experts(ffn_in)
    router_all = shared_all[:, 2112:]
    probs = jax.nn.softmax(dot(expert_rows, router_all), axis=1)
    own = (jnp.arange(experts_count, dtype=jnp.int32) == expert)[None, :].astype(F32)
    gate = jnp.sum(probs * own, axis=1, keepdims=True)
    plain_grad = dot(expert_cot, down_w, 1, 1)
    gate_lin = dot(expert_rows, gate_w)
    up_lin = dot(expert_rows, up_w)
    silu, slope = silu_parts(gate_lin)
    act = silu * up_lin
    act_low = (gate * act).astype(BF16)
    inner = jnp.sum(act * plain_grad, axis=1, keepdims=True)
    act_grad = gate * plain_grad
    gate_grad = (act_grad * up_lin * slope).astype(BF16)
    up_grad = (act_grad * silu).astype(BF16)
    logit_grad = (inner * gate * (own - probs)).astype(BF16)
    row_grad = (
        dot(gate_grad, gate_w, 1, 1) + dot(up_grad, up_w, 1, 1) + dot(logit_grad, router_all, 1, 1)
    ).astype(BF16)
    routed_back = from_experts(row_grad)
    piece = dot(act_low, down_w).astype(BF16)
    piece, _ = lax.optimization_barrier((piece, routed_back))
    routed_out = from_experts(piece)
    expert_down_grad = dot(act_low, expert_cot, 0, 0)[None]
    expert_gate_grad = dot(expert_rows, gate_grad, 0, 0)[None]
    expert_up_grad = dot(expert_rows, up_grad, 0, 0)[None]
    router_grad = dot(expert_rows, logit_grad, 0, 0)

    ffn_two = both_cores(ffn_in)
    cot_two = both_cores(cotangent)
    gate_up_all = shared_all[:, :1408]
    down_all = shared_all[:, 1408:2112]
    shared_lin = dot(ffn_two, gate_up_all)
    shared_up_lin = shared_lin[:, 704:]
    shared_silu, shared_slope = silu_parts(shared_lin[:, :704])
    shared_act = (shared_silu * shared_up_lin).astype(BF16)
    shared_dact = dot(cot_two, down_all)
    shared_dlin = jnp.concatenate(
        [shared_dact * shared_up_lin * shared_slope, shared_dact * shared_silu], axis=1
    ).astype(BF16)
    shared_out = core_sum(dot(shared_act, down_all, 1, 1))
    shared_back = core_sum(dot(shared_dlin, gate_up_all, 1, 1))
    gate_up_grad = dot(ffn_two, shared_dlin, 0, 0)
    shared_down_grad = dot(cot_two, shared_act, 0, 0)
    shared_sum = scatter_rows(
        jnp.concatenate([gate_up_grad, shared_down_grad, router_grad], axis=1).astype(BF16)
    )

    cot_f = cotangent.astype(F32)
    layer_out = (resid + half_sum(shared_out + routed_out)).astype(BF16)
    ffn_grad = half_sum(shared_back + routed_back)
    resid_grad = cot_f + norm_back(ffn_grad * gain_two, normed_two, inverse_two)
    first_lane = jnp.broadcast_to(jnp.arange(64)[None, :] == 0, (rows, 64)).astype(BF16)
    ffn_gain_part = dot((ffn_grad * normed_two).astype(BF16), first_lane, 0, 0)

    resid_two = both_cores(resid_grad.astype(BF16))
    out_grad = dot(resid_two, attended, 0, 0)
    heads_grad = dot(resid_two, out_all).astype(BF16)
    heads_sent = heads_grad.reshape(2, rows, 2, 256).transpose(0, 2, 1, 3).reshape(4, rows, 256)
    heads_got = exchange(heads_sent, "y")
    back = exchange(attention_backward(msg, heads_got, doc_row, doc_col), "y")
    back = back.reshape(2, 2, rows, MSG)

    def columns(low, high):
        part = back[..., low:high].transpose(0, 2, 1, 3)
        return part.reshape(2 * rows, 2 * (high - low))

    turned = rotate(columns(QR, KV).astype(F32), cosine, -sine)
    kv_grad = columns(KV, KR)
    key_back = jnp.sum(back[..., KR:].astype(F32), axis=1).reshape(2 * rows, 128)
    key_back = rotate(key_back, cosine, -sine)
    key_back = jnp.concatenate(
        [key_back[:, :32] + key_back[:, 32:64], key_back[:, 64:96] + key_back[:, 96:]], axis=1
    )
    latent_grad = norm_back(dot(kv_grad, up_all, 1, 1), latent_normed, inverse_lat)
    lin_grad = jnp.concatenate(
        [columns(0, QR), turned.astype(BF16), latent_grad.astype(BF16), key_back.astype(BF16)],
        axis=1,
    )
    normed_grad = dot(lin_grad, in_all[:, :1344], 1, 1)
    attn_in_grad = half_sum(core_sum(normed_grad))
    inverse_one = rms(tokens_f)
    input_grad = resid_grad + norm_back(attn_in_grad, tokens_f * inverse_one, inverse_one)
    in_grad = dot(normed_low, lin_grad, 0, 0)
    up_grad_part = dot(latent_low, kv_grad, 0, 0).reshape(width, 256)
    attn_sum = scatter_rows(
        jnp.concatenate([in_grad, ffn_gain_part, out_grad, up_grad_part], axis=1).astype(BF16)
    )

    query_sum = attn_sum[..., :768]
    up_sum = attn_sum[..., 1920:]
    down_sum = attn_sum[0, :, 768:1344] + attn_sum[1, :, 768:1344]
    attn_gain_part = jnp.sum(query_pack.astype(F32) * query_sum, axis=(0, 2)) + jnp.sum(
        latent_down.astype(F32) * down_sum, axis=1
    )
    latent_gain_part = jnp.sum(up_pack.reshape(2, 32, 256).astype(F32) * up_sum, axis=(0, 2))
    router_sum = shared_sum[0, :, 2112:] + shared_sum[1, :, 2112:]
    small = jnp.concatenate(
        [down_sum, router_sum, attn_gain_part[:, None], latent_gain_part[:, None]], axis=1
    )
    small = small + shift(small, "t", 1)
    attn_gain_grad = small[:, 640]
    latent_gain_grad = jnp.sum(small[:, 641].reshape(8, 4), axis=1)
    latent_down_grad = gain_col * small[:, :576]
    router_out = small[:, 576:640]
    query_plain = query_sum[..., :512].reshape(2, 32, 2, 2, NOPE)
    query_turn = query_sum[..., 512:].reshape(2, 32, 2, 2, 2, 32).transpose(0, 1, 2, 4, 3, 5)
    query_turn = query_turn.reshape(2, 32, 2, 2, ROPE)
    query_out = jnp.concatenate([query_plain, query_turn], axis=4).transpose(1, 0, 2, 3, 4)
    query_out = gain_col * query_out.reshape(32, 2 * 4 * HEAD)
    up_out = up_sum.reshape(2, 8, 4, 256).transpose(1, 0, 2, 3).reshape(8, 2048)
    up_out = latent_gain.astype(F32)[:, None] * up_out
    out_out = attn_sum[..., 1408:1920].transpose(0, 2, 1).reshape(1024, 32)
    ffn_gain_grad = attn_sum[0, :, 1344] + attn_sum[1, :, 1344]
    shared_rows = shared_sum.transpose(1, 0, 2)
    return (
        layer_out,
        input_grad,
        attn_gain_grad,
        query_out,
        latent_down_grad,
        latent_gain_grad,
        up_out,
        out_out,
        ffn_gain_grad,
        router_out,
        shared_rows[..., :704].reshape(32, 1408),
        shared_rows[..., 704:1408].reshape(32, 1408),
        shared_sum[..., 1408:2112].transpose(0, 2, 1).reshape(1408, 32),
        expert_gate_grad,
        expert_up_grad,
        expert_down_grad,
    )


def solution(mesh):
    fine = Mesh(mesh.devices.reshape(4, 2, 2, 4, 2), ("x", "z", "c", "y", "t"))
    fsdp = ("x", "z", "c")
    every = ("x", "z", "c", "y")
    in_specs = (
        P(every, None),
        P(fsdp, None),
        P(every, None),
        P(every),
        P(every, "t"),
        P(every, None),
        P(every),
        P(every, "t"),
        P("t", every),
        P(every),
        P(every, None),
        P(every, "t"),
        P(every, "t"),
        P("t", every),
        P(every, None, "t"),
        P(every, None, "t"),
        P(every, "t", None),
        P(every, None),
    )
    out_specs = (
        P(every, None),
        P(every, None),
        P(every),
        P(every, "t"),
        P(every, None),
        P(every),
        P(every, "t"),
        P("t", every),
        P(every),
        P(every, None),
        P(every, "t"),
        P(every, "t"),
        P("t", every),
        P(every, None, "t"),
        P(every, None, "t"),
        P(every, "t", None),
    )
    return jax.shard_map(shards, mesh=fine, in_specs=in_specs, out_specs=out_specs, check_vma=False)
```

time: 3960 us -> 878 us (0.22)
  waiting for transfers between devices: 2880 us -> 250 us
  blocking collectives: 619 us -> 20.4 us
  starting transfers between devices: 67.6 us -> 170 us
  local copies, waits for them, and re-layouts: 122 us -> 203 us
    reduce_scatter x8 -> x0, waiting for transfers between devices: 2030 us -> none  [the longest x1 306 us: shards(): lax.psum_scatter(query_weight_grad, ('fsdp', 'ctx'), scatter_dimension=0,...]
    all_gather x7 -> x0, waiting for transfers between devices: 672 us -> none  [the longest x1 166 us: shards(): lax.all_gather(shared_down, ('fsdp', 'ctx'), axis=1, tiled=True)]
    unnamed x2 -> x0, blocking collectives: 417 us -> none
    ppermute x0 -> x94, waiting for transfers between devices: none -> 240 us  [shift(): lax.ppermute(values, axis, [(j, (j + step) % size) for j in range(size)])]
    all_gather x1 -> x0, blocking collectives: 170 us -> none  [shards(): lax.all_gather(router, ('fsdp', 'ctx'), axis=0, tiled=True)]
    ppermute x0 -> x94, starting transfers between devices: none -> 124 us  [shift(): lax.ppermute(values, axis, [(j, (j + step) % size) for j in range(size)])]
    all_to_all x8 -> x6, waiting for transfers between devices: 94.2 us -> 9.79 us  [the longest x2 8.96 us: to_experts(): got = lax.all_to_all(sent, every, split_axis=0, concat_axis=0, tiled=True)]
    psum x3 -> x0, waiting for transfers between devices: 82.3 us -> none  [the longest x1 41.9 us: shards(): lax.psum((shared_part + routed_part).astype(jnp.bfloat16), 'tp')]
  transfers between devices with their start and end apart: 26 -> 100, of which waited for: 20 -> 28; matrix products, arithmetic and copies ran while one was open for 8% -> 38% of each run, Pallas kernels for 0% -> 0%
where the time goes in v1:
time: 878 us; the launch traced here: 866 us
  waiting for transfers between devices  250 us (28%)
  local copies, waits for them, and re-layouts  203 us (23%)
  starting transfers between devices  170 us (19%)
  matrix products  137 us (16%)
  other arithmetic  74.8 us (9%)
  blocking collectives  20.4 us (2%)
    ppermute x94, waiting for transfers between devices, shift(): lax.ppermute(values, axis, [(j, (j + step) % size) for j in range(size)])  240 us
    dot_general x34, matrix products, dot(): lax.dot_general(left, right, (((left_dim,), (right_dim,)), ((), ())), pre...  137 us
    ppermute x94, starting transfers between devices, shift(): lax.ppermute(values, axis, [(j, (j + step) % size) for j in range(size)])  124 us
    dynamic_update_slice x48, local copies, waits for them, and re-layouts, put(): return lax.dynamic_update_slice(buffer, piece[None], start)  46 us
    all_to_all x2, starting transfers between devices, from_experts(): got = lax.all_to_all(sent, every, split_axis=0, concat_axis=0, tiled=True)  20.8 us
  transfers between devices with their start and end apart: 100, of which 28 were waited for; matrix products, arithmetic and copies ran while one was open for 38% of the time, Pallas kernels for 0%

profile of v1, /device:TPU:1, one launch (start us, length us, event | category | flops | bytes accessed | tf_op | source)
XLA Modules:
  0.0 866.0 jit_solution(1144470227653524009)
XLA Ops:
  79.3 10.6 %collective-permute-done.14 = bf16[4,2,32,2176]{3,2,0,1:T(8,128)(2,1)S(1)} collective-permute-done((bf16[4,2,32,2176]{3,2,0,1:T(8,128)(2,1)}, bf16[4,2,32,2176]{3,2,0,1:T(8,128)(2,1)S(1)}, u32[]{:S(2)}, u32[]{:S(2)}) %collective-permute-start.14) | collective-permute-done | bytes 1114144 | tf_op jit(solution)/shard_map/ppermute | solution.py:28
  105.7 7.9 pad_maximum_fusion
  113.5 7.9 copy.515
  161.0 9.6 %all_to_all.40 = bf16[2,32,2176]{2,1,0:T(8,128)(2,1)S(1)} all-to-all(bf16[2,32,2176]{2,1,0:T(8,128)(2,1)S(1)} %bitcast.882), channel_id=1, replica_groups=mesh['x'=4,'z'=2,'c'=2,'y'=4,'t'=2] {'c'}, dimensions={0} | all-to-all | bytes 557056 | tf_op jit(solution)/shard_map/all_to_all | solution.py:93
  229.0 8.0 collective-permute-done.26
  279.7 34.5 %collective-permute-done.43 = bf16[2,2,32,2176]{3,2,0,1:T(8,128)(2,1)} collective-permute-done((bf16[2,2,32,2176]{3,2,0,1:T(8,128)(2,1)}, bf16[2,2,32,2176]{3,2,0,1:T(8,128)(2,1)}, u32[]{:S(2)}, u32[]{:S(2)}) %collective-permute-start.43) | collective-permute-done | bytes 557088 | tf_op jit(solution)/shard_map/ppermute | solution.py:28
  321.8 8.0 pad_maximum_fusion.1
  338.6 9.4 %all-to-all-start.3 = ((bf16[64,16,2048]{2,1,0:T(8,128)(2,1)}), bf16[64,16,2048]{2,1,0:T(8,128)(2,1)}, u32[]{:S(2)}, u32[]{:S(2)}) async-start(bf16[64,16,2048]{2,1,0:T(8,128)(2,1)} %bitcast.825), calls=%async_computation.3 | async-start | bytes 8388608 | tf_op jit(solution)/shard_map/all_to_all | solution.py:421
  365.1 6.8 copy.574
  376.0 7.2 fusion.15
  383.2 6.9 fusion.19
  390.2 9.0 %all-to-all-done.3 = bf16[64,16,2048]{2,1,0:T(8,128)(2,1)} async-done(((bf16[64,16,2048]{2,1,0:T(8,128)(2,1)}), bf16[64,16,2048]{2,1,0:T(8,128)(2,1)}, u32[]{:S(2)}, u32[]{:S(2)}) %all-to-all-start.3) | async-done | bytes 4194336 | tf_op jit(solution)/shard_map/all_to_all | solution.py:421
  399.1 7.9 multiply_reduce_fusion
  410.6 7.4 convolution_bitcast_fusion.1
  421.6 7.2 convolution_bitcast_fusion
  433.8 7.1 convolution_bitcast_fusion.2
  445.5 9.9 %all-to-all-start.4 = ((bf16[64,16,2048]{2,1,0:T(8,128)(2,1)}), bf16[64,16,2048]{2,1,0:T(8,128)(2,1)}, u32[]{:S(2)}, u32[]{:S(2)}) async-start(bf16[64,16,2048]{2,1,0:T(8,128)(2,1)} %bitcast.836), calls=%async_computation.4 | async-start | bytes 8388608 | tf_op jit(solution)/shard_map/all_to_all | solution.py:426
  458.9 13.7 %concatenate.198 = bf16[4,2,2,4,32,2176]{5,4,1,3,2,0:T(8,128)(2,1)} concatenate(bf16[4,2,2,4,32,1408]{5,4,1,3,2,0:T(8,128)(2,1)} %convolution_convert_fusion, bf16[4,2,2,4,32,704]{5,4,1,3,2,0:T(8,128)(2,1)} %convolution_convert_fusion.5, bf16[4,2,2,4,32,64]{5,4,1,3,2,0:T(8,128)(2,1)S(1)} %fusion.40), dimensions={5} | concatenate | bytes 17825792 | tf_op jit(solution)/shard_map/concatenate | solution.py:477
  487.2 28.2 %collective-permute-done.78 = bf16[2,2,32,2176]{3,2,1,0:T(8,128)(2,1)S(1)} collective-permute-done((bf16[2,2,32,2176]{3,2,1,0:T(8,128)(2,1)S(1)}, bf16[2,2,32,2176]{3,2,1,0:T(8,128)(2,1)S(1)}, u32[]{:S(2)}, u32[]{:S(2)}) %collective-permute-start.78) | collective-permute-done | bytes 557088 | tf_op jit(solution)/shard_map/ppermute | solution.py:28
  519.1 10.8 %collective-permute-done.84 = bf16[2,2,32,2176]{3,2,1,0:T(8,128)(2,1)S(1)} collective-permute-done((bf16[2,2,32,2176]{3,2,1,0:T(8,128)(2,1)S(1)}, bf16[2,2,32,2176]{3,2,1,0:T(8,128)(2,1)S(1)}, u32[]{:S(2)}, u32[]{:S(2)}) %collective-permute-start.84) | collective-permute-done | bytes 557088 | tf_op jit(solution)/shard_map/ppermute | solution.py:28
  531.3 10.6 %collective-permute-done.79 = bf16[4,2,32,2176]{3,2,1,0:T(8,128)(2,1)S(1)} collective-permute-done((bf16[4,2,32,2176]{3,2,1,0:T(8,128)(2,1)S(1)}, bf16[4,2,32,2176]{3,2,1,0:T(8,128)(2,1)S(1)}, u32[]{:S(2)}, u32[]{:S(2)}) %collective-permute-start.79) | collective-permute-done | bytes 1114144 | tf_op jit(solution)/shard_map/ppermute | solution.py:28
  547.7 6.5 collective-permute-done.87
  556.7 10.5 %collective-permute-done.85 = bf16[4,2,32,2176]{3,2,1,0:T(8,128)(2,1)S(1)} collective-permute-done((bf16[4,2,32,2176]{3,2,1,0:T(8,128)(2,1)S(1)}, bf16[4,2,32,2176]{3,2,1,0:T(8,128)(2,1)S(1)}, u32[]{:S(2)}, u32[]{:S(2)}) %collective-permute-start.85) | collective-permute-done | bytes 1114144 | tf_op jit(solution)/shard_map/ppermute | solution.py:28
  575.4 10.9 %all-to-all-start.5 = ((bf16[64,16,2048]{2,1,0:T(8,128)(2,1)}), bf16[64,16,2048]{2,1,0:T(8,128)(2,1)}, u32[]{:S(2)}, u32[]{:S(2)}) async-start(bf16[64,16,2048]{2,1,0:T(8,128)(2,1)} %bitcast.851), calls=%async_computation.5 | async-start | bytes 8388608 | tf_op jit(solution)/shard_map/all_to_all | solution.py:426
  595.5 44.1 %collective-permute-done.83 = bf16[2,32,2176]{2,1,0:T(8,128)(2,1)S(1)} collective-permute-done((bf16[2,32,2176]{2,1,0:T(8,128)(2,1)S(1)}, bf16[2,32,2176]{2,1,0:T(8,128)(2,1)S(1)}, u32[]{:S(2)}, u32[]{:S(2)}) %collective-permute-start.83) | collective-permute-done | bytes 278560 | tf_op jit(solution)/shard_map/ppermute | solution.py:28
  665.6 11.3 %collective-permute-done.46 = bf16[128,2048]{1,0:T(8,128)(2,1)} collective-permute-done((bf16[128,2048]{1,0:T(8,128)(2,1)}, bf16[128,2048]{1,0:T(8,128)(2,1)}, u32[]{:S(2)}, u32[]{:S(2)}) %collective-permute-start.46) | collective-permute-done | bytes 524320 | tf_op jit(solution)/shard_map/ppermute | solution.py:28
  716.3 7.2 collective-permute-done.55
  751.3 13.7 %concatenate.189 = bf16[4,2,2,4,32,2176]{5,4,3,2,1,0:T(8,128)(2,1)} concatenate(bf16[4,2,2,4,32,1344]{5,4,3,2,1,0:T(8,128)(2,1)} %convolution_convert_fusion.1, bf16[4,2,2,4,32,64]{5,4,3,2,1,0:T(8,128)(2,1)} %convolution_convert_fusion.9, bf16[4,2,2,4,32,512]{5,4,3,2,1,0:T(8,128)(2,1)} %convolution_convert_fusion.6, bf16[4,2,2,4,32,256]{5,4,3,2,1,0:T(8,128)(2,1)S(1)} %concatenate.188), dimensions={5} | concatenate | bytes 17825792 | tf_op jit(solution)/shard_map/concatenate | solution.py:518
  765.0 6.4 fusion.173
  778.4 7.0 collective-permute-done.61
  793.2 20.6 %collective-permute-done.70 = bf16[4,2,32,2176]{3,2,0,1:T(8,128)(2,1)S(1)} collective-permute-done((bf16[4,2,32,2176]{3,2,0,1:T(8,128)(2,1)S(1)}, bf16[4,2,32,2176]{3,2,0,1:T(8,128)(2,1)S(1)}, u32[]{:S(2)}, u32[]{:S(2)}) %collective-permute-start.70) | collective-permute-done | bytes 1114144 | tf_op jit(solution)/shard_map/ppermute | solution.py:28
  841.9 10.8 %all_to_all.41 = f32[2,32,2176]{2,1,0:T(8,128)S(1)} all-to-all(f32[2,32,2176]{2,1,0:T(8,128)S(1)} %convert_add_fusion.16), channel_id=1, replica_groups=mesh['x'=4,'z'=2,'c'=2,'y'=4,'t'=2] {'c'}, dimensions={0} | all-to-all | bytes 1114112 | tf_op jit(solution)/shard_map/all_to_all | solution.py:107
  (742 shorter events, 485.0 us)
Async XLA Ops:
  0.7 34.3 %collective-permute-start = (bf16[128,2048]{1,0:T(8,128)(2,1)}, bf16[128,2048]{1,0:T(8,128)(2,1)}, u32[]{:S(2)}, u32[]{:S(2)}) collective-permute-start(bf16[128,2048]{1,0:T(8,128)(2,1)} %param.18), channel_id=1, source_target_pairs={{0,8},{8,0},{1,9},{9,1},{2,10},{10,2},{3,11},{11,3},{4,12},{12,4},... | collective-permute-start | bytes 1572872 | tf_op jit(solution)/shard_map/ppermute | solution.py:28
  13.9 26.3 %collective-permute-start.47 = (bf16[128,2048]{1,0:T(8,128)(2,1)}, bf16[128,2048]{1,0:T(8,128)(2,1)}, u32[]{:S(2)}, u32[]{:S(2)}) collective-permute-start(bf16[128,2048]{1,0:T(8,128)(2,1)} %param.35), channel_id=1, source_target_pairs={{0,8},{8,0},{1,9},{9,1},{2,10},{10,2},{3,11},{11,3},{4,12},{12,4},... | collective-permute-start | bytes 1572872 | tf_op jit(solution)/shard_map/ppermute | solution.py:28
  191.9 28.4 %collective-permute-start.25 = (bf16[128,2048]{1,0:T(8,128)(2,1)}, bf16[128,2048]{1,0:T(8,128)(2,1)}, u32[]{:S(2)}, u32[]{:S(2)}) collective-permute-start(bf16[128,2048]{1,0:T(8,128)(2,1)} %fusion.81), channel_id=1, source_target_pairs={{0,8},{8,0},{1,9},{9,1},{2,10},{10,2},{3,11},{11,3},{4,12},{12,4},... | collective-permute-start | bytes 1572872 | tf_op jit(solution)/shard_map/ppermute | solution.py:28
  213.0 39.6 %collective-permute-start.41 = (bf16[4,2,32,2176]{3,2,0,1:T(8,128)(2,1)}, bf16[4,2,32,2176]{3,2,0,1:T(8,128)(2,1)}, u32[]{:S(2)}, u32[]{:S(2)}) collective-permute-start(bf16[4,2,32,2176]{3,2,0,1:T(8,128)(2,1)} %bitcast_dynamic-update-slice_fusion.33), channel_id=1, source_target_pairs={{0,32},{32,64},{64,96},{96,0},{1,33},{33,65},{65,97},{97,1},{2,34}... | collective-permute-start | bytes 3342344 | tf_op jit(solution)/shard_map/ppermute | solution.py:28
  213.0 42.8 %collective-permute-start.42 = (bf16[4,2,32,2176]{3,2,0,1:T(8,128)(2,1)}, bf16[4,2,32,2176]{3,2,0,1:T(8,128)(2,1)}, u32[]{:S(2)}, u32[]{:S(2)}) collective-permute-start(bf16[4,2,32,2176]{3,2,0,1:T(8,128)(2,1)} %bitcast_dynamic-update-slice_fusion.33), channel_id=1, source_target_pairs={{0,96},{32,0},{64,32},{96,64},{1,97},{33,1},{65,33},{97,65},{2,98}... | collective-permute-start | bytes 3342344 | tf_op jit(solution)/shard_map/ppermute | solution.py:28
  217.0 42.2 %collective-permute-start.33 = (bf16[4,2,32,2176]{3,2,0,1:T(8,128)(2,1)}, bf16[4,2,32,2176]{3,2,0,1:T(8,128)(2,1)}, u32[]{:S(2)}, u32[]{:S(2)}) collective-permute-start(bf16[4,2,32,2176]{3,2,0,1:T(8,128)(2,1)} %bitcast_dynamic-update-slice_fusion.35), channel_id=1, source_target_pairs={{0,2},{2,4},{4,6},{6,0},{1,3},{3,5},{5,7},{7,1},{8,10},{10,12},{12... | collective-permute-start | bytes 3342344 | tf_op jit(solution)/shard_map/ppermute | solution.py:28
  217.0 45.3 %collective-permute-start.34 = (bf16[4,2,32,2176]{3,2,0,1:T(8,128)(2,1)}, bf16[4,2,32,2176]{3,2,0,1:T(8,128)(2,1)}, u32[]{:S(2)}, u32[]{:S(2)}) collective-permute-start(bf16[4,2,32,2176]{3,2,0,1:T(8,128)(2,1)} %bitcast_dynamic-update-slice_fusion.35), channel_id=1, source_target_pairs={{0,6},{2,0},{4,2},{6,4},{1,7},{3,1},{5,3},{7,5},{8,14},{10,8},{12,... | collective-permute-start | bytes 3342344 | tf_op jit(solution)/shard_map/ppermute | solution.py:28
  239.3 35.7 %collective-permute-start.27 = (bf16[128,2048]{1,0:T(8,128)(2,1)}, bf16[128,2048]{1,0:T(8,128)(2,1)}, u32[]{:S(2)}, u32[]{:S(2)}) collective-permute-start(bf16[128,2048]{1,0:T(8,128)(2,1)} %multiply_convert_fusion.4), channel_id=1, source_target_pairs={{0,8},{8,0},{1,9},{9,1},{2,10},{10,2},{3,11},{11,3},{4,12},{12,4},... | collective-permute-start | bytes 1572872 | tf_op jit(solution)/shard_map/ppermute | solution.py:28
  246.8 91.8 %all-to-all-start.2 = ((bf16[64,16,2048]{2,1,0:T(8,128)(2,1)}), bf16[64,16,2048]{2,1,0:T(8,128)(2,1)}, u32[]{:S(2)}, u32[]{:S(2)}) async-start(bf16[64,16,2048]{2,1,0:T(8,128)(2,1)} %bitcast.826), calls=%async_computation.2 | async-start | bytes 8388608 | tf_op jit(solution)/shard_map/all_to_all | solution.py:421
  254.5 59.7 %collective-permute-start.43 = (bf16[2,2,32,2176]{3,2,0,1:T(8,128)(2,1)}, bf16[2,2,32,2176]{3,2,0,1:T(8,128)(2,1)}, u32[]{:S(2)}, u32[]{:S(2)}) collective-permute-start(bf16[2,2,32,2176]{3,2,0,1:T(8,128)(2,1)} %slice.693), channel_id=1, source_target_pairs={{0,32},{32,64},{64,96},{96,0},{1,33},{33,65},{65,97},{97,1},{2,34}... | collective-permute-start | bytes 1671176 | tf_op jit(solution)/shard_map/ppermute | solution.py:28
  257.7 58.4 %collective-permute-start.44 = (bf16[2,2,32,2176]{3,2,0,1:T(8,128)(2,1)}, bf16[2,2,32,2176]{3,2,0,1:T(8,128)(2,1)}, u32[]{:S(2)}, u32[]{:S(2)}) collective-permute-start(bf16[2,2,32,2176]{3,2,0,1:T(8,128)(2,1)} %slice.694), channel_id=1, source_target_pairs={{0,96},{32,0},{64,32},{96,64},{1,97},{33,1},{65,33},{97,65},{2,98}... | collective-permute-start | bytes 1671176 | tf_op jit(solution)/shard_map/ppermute | solution.py:28
  261.1 56.9 %collective-permute-start.35 = (bf16[2,2,32,2176]{3,2,0,1:T(8,128)(2,1)}, bf16[2,2,32,2176]{3,2,0,1:T(8,128)(2,1)}, u32[]{:S(2)}, u32[]{:S(2)}) collective-permute-start(bf16[2,2,32,2176]{3,2,0,1:T(8,128)(2,1)} %slice.689), channel_id=1, source_target_pairs={{0,2},{2,4},{4,6},{6,0},{1,3},{3,5},{5,7},{7,1},{8,10},{10,12},{12... | collective-permute-start | bytes 1671176 | tf_op jit(solution)/shard_map/ppermute | solution.py:28
  264.2 55.7 %collective-permute-start.36 = (bf16[2,2,32,2176]{3,2,0,1:T(8,128)(2,1)}, bf16[2,2,32,2176]{3,2,0,1:T(8,128)(2,1)}, u32[]{:S(2)}, u32[]{:S(2)}) collective-permute-start(bf16[2,2,32,2176]{3,2,0,1:T(8,128)(2,1)} %slice.690), channel_id=1, source_target_pairs={{0,6},{2,0},{4,2},{6,4},{1,7},{3,1},{5,3},{7,5},{8,14},{10,8},{12,... | collective-permute-start | bytes 1671176 | tf_op jit(solution)/shard_map/ppermute | solution.py:28
  338.6 60.5 %all-to-all-start.3 = ((bf16[64,16,2048]{2,1,0:T(8,128)(2,1)}), bf16[64,16,2048]{2,1,0:T(8,128)(2,1)}, u32[]{:S(2)}, u32[]{:S(2)}) async-start(bf16[64,16,2048]{2,1,0:T(8,128)(2,1)} %bitcast.825), calls=%async_computation.3 | async-start | bytes 8388608 | tf_op jit(solution)/shard_map/all_to_all | solution.py:421
  353.6 215.6 %collective-permute-start.48 = (bf16[128,2048]{1,0:T(8,128)(2,1)}, bf16[128,2048]{1,0:T(8,128)(2,1)}, u32[]{:S(2)}, u32[]{:S(2)}) collective-permute-start(bf16[128,2048]{1,0:T(8,128)(2,1)} %fusion.83), channel_id=1, source_target_pairs={{0,8},{8,0},{1,9},{9,1},{2,10},{10,2},{3,11},{11,3},{4,12},{12,4},... | collective-permute-start | bytes 1572872 | tf_op jit(solution)/shard_map/ppermute | solution.py:28
  358.1 290.2 %collective-permute-start.45 = (bf16[128,2048]{1,0:T(8,128)(2,1)}, bf16[128,2048]{1,0:T(8,128)(2,1)}, u32[]{:S(2)}, u32[]{:S(2)}) collective-permute-start(bf16[128,2048]{1,0:T(8,128)(2,1)} %fusion.82), channel_id=1, source_target_pairs={{0,8},{8,0},{1,9},{9,1},{2,10},{10,2},{3,11},{11,3},{4,12},{12,4},... | collective-permute-start | bytes 1572872 | tf_op jit(solution)/shard_map/ppermute | solution.py:28
  445.5 126.4 %all-to-all-start.4 = ((bf16[64,16,2048]{2,1,0:T(8,128)(2,1)}), bf16[64,16,2048]{2,1,0:T(8,128)(2,1)}, u32[]{:S(2)}, u32[]{:S(2)}) async-start(bf16[64,16,2048]{2,1,0:T(8,128)(2,1)} %bitcast.836), calls=%async_computation.4 | async-start | bytes 8388608 | tf_op jit(solution)/shard_map/all_to_all | solution.py:426
  481.2 34.3 %collective-permute-start.78 = (bf16[2,2,32,2176]{3,2,1,0:T(8,128)(2,1)S(1)}, bf16[2,2,32,2176]{3,2,1,0:T(8,128)(2,1)S(1)}, u32[]{:S(2)}, u32[]{:S(2)}) collective-permute-start(bf16[2,2,32,2176]{3,2,1,0:T(8,128)(2,1)S(1)} %get-tuple-element.72), channel_id=1, source_target_pairs={{0,6},{2,0},{4,2},{6,4},{1,7},{3,1},{5,3},{7,5},{8,14},{10,8},{12,... | collective-permute-start | bytes 1671176 | tf_op jit(solution)/shard_map/ppermute | solution.py:28
  483.9 33.1 %collective-permute-start.76 = (bf16[2,2,32,2176]{3,2,1,0:T(8,128)(2,1)S(1)}, bf16[2,2,32,2176]{3,2,1,0:T(8,128)(2,1)S(1)}, u32[]{:S(2)}, u32[]{:S(2)}) collective-permute-start(bf16[2,2,32,2176]{3,2,1,0:T(8,128)(2,1)S(1)} %get-tuple-element.71), channel_id=1, source_target_pairs={{0,2},{2,4},{4,6},{6,0},{1,3},{3,5},{5,7},{7,1},{8,10},{10,12},{12... | collective-permute-start | bytes 1671176 | tf_op jit(solution)/shard_map/ppermute | solution.py:28
  484.4 34.2 %collective-permute-start.86 = (bf16[2,2,32,2176]{3,2,1,0:T(8,128)(2,1)S(1)}, bf16[2,2,32,2176]{3,2,1,0:T(8,128)(2,1)S(1)}, u32[]{:S(2)}, u32[]{:S(2)}) collective-permute-start(bf16[2,2,32,2176]{3,2,1,0:T(8,128)(2,1)S(1)} %get-tuple-element.64), channel_id=1, source_target_pairs={{0,96},{32,0},{64,32},{96,64},{1,97},{33,1},{65,33},{97,65},{2,98}... | collective-permute-start | bytes 1671176 | tf_op jit(solution)/shard_map/ppermute | solution.py:28
  518.6 26.4 %collective-permute-start.77 = (bf16[4,2,32,2176]{3,2,1,0:T(8,128)(2,1)S(1)}, bf16[4,2,32,2176]{3,2,1,0:T(8,128)(2,1)S(1)}, u32[]{:S(2)}, u32[]{:S(2)}) collective-permute-start(bf16[4,2,32,2176]{3,2,1,0:T(8,128)(2,1)S(1)} %pad_maximum_fusion.6), channel_id=1, source_target_pairs={{0,2},{2,4},{4,6},{6,0},{1,3},{3,5},{5,7},{7,1},{8,10},{10,12},{12... | collective-permute-start | bytes 3342344 | tf_op jit(solution)/shard_map/ppermute | solution.py:28
  547.4 38.9 %collective-permute-start.80 = (bf16[1,32,2176]{2,1,0:T(8,128)(2,1)}, bf16[1,32,2176]{2,1,0:T(8,128)(2,1)}, u32[]{:S(2)}, u32[]{:S(2)}) collective-permute-start(bf16[1,32,2176]{2,1,0:T(8,128)(2,1)} %get-tuple-element.67), channel_id=1, source_target_pairs={{0,32},{32,64},{64,96},{96,0},{1,33},{33,65},{65,97},{97,1},{2,34}... | collective-permute-start | bytes 417800 | tf_op jit(solution)/shard_map/ppermute | solution.py:28
  554.2 32.2 %collective-permute-start.82 = (bf16[1,32,2176]{2,1,0:T(8,128)(2,1)}, bf16[1,32,2176]{2,1,0:T(8,128)(2,1)}, u32[]{:S(2)}, u32[]{:S(2)}) collective-permute-start(bf16[1,32,2176]{2,1,0:T(8,128)(2,1)} %get-tuple-element.69), channel_id=1, source_target_pairs={{0,96},{32,0},{64,32},{96,64},{1,97},{33,1},{65,33},{97,65},{2,98}... | collective-permute-start | bytes 417800 | tf_op jit(solution)/shard_map/ppermute | solution.py:28
  575.4 73.0 %all-to-all-start.5 = ((bf16[64,16,2048]{2,1,0:T(8,128)(2,1)}), bf16[64,16,2048]{2,1,0:T(8,128)(2,1)}, u32[]{:S(2)}, u32[]{:S(2)}) async-start(bf16[64,16,2048]{2,1,0:T(8,128)(2,1)} %bitcast.851), calls=%async_computation.5 | async-start | bytes 8388608 | tf_op jit(solution)/shard_map/all_to_all | solution.py:426
  588.4 51.2 %collective-permute-start.83 = (bf16[2,32,2176]{2,1,0:T(8,128)(2,1)S(1)}, bf16[2,32,2176]{2,1,0:T(8,128)(2,1)S(1)}, u32[]{:S(2)}, u32[]{:S(2)}) collective-permute-start(bf16[2,32,2176]{2,1,0:T(8,128)(2,1)S(1)} %pad_maximum_fusion.23), channel_id=1, source_target_pairs={{0,96},{32,0},{64,32},{96,64},{1,97},{33,1},{65,33},{97,65},{2,98}... | collective-permute-start | bytes 835592 | tf_op jit(solution)/shard_map/ppermute | solution.py:28
  591.3 51.3 %collective-permute-start.81 = (bf16[2,32,2176]{2,1,0:T(8,128)(2,1)S(1)}, bf16[2,32,2176]{2,1,0:T(8,128)(2,1)S(1)}, u32[]{:S(2)}, u32[]{:S(2)}) collective-permute-start(bf16[2,32,2176]{2,1,0:T(8,128)(2,1)S(1)} %pad_maximum_fusion.22), channel_id=1, source_target_pairs={{0,32},{32,64},{64,96},{96,0},{1,33},{33,65},{65,97},{97,1},{2,34}... | collective-permute-start | bytes 835592 | tf_op jit(solution)/shard_map/ppermute | solution.py:28
  592.9 49.8 %collective-permute-start.91 = (bf16[2,32,2176]{2,1,0:T(8,128)(2,1)S(1)}, bf16[2,32,2176]{2,1,0:T(8,128)(2,1)S(1)}, u32[]{:S(2)}, u32[]{:S(2)}) collective-permute-start(bf16[2,32,2176]{2,1,0:T(8,128)(2,1)S(1)} %pad_maximum_fusion.25), channel_id=1, source_target_pairs={{0,6},{2,0},{4,2},{6,4},{1,7},{3,1},{5,3},{7,5},{8,14},{10,8},{12,... | collective-permute-start | bytes 835592 | tf_op jit(solution)/shard_map/ppermute | solution.py:28
  595.5 47.3 %collective-permute-start.89 = (bf16[2,32,2176]{2,1,0:T(8,128)(2,1)S(1)}, bf16[2,32,2176]{2,1,0:T(8,128)(2,1)S(1)}, u32[]{:S(2)}, u32[]{:S(2)}) collective-permute-start(bf16[2,32,2176]{2,1,0:T(8,128)(2,1)S(1)} %pad_maximum_fusion.24), channel_id=1, source_target_pairs={{0,2},{2,4},{4,6},{6,0},{1,3},{3,5},{5,7},{7,1},{8,10},{10,12},{12... | collective-permute-start | bytes 835592 | tf_op jit(solution)/shard_map/ppermute | solution.py:28
  654.5 28.3 %all-to-all-start.7 = ((f32[2,32,2176]{2,1,0:T(8,128)}), f32[2,32,2176]{2,1,0:T(8,128)}, u32[]{:S(2)}, u32[]{:S(2)}) async-start(f32[2,32,2176]{2,1,0:T(8,128)} %convert_add_fusion.13), calls=%async_computation.7 | async-start | bytes 1114112 | tf_op jit(solution)/shard_map/all_to_all | solution.py:107
  743.8 33.1 %collective-permute-start.57 = (bf16[128,2048]{1,0:T(8,128)(2,1)}, bf16[128,2048]{1,0:T(8,128)(2,1)}, u32[]{:S(2)}, u32[]{:S(2)}) collective-permute-start(bf16[128,2048]{1,0:T(8,128)(2,1)} %fusion.84), channel_id=1, source_target_pairs={{0,8},{8,0},{1,9},{9,1},{2,10},{10,2},{3,11},{11,3},{4,12},{12,4},... | collective-permute-start | bytes 1572872 | tf_op jit(solution)/shard_map/ppermute | solution.py:28
  785.6 32.0 %collective-permute-start.62 = (bf16[4,2,32,2176]{3,2,1,0:T(8,128)(2,1)S(1)}, bf16[4,2,32,2176]{3,2,1,0:T(8,128)(2,1)S(1)}, u32[]{:S(2)}, u32[]{:S(2)}) collective-permute-start(bf16[4,2,32,2176]{3,2,1,0:T(8,128)(2,1)S(1)} %pad_maximum_fusion.3), channel_id=1, source_target_pairs={{0,6},{2,0},{4,2},{6,4},{1,7},{3,1},{5,3},{7,5},{8,14},{10,8},{12,... | collective-permute-start | bytes 3342344 | tf_op jit(solution)/shard_map/ppermute | solution.py:28
  792.2 25.5 %collective-permute-start.60 = (bf16[4,2,32,2176]{3,2,1,0:T(8,128)(2,1)S(1)}, bf16[4,2,32,2176]{3,2,1,0:T(8,128)(2,1)S(1)}, u32[]{:S(2)}, u32[]{:S(2)}) collective-permute-start(bf16[4,2,32,2176]{3,2,1,0:T(8,128)(2,1)S(1)} %pad_maximum_fusion.2), channel_id=1, source_target_pairs={{0,2},{2,4},{4,6},{6,0},{1,3},{3,5},{5,7},{7,1},{8,10},{10,12},{12... | collective-permute-start | bytes 3342344 | tf_op jit(solution)/shard_map/ppermute | solution.py:28
  (160 other events, 1998.2 us)

commit v2 on v1

v2 whole, which is shorter than its diff:
```python
import functools

import jax
import jax.numpy as jnp
import numpy as np
from jax import lax
from jax.experimental import pallas as pl
from jax.experimental.pallas import tpu as pltpu
from jax.sharding import Mesh
from jax.sharding import PartitionSpec as P

NOPE = 128
ROPE = 64
VDIM = 128
LATENT = 512
HEAD = NOPE + ROPE
EPS = 1e-06
SCALE = HEAD ** (-0.5)
F32 = jnp.float32
BF16 = jnp.bfloat16


def dot(left, right, left_dim=1, right_dim=0):
    return lax.dot_general(
        left, right, (((left_dim,), (right_dim,)), ((), ())), preferred_element_type=F32
    )


def shift(values, axis, step):
    size = lax.axis_size(axis)
    return lax.ppermute(values, axis, [(j, (j + step) % size) for j in range(size)])


def diagonal(values):
    return lax.ppermute(values, ("z", "c"), [(0, 3), (1, 2), (2, 1), (3, 0)])


def pick(buffer, index):
    return lax.dynamic_index_in_dim(buffer, index, 0, keepdims=False)


def in_order(own, other, index):
    return jnp.stack([jnp.where(index == 0, own, other), jnp.where(index == 0, other, own)])


def gather_rows(halves, at):
    x, z, core, y = (lax.axis_index(name) for name in ("x", "z", "c", "y"))
    lanes = halves.shape[-1]
    keep, send = pick(halves, core), pick(halves, 1 - core)
    across, beside, corner = shift(send, "c", 1), shift(keep, "z", 1), diagonal(send)
    final = jnp.zeros((4, 2, 2, 4, 32, lanes), halves.dtype)

    def put_one(buffer, piece, level, place):
        start = (0, level, core, place % 4, 0, 0)
        return lax.dynamic_update_slice(buffer, piece.reshape(4, 1, 1, 1, 32, lanes), start)

    def put_two(buffer, piece, level, place):
        start = (place % 4, level, 1 - core, 0, 0, 0)
        return lax.dynamic_update_slice(buffer, piece.reshape(1, 1, 1, 4, 32, lanes), start)

    first = [line_up(at, 0, keep, "x"), line_up(at, 0, beside, "x")]
    second = [line_up(at, 3, across, "y"), line_up(at, 3, corner, "y")]
    levels = (z, 1 - z)
    for put, lines, axis, place in ((put_one, first, "y", y), (put_two, second, "x", x)):
        for line, level in zip(lines, levels, strict=True):
            final = put(final, line, level, place)
    near = {}
    for name, lines, axis in (("one", first, "y"), ("two", second, "x")):
        near[name] = [(shift(line, axis, 1), shift(line, axis, -1)) for line in lines]
    far = {}
    for name, axis in (("one", "y"), ("two", "x")):
        far[name] = (shift(near[name][0][0], axis, 1), shift(near[name][1][1], axis, -1))
    for name, put, place in (("one", put_one, y), ("two", put_two, x)):
        for (left, right), level in zip(near[name], levels, strict=True):
            final = put(put(final, left, level, place + 3), right, level, place + 1)
    for name, put, place in (("one", put_one, y), ("two", put_two, x)):
        for piece, level in zip(far[name], levels, strict=True):
            final = put(final, piece, level, place + 2)
    return final.reshape(-1, lanes)


def line_kernel(index, at, *refs):
    for step in range(4):
        refs[4][lax.rem(at[index] + 4 - step, 4)] = refs[step][...]


def line_up(at, index, block, axis):
    blocks = [block] + [shift(block, axis, step) for step in (1, 2, 3)]
    return call(
        functools.partial(line_kernel, index), (4,) + block.shape, BF16, at, *blocks
    )


def ring_sum(parts, axis):
    low = shift(parts[2][0], axis, 1)
    high = shift(parts[2][1], axis, -1)
    right_high = shift(parts[1][1], axis, 1)
    left_low = shift(parts[3][0], axis, -1)
    right_low = shift(add_low(parts[1][0], low), axis, 1)
    left_high = shift(add_low(parts[3][1], high), axis, -1)
    return [add_low(parts[0][0], left_low, right_low), add_low(parts[0][1], right_high, left_high)]


def add_low(*values):
    return sum(value.astype(F32) for value in values).astype(BF16)


def direct_sum(line, axis):
    me = lax.axis_index(axis)
    got = [shift(pick(line, (me + step) % 4), axis, step) for step in (1, 2, 3)]
    return add_low(pick(line, me), *got)


def scatter_rows(one, two):
    one = [direct_sum(line, "x") for line in ring_sum(one, "y")]
    two = [direct_sum(line, "y") for line in ring_sum(two, "x")]
    beside, across, corner = shift(one[1], "z", 1), shift(two[0], "c", 1), diagonal(two[1])
    own = one[0].astype(F32) + beside.astype(F32)
    other = across.astype(F32) + corner.astype(F32)
    return in_order(own, other, lax.axis_index("c"))


def to_ring(pieces):
    return [pieces[0]] + [shift(pieces[step], "y", step) for step in (1, 2, 3)]


def half_sum(partial):
    low = partial.astype(BF16)
    return low.astype(F32) + shift(low, "t", 1).astype(F32)


def core_sum(own, other):
    return own + shift(other, "c", 1).astype(F32)


def call(kernel, shapes, dtypes, at, *operands, scratch=(), flops=1_000_000, many=False):
    if not many:
        shapes, dtypes = [shapes], [dtypes]
    out_shape = [jax.ShapeDtypeStruct(s, d) for s, d in zip(shapes, dtypes, strict=True)]
    moved = sum(o.size * o.dtype.itemsize for o in operands)
    moved += sum(int(np.prod(s)) * jnp.dtype(d).itemsize for s, d in zip(shapes, dtypes, strict=True))
    outs = pl.pallas_call(
        kernel,
        out_shape=out_shape,
        in_specs=[pl.BlockSpec(memory_space=pltpu.SMEM)]
        + [pl.BlockSpec(memory_space=pltpu.VMEM)] * len(operands),
        out_specs=[pl.BlockSpec(memory_space=pltpu.VMEM)] * len(out_shape),
        scratch_shapes=scratch,
        compiler_params=pltpu.CompilerParams(vmem_limit_bytes=56 * 1024 * 1024),
        cost_estimate=pl.CostEstimate(flops=flops, bytes_accessed=moved, transcendentals=0),
    )(at, *operands)
    return outs if many else outs[0]


MSG = 1024
QR = 256
KV = 384
KR = 896


def rows_at(index):
    return pl.ds(pl.multiple_of(index * 128, 128), 128)


def lanes_at(index, size, base=0):
    return pl.ds(pl.multiple_of(base + index * size, 128), size)


def owner(at, place):
    return jnp.bitwise_xor(lax.shift_right_logical(place, 1), at[2]), jnp.bitwise_and(place, 1)


def ahead(at, step):
    return lax.rem(at[3] + step, 4)


def behind(at, step):
    return lax.rem(at[3] + 4 - step, 4)


def turn(values, cosine, sine):
    return values * cosine + pltpu.roll(values, 64, 1) * sine


def project_kernel(
    at, own, other, weights, up, cosine, sine, m0, m1, m2, m3, normed, low, plain, inverse, query, keys, key
):
    for index, block in enumerate((own, other)):
        values = block[...].astype(F32)
        scale = lax.rsqrt(jnp.mean(values * values, axis=1, keepdims=True) + EPS)
        normed[index * 128 : index * 128 + 128] = (values * scale).astype(BF16)
    lin = dot(normed[...], weights[...])
    cos, sin = cosine[...], sine[...]
    query[:, :512] = lin[:, :512].astype(BF16)
    for pair in range(2):
        span = slice(512 + pair * 128, 640 + pair * 128)
        query[:, span] = turn(lin[:, span], cos, sin).astype(BF16)
    key[...] = turn(lin[:, 1280:], cos, sin).astype(BF16)
    latent = lin[:, 768:1280]
    scale = lax.rsqrt(jnp.mean(latent * latent, axis=1, keepdims=True) + EPS)
    latent = latent * scale
    plain[...] = latent
    low[...] = latent.astype(BF16)
    inverse[...] = jnp.broadcast_to(scale, inverse.shape)
    keys[...] = dot(low[...], up[...]).astype(BF16)
    for step, out in enumerate((m0, m1, m2, m3)):
        block, pair = owner(at, ahead(at, step))
        rows = rows_at(block)
        out[:, :QR] = query[rows, lanes_at(pair, 256)]
        out[:, QR:KV] = query[rows, lanes_at(pair, 128, 512)]
        out[:, KV:KR] = keys[rows, lanes_at(pair, 512)]
        out[:, KR:] = key[rows, :]


def head_lanes(rows, head):
    lane = lax.broadcasted_iota(jnp.int32, (rows, 128), 1)
    return jnp.where(((lane >> 5) & 1) == head, 1.0, 0.0).astype(F32)


def head_keys(msg_ref, head):
    rotated = msg_ref[:, :, KR:].reshape(512, 128).astype(F32) * head_lanes(512, head)
    plain = msg_ref[:, :, KV + head * 256 : KV + head * 256 + 128].reshape(512, 128)
    return jnp.concatenate([plain, rotated.astype(BF16)], axis=1)


def head_values(msg_ref, head):
    return msg_ref[:, :, KV + head * 256 + 128 : KV + head * 256 + 256].reshape(512, 128)


def block_probs(query, keys, row_ref, col_ref, block):
    count = (block + 1) * 128
    scores = dot(query, keys[:count], 1, 1) * SCALE
    rows = lax.broadcasted_iota(jnp.int32, (128, count), 0) + block * 128
    cols = lax.broadcasted_iota(jnp.int32, (128, count), 1)
    same = col_ref[block * 128 : count, :] == row_ref[:, :count]
    scores = jnp.where(same & (cols <= rows), scores, -1e30)
    powers = jnp.exp(scores - jnp.max(scores, axis=1, keepdims=True))
    return powers / jnp.sum(powers, axis=1, keepdims=True)


def block_query(msg_ref, head, block):
    return jnp.concatenate(
        [msg_ref[block, :, head * 128 : head * 128 + 128], msg_ref[block, :, QR:KV]], axis=1
    )


def forward_kernel(at, m0, m1, m2, m3, row_ref, col_ref, msg_ref, o0, o1, o2, o3, mixed):
    for step, piece in enumerate((m0, m1, m2, m3)):
        msg_ref[behind(at, step)] = piece[...]
    for head in range(2):
        keys = head_keys(msg_ref, head)
        values = head_values(msg_ref, head)
        for block in range(4):
            query = block_query(msg_ref, head, block)
            probs = block_probs(query, keys, row_ref, col_ref, block)
            part = dot(probs.astype(BF16), values[: (block + 1) * 128])
            mixed[block, :, head * 128 : head * 128 + 128] = part.astype(BF16)
    for step, out in enumerate((o0, o1, o2, o3)):
        out[...] = mixed[ahead(at, step)]


def output_kernel(at, p0, p1, p2, p3, weights, attended, own, other):
    for step, piece in enumerate((p0, p1, p2, p3)):
        block, pair = owner(at, behind(at, step))
        attended[rows_at(block), lanes_at(pair, 256)] = piece[...]
    own[...] = dot(attended[:128], weights[...], 1, 1)
    other[...] = dot(attended[128:], weights[...], 1, 1).astype(BF16)


def heads_kernel(at, own, other, weights, h0, h1, h2, h3, grad):
    grad[:128] = dot(own[...], weights[...]).astype(BF16)
    grad[128:] = dot(other[...], weights[...]).astype(BF16)
    for step, out in enumerate((h0, h1, h2, h3)):
        block, pair = owner(at, ahead(at, step))
        out[...] = grad[rows_at(block), lanes_at(pair, 256)]


def backward_kernel(
    at, msg_ref, g0, g1, g2, g3, row_ref, col_ref, o0, o1, o2, o3, grad_ref, out_ref, key_acc, value_acc
):
    for step, piece in enumerate((g0, g1, g2, g3)):
        grad_ref[behind(at, step)] = piece[...]
    for head in range(2):
        keys = head_keys(msg_ref, head)
        values = head_values(msg_ref, head)
        key_acc[...] = jnp.zeros_like(key_acc)
        value_acc[...] = jnp.zeros_like(value_acc)
        lanes = head_lanes(128, head)
        for block in range(4):
            count = (block + 1) * 128
            query = block_query(msg_ref, head, block)
            probs = block_probs(query, keys, row_ref, col_ref, block)
            grad = grad_ref[block, :, head * 128 : head * 128 + 128]
            probs_grad = dot(grad, values[:count], 1, 1)
            inner = jnp.sum(probs * probs_grad, axis=1, keepdims=True)
            score_grad = (probs * (probs_grad - inner) * SCALE).astype(BF16)
            query_grad = dot(score_grad, keys[:count])
            out_ref[block, :, head * 128 : head * 128 + 128] = query_grad[:, :128].astype(BF16)
            turned = query_grad[:, 128:]
            if head == 1:
                turned = turned + out_ref[block, :, QR:KV].astype(F32)
            out_ref[block, :, QR:KV] = turned.astype(BF16)
            key_acc[:count] += dot(score_grad, query, 0, 0)
            value_acc[:count] += dot(probs.astype(BF16), grad, 0, 0)
        base = KV + head * 256
        for block in range(4):
            span = slice(block * 128, block * 128 + 128)
            out_ref[block, :, base : base + 128] = key_acc[span, :128].astype(BF16)
            out_ref[block, :, base + 128 : base + 256] = value_acc[span, :].astype(BF16)
            turned = key_acc[span, 128:] * lanes
            if head == 1:
                turned = turned + out_ref[block, :, KR:].astype(F32)
            out_ref[block, :, KR:] = turned.astype(BF16)
    for step, out in enumerate((o0, o1, o2, o3)):
        out[...] = out_ref[ahead(at, step)]


def return_kernel(
    at, b0, b1, b2, b3, weights, up, cosine, sine, plain, inverse, lin_grad, kv_grad, own, other, key
):
    for step, piece in enumerate((b0, b1, b2, b3)):
        block, pair = owner(at, behind(at, step))
        rows = rows_at(block)
        lin_grad[rows, lanes_at(pair, 256)] = piece[:, :QR]
        turned = turn(piece[:, QR:KV].astype(F32), cosine[rows, :], -sine[rows, :])
        lin_grad[rows, lanes_at(pair, 128, 512)] = turned.astype(BF16)
        kv_grad[rows, lanes_at(pair, 512)] = piece[:, KV:KR]
        key[rows_at(block + 2 * pair), :] = piece[:, KR:].astype(F32)
    turned = turn(key[:256] + key[256:], cosine[...], -sine[...])
    lin_grad[:, 1280:] = turned.astype(BF16)
    grad = dot(kv_grad[...], up[...], 1, 1)
    latent = plain[...]
    grad = inverse[:, :1] * (grad - latent * jnp.mean(grad * latent, axis=1, keepdims=True))
    lin_grad[:, 768:1280] = grad.astype(BF16)
    own[...] = dot(lin_grad[:128], weights[...], 1, 1)
    other[...] = dot(lin_grad[128:], weights[...], 1, 1).astype(BF16)


def grads_kernel(at, normed, lin_grad, own, other, attended, up, tail, *refs):
    one, two, rows = refs[:8], refs[8:16], refs[16]
    for step in range(4):
        column = lax.rem(at[0] + step, 4)
        for side in range(2):
            level = at[1] if side == 0 else 1 - at[1]
            start = pl.multiple_of((column * 2 + level) * 256, 256)
            span = pl.ds(start, 256)
            part = dot(normed[:, span], lin_grad[...], 0, 0).astype(BF16)
            rows[:, :, :1408] = part.reshape(8, 32, 1408)
            part = dot(own[:, span], attended[:128], 0, 0) + dot(other[:, span], attended[128:], 0, 0)
            rows[:, :, 1408:1920] = part.astype(BF16).reshape(8, 32, 512)
            rows[:, :, 1920:2176] = up[span, :].reshape(8, 32, 256)
            rows[:, :, 2176:] = tail[span, :].reshape(8, 32, 128)
            for place in range(4):
                one[place * 2 + side][column] = rows[at[2] * 4 + ahead(at, place)]
            two[step * 2 + side][...] = rows[pl.ds((1 - at[2]) * 4, 4)]


def shared_grads_kernel(at, own, other, lin_grad, cot, cot_other, act, out):
    for block in range(8):
        span = slice(block * 256, block * 256 + 256)
        part = dot(own[:, span], lin_grad[:128], 0, 0) + dot(other[:, span], lin_grad[128:], 0, 0)
        part = part.astype(BF16).reshape(2, 4, 32, 1408)
        for core in range(2):
            out[block, :, core, :, :1408] = part[core]
        part = dot(cot[:, span], act[:128], 0, 0) + dot(cot_other[:, span], act[128:], 0, 0)
        part = part.astype(BF16).reshape(2, 4, 32, 704)
        for core in range(2):
            out[block, :, core, :, 1408:] = part[core]


def doc_positions(doc_row):
    places = jnp.arange(doc_row.shape[0], dtype=jnp.int32)
    starts = jnp.concatenate([jnp.ones((1,), bool), doc_row[1:] != doc_row[:-1]])
    begins = lax.cummax(jnp.where(starts, places, 0), axis=0)
    return places - begins


def norm_back(scaled, normed, inverse):
    return inverse * (scaled - normed * jnp.mean(scaled * normed, axis=1, keepdims=True))


def silu_parts(lin):
    sig = jax.nn.sigmoid(lin)
    return lin * sig, sig * (1.0 + lin * (1.0 - sig))


def rms(values):
    return lax.rsqrt(jnp.mean(values * values, axis=1, keepdims=True) + EPS)


def shards(
    tokens_in,
    documents,
    routes,
    attn_gain,
    query_weight,
    latent_down,
    latent_gain,
    latent_up,
    output_weight,
    ffn_gain,
    router,
    shared_gate,
    shared_up,
    shared_down,
    expert_gate,
    expert_up,
    expert_down,
    cotangent,
):
    core = lax.axis_index("c")
    spot = lax.axis_index("y")
    at = jnp.stack([lax.axis_index("x"), lax.axis_index("z"), core, spot]).astype(jnp.int32)
    expert = (lax.axis_index("x") * 4 + lax.axis_index("z") * 2 + core) * 4 + spot
    rows = tokens_in.shape[0]
    width = tokens_in.shape[1]
    experts_count = router.shape[1]
    capacity = 16
    every = ("x", "z", "c", "y")

    gain_col = attn_gain.astype(F32)[:, None]
    heads = query_weight.reshape(32, 2, 2, 2, HEAD)
    query_plain = heads[..., :NOPE].reshape(32, 2, 512)
    query_turn = heads[..., NOPE:].reshape(32, 2, 2, 2, 2, 32).transpose(0, 1, 2, 4, 3, 5)
    query_pack = jnp.concatenate([query_plain, query_turn.reshape(32, 2, 256)], axis=2)
    query_pack = query_pack.transpose(1, 0, 2)
    down_pack = jnp.concatenate(
        [latent_down[:, :544], latent_down[:, 512:], latent_down[:, 544:]], axis=1
    )
    up_pack = latent_up.reshape(8, 2, 4, 256).transpose(1, 0, 2, 3)
    up_scaled = (up_pack.astype(F32) * latent_gain.astype(F32)[None, :, None, None]).astype(BF16)
    shared_pack = jnp.concatenate(
        [
            shared_gate.reshape(32, 2, 704),
            shared_up.reshape(32, 2, 704),
            shared_down.reshape(2, 704, 32).transpose(2, 0, 1),
        ],
        axis=2,
    )
    both = jnp.concatenate([router, ffn_gain[:, None]], axis=1)
    pack = jnp.concatenate(
        [
            (query_pack.astype(F32) * gain_col).astype(BF16),
            jnp.broadcast_to((down_pack.astype(F32) * gain_col).astype(BF16), (2, 32, 640)),
            output_weight.reshape(2, 512, 32).transpose(0, 2, 1),
            up_scaled.reshape(2, 32, 256),
            shared_pack.transpose(1, 0, 2),
            jnp.broadcast_to(jnp.pad(both, ((0, 0), (0, 63))), (2, 32, 128)),
        ],
        axis=2,
    )
    weights = gather_rows(pack, at)
    in_all = weights[:, :1408]
    out_all = weights[:, 1408:1920]
    up_all = weights[:, 1920:2176].reshape(LATENT, 1024)
    gate_up_all = weights[:, 2176:3584]
    down_all = weights[:, 3584:4288]
    router_all = weights[:, 4288:4352]

    named = jnp.any(
        routes.T[None, :, :] == jnp.arange(experts_count, dtype=jnp.int32)[:, None, None], axis=1
    )
    before = jnp.arange(rows)[:, None] < jnp.arange(rows)[None, :]
    place = dot(named.astype(BF16), before.astype(BF16))
    slots = (
        named[:, None, :] & (place[:, None, :] == jnp.arange(capacity, dtype=F32)[None, :, None])
    ).astype(BF16)
    slots = slots.reshape(experts_count * capacity, rows)

    def to_experts(values):
        sent = dot(slots, values).astype(BF16).reshape(experts_count, capacity, width)
        got = lax.all_to_all(sent, every, split_axis=0, concat_axis=0, tiled=True)
        return got.reshape(-1, width)

    def return_rows(values):
        sent = values.reshape(experts_count, capacity, width)
        got = lax.all_to_all(sent, every, split_axis=0, concat_axis=0, tiled=True)
        return got.reshape(-1, width)

    cot_sent, in_all = lax.optimization_barrier((cotangent, in_all))
    expert_cot = to_experts(cot_sent)

    docs = jnp.concatenate([documents, shift(documents, "c", 1)])
    positions = jax.vmap(doc_positions)(docs)
    local_pos = lax.dynamic_slice_in_dim(positions, spot * rows, rows, axis=1).reshape(-1)
    steps = jnp.arange(ROPE // 2, dtype=F32)
    angles = local_pos.astype(F32)[:, None] * (10000.0 ** (-steps / (ROPE // 2)))[None, :]
    cosine = jnp.tile(jnp.cos(angles), (1, 4))
    sine = jnp.sin(angles)
    sine = jnp.concatenate([-sine, -sine, sine, sine], axis=1)
    doc = jnp.where(spot // 2 == core, docs[0], docs[1])
    doc_row, doc_col = doc[None, :], doc[:, None]

    tokens_other = shift(tokens_in, "c", 1)
    sent = [(rows, MSG)] * 4
    two = 2 * rows
    *sent, normed_low, latent_low, latent_normed, latent_inverse = call(
        project_kernel,
        sent + [(two, width), (two, LATENT), (two, LATENT), (two, 128)],
        [BF16] * 6 + [F32, F32],
        at,
        tokens_in,
        tokens_other,
        in_all,
        up_all,
        cosine,
        sine,
        scratch=[
            pltpu.VMEM((two, 768), BF16),
            pltpu.VMEM((two, 1024), BF16),
            pltpu.VMEM((two, 128), BF16),
        ],
        flops=1_800_000_000,
        many=True,
    )
    received = to_ring(sent)
    received[0], expert_cot = lax.optimization_barrier((received[0], expert_cot))
    msg, *mixed = call(
        forward_kernel,
        [(4, rows, MSG)] + [(rows, 256)] * 4,
        [BF16] * 5,
        at,
        *received,
        doc_row,
        doc_col,
        scratch=[pltpu.VMEM((4, rows, 256), BF16)],
        flops=500_000_000,
        many=True,
    )
    attended, out_own, out_other = call(
        output_kernel,
        [(two, 512), (rows, width), (rows, width)],
        [BF16, F32, BF16],
        at,
        *to_ring(mixed),
        out_all,
        flops=600_000_000,
        many=True,
    )
    tokens_f = tokens_in.astype(F32)
    resid = tokens_f + half_sum(core_sum(out_own, out_other))

    pointer = jnp.broadcast_to(jnp.arange(64)[None, :] == 0, (8, 64)).astype(BF16)
    gain_two = dot(pointer, weights[:, 4352:], 1, 1)[:1]
    inverse_two = rms(resid)
    normed_two = resid * inverse_two
    ffn_in = (normed_two * gain_two).astype(BF16)
    expert_rows = to_experts(ffn_in)

    ffn_other = shift(ffn_in, "c", 1)
    cot_other = shift(cotangent, "c", 1)
    ffn_two = jnp.concatenate([ffn_in, ffn_other])
    cot_two = jnp.concatenate([cotangent, cot_other])
    shared_lin = dot(ffn_two, gate_up_all)
    shared_up_lin = shared_lin[:, 704:]
    shared_silu, shared_slope = silu_parts(shared_lin[:, :704])
    shared_act = (shared_silu * shared_up_lin).astype(BF16)
    shared_dact = dot(cot_two, down_all)
    shared_dlin = jnp.concatenate(
        [shared_dact * shared_up_lin * shared_slope, shared_dact * shared_silu], axis=1
    ).astype(BF16)
    shared_out = dot(shared_act, down_all, 1, 1)
    shared_out = core_sum(shared_out[:rows], shared_out[rows:].astype(BF16))
    shared_back = dot(shared_dlin, gate_up_all, 1, 1)
    shared_back = core_sum(shared_back[:rows], shared_back[rows:].astype(BF16))
    shared_grads = call(
        shared_grads_kernel,
        (8, 4, 2, 32, 2112),
        BF16,
        at,
        ffn_in,
        ffn_other,
        shared_dlin,
        cotangent,
        cot_other,
        shared_act,
        flops=2_200_000_000,
    )
    shared_sum = lax.psum_scatter(
        shared_grads.reshape(width, -1), ("x", "z", "y"), scatter_dimension=0, tiled=True
    ).reshape(2, 32, -1)

    gate_w, up_w, down_w = expert_gate[0], expert_up[0], expert_down[0]
    plain_grad = dot(expert_cot, down_w, 1, 1)
    expert_rows, shared_back, shared_out, plain_grad, shared_grads = lax.optimization_barrier(
        (expert_rows, shared_back, shared_out, plain_grad, shared_grads)
    )
    probs = jax.nn.softmax(dot(expert_rows, router_all), axis=1)
    mine = (jnp.arange(experts_count, dtype=jnp.int32) == expert)[None, :].astype(F32)
    gate = jnp.sum(probs * mine, axis=1, keepdims=True)
    gate_lin = dot(expert_rows, gate_w)
    up_lin = dot(expert_rows, up_w)
    silu, slope = silu_parts(gate_lin)
    act = silu * up_lin
    act_low = (gate * act).astype(BF16)
    inner = jnp.sum(act * plain_grad, axis=1, keepdims=True)
    act_grad = gate * plain_grad
    gate_grad = (act_grad * up_lin * slope).astype(BF16)
    up_grad = (act_grad * silu).astype(BF16)
    logit_grad = (inner * gate * (mine - probs)).astype(BF16)
    row_grad = (
        dot(gate_grad, gate_w, 1, 1) + dot(up_grad, up_w, 1, 1) + dot(logit_grad, router_all, 1, 1)
    ).astype(BF16)
    back_rows = return_rows(row_grad)
    piece = dot(act_low, down_w).astype(BF16)
    expert_down_grad = dot(act_low, expert_cot, 0, 0)[None]
    expert_gate_grad = dot(expert_rows, gate_grad, 0, 0)[None]
    expert_up_grad = dot(expert_rows, up_grad, 0, 0)[None]
    router_grad = dot(expert_rows, logit_grad, 0, 0)
    back_rows, piece, expert_down_grad, expert_gate_grad, expert_up_grad, router_grad = (
        lax.optimization_barrier(
            (back_rows, piece, expert_down_grad, expert_gate_grad, expert_up_grad, router_grad)
        )
    )
    routed_back = dot(slots, back_rows, 0, 0)
    cot_f = cotangent.astype(F32)
    ffn_grad = half_sum(shared_back + routed_back)
    resid_grad = cot_f + norm_back(ffn_grad * gain_two, normed_two, inverse_two)
    first_lane = jnp.broadcast_to(jnp.arange(64)[None, :] == 0, (rows, 64)).astype(BF16)
    ffn_gain_part = dot((ffn_grad * normed_two).astype(BF16), first_lane, 0, 0)

    resid_low = resid_grad.astype(BF16)
    resid_other = shift(resid_low, "c", 1)
    heads_grad = call(
        heads_kernel,
        [(rows, 256)] * 4,
        [BF16] * 4,
        at,
        resid_low,
        resid_other,
        out_all,
        scratch=[pltpu.VMEM((two, 512), BF16)],
        flops=600_000_000,
        many=True,
    )
    heads_got = to_ring(heads_grad)
    piece, heads_got[0] = lax.optimization_barrier((piece, heads_got[0]))
    back = call(
        backward_kernel,
        [(rows, MSG)] * 4,
        [BF16] * 4,
        at,
        msg,
        *heads_got,
        doc_row,
        doc_col,
        scratch=[
            pltpu.VMEM((4, rows, 256), BF16),
            pltpu.VMEM((4, rows, MSG), BF16),
            pltpu.VMEM((512, 256), F32),
            pltpu.VMEM((512, 128), F32),
        ],
        flops=1_500_000_000,
        many=True,
    )
    lin_grad, kv_grad, in_own, in_other = call(
        return_kernel,
        [(two, 1408), (two, 1024), (rows, width), (rows, width)],
        [BF16, BF16, F32, BF16],
        at,
        *to_ring(back),
        in_all,
        up_all,
        cosine,
        sine,
        latent_normed,
        latent_inverse,
        scratch=[pltpu.VMEM((512, 128), F32)],
        flops=1_800_000_000,
        many=True,
    )
    up_part = dot(latent_low, kv_grad, 0, 0).astype(BF16).reshape(width, 256)
    tail = jnp.concatenate([router_grad, ffn_gain_part], axis=1).astype(BF16)
    pieces = call(
        grads_kernel,
        [(4, 32, 2304)] * 16,
        [BF16] * 16,
        at,
        normed_low,
        lin_grad,
        resid_low,
        resid_other,
        attended,
        up_part,
        tail,
        scratch=[pltpu.VMEM((8, 32, 2304), BF16)],
        flops=2_200_000_000,
        many=True,
    )
    pairs = [pieces[2 * i : 2 * i + 2] for i in range(8)]
    attn_sum = scatter_rows(pairs[:4], pairs[4:])

    attn_in_grad = half_sum(core_sum(in_own, in_other))
    inverse_one = rms(tokens_f)
    input_grad = resid_grad + norm_back(attn_in_grad, tokens_f * inverse_one, inverse_one)
    routed_out = dot(slots, return_rows(piece), 0, 0)
    layer_out = (resid + half_sum(shared_out + routed_out)).astype(BF16)

    shared_sum = lax.all_to_all(shared_sum, "c", split_axis=0, concat_axis=0, tiled=True)
    shared_sum = shared_sum.astype(F32)
    query_sum = attn_sum[..., :768]
    up_sum = attn_sum[..., 1920:2176]
    down_sum = attn_sum[0, :, 768:1408] + attn_sum[1, :, 768:1408]
    down_sum = jnp.concatenate(
        [
            down_sum[:, :512],
            down_sum[:, 512:544] + down_sum[:, 544:576],
            down_sum[:, 576:608] + down_sum[:, 608:],
        ],
        axis=1,
    )
    attn_gain_part = jnp.sum(query_pack.astype(F32) * query_sum, axis=(0, 2)) + jnp.sum(
        latent_down.astype(F32) * down_sum, axis=1
    )
    latent_gain_part = jnp.sum(up_pack.reshape(2, 32, 256).astype(F32) * up_sum, axis=(0, 2))
    tail_sum = attn_sum[0, :, 2176:] + attn_sum[1, :, 2176:]
    small = jnp.concatenate(
        [down_sum, tail_sum[:, :64], attn_gain_part[:, None], latent_gain_part[:, None]], axis=1
    )
    small = small + shift(small, "t", 1)
    attn_gain_grad = small[:, 640]
    latent_gain_grad = jnp.sum(small[:, 641].reshape(8, 4), axis=1)
    latent_down_grad = gain_col * small[:, :576]
    router_out = small[:, 576:640]
    query_plain = query_sum[..., :512].reshape(2, 32, 2, 2, NOPE)
    query_turn = query_sum[..., 512:].reshape(2, 32, 2, 2, 2, 32).transpose(0, 1, 2, 4, 3, 5)
    query_turn = query_turn.reshape(2, 32, 2, 2, ROPE)
    query_out = jnp.concatenate([query_plain, query_turn], axis=4).transpose(1, 0, 2, 3, 4)
    query_out = gain_col * query_out.reshape(32, 2 * 4 * HEAD)
    up_out = up_sum.reshape(2, 8, 4, 256).transpose(1, 0, 2, 3).reshape(8, 2048)
    up_out = latent_gain.astype(F32)[:, None] * up_out
    out_out = attn_sum[..., 1408:1920].transpose(0, 2, 1).reshape(1024, 32)
    ffn_gain_grad = tail_sum[:, 64]
    shared_rows = shared_sum.transpose(1, 0, 2)
    return (
        layer_out,
        input_grad,
        attn_gain_grad,
        query_out,
        latent_down_grad,
        latent_gain_grad,
        up_out,
        out_out,
        ffn_gain_grad,
        router_out,
        shared_rows[..., :704].reshape(32, 1408),
        shared_rows[..., 704:1408].reshape(32, 1408),
        shared_sum[..., 1408:2112].transpose(0, 2, 1).reshape(1408, 32),
        expert_gate_grad,
        expert_up_grad,
        expert_down_grad,
    )


def solution(mesh):
    fine = Mesh(mesh.devices.reshape(4, 2, 2, 4, 2), ("x", "z", "c", "y", "t"))
    fsdp = ("x", "z", "c")
    every = ("x", "z", "c", "y")
    in_specs = (
        P(every, None),
        P(fsdp, None),
        P(every, None),
        P(every),
        P(every, "t"),
        P(every, None),
        P(every),
        P(every, "t"),
        P("t", every),
        P(every),
        P(every, None),
        P(every, "t"),
        P(every, "t"),
        P("t", every),
        P(every, None, "t"),
        P(every, None, "t"),
        P(every, "t", None),
        P(every, None),
    )
    out_specs = (
        P(every, None),
        P(every, None),
        P(every),
        P(every, "t"),
        P(every, None),
        P(every),
        P(every, "t"),
        P("t", every),
        P(every),
        P(every, None),
        P(every, "t"),
        P(every, "t"),
        P("t", every),
        P(every, None, "t"),
        P(every, None, "t"),
        P(every, "t", None),
    )
    return jax.shard_map(shards, mesh=fine, in_specs=in_specs, out_specs=out_specs, check_vma=False)
```

time: 878 us -> 824 us (0.938)
  local copies, waits for them, and re-layouts: 203 us -> 90.4 us
  waiting for transfers between devices: 250 us -> 334 us
  Pallas kernels: 7.34 us -> 63.7 us
  matrix products: 137 us -> 96.7 us
  other arithmetic: 74.8 us -> 38.7 us
  blocking collectives: 20.4 us -> 6.19 us
  between operations: 3.49 us -> 15.8 us
    pallas_call x2 -> x12, Pallas kernels: 7.34 us -> 63.7 us  [call(): pl.pallas_call(kernel, out_shape=out_shape, in_specs=[pl.BlockSpec(memory...]
    dot_general x34 -> x24, matrix products: 137 us -> 96.7 us  [dot(): lax.dot_general(left, right, (((left_dim,), (right_dim,)), ((), ())), pre...]
    ppermute x94 -> x78, waiting for transfers between devices: 240 us -> 276 us  [shift(): lax.ppermute(values, axis, [(j, (j + step) % size) for j in range(size)])]
    concatenate x9 -> x1, local copies, waits for them, and re-layouts: 34.3 us -> 0.09 us  [shards(): jnp.concatenate([down_sum, tail_sum[:, :64], attn_gain_part[:, None], lat...]
    another operation x24 -> x5, other arithmetic: 30.2 us -> 1.66 us  [the longest x2 15.9 us: gather_rows(): jnp.stack([one.transpose(1, 2, 0, 3, 4), two.transpose(0, 2, 1, 3, 4)], a...]
    all_to_all x2, waiting for transfers between devices: 8.96 us -> 32.6 us  [to_experts(): got = lax.all_to_all(sent, every, split_axis=0, concat_axis=0, tiled=True)]
    slice x45 -> x10, local copies, waits for them, and re-layouts: 36.7 us -> 16.1 us  [the longest x1 5.51 us: shards(): in_all = weights[:, :1408]]
    another operation x20 -> x2, local copies, waits for them, and re-layouts: 20.6 us -> 0.55 us
  transfers between devices with their start and end apart: 100 -> 85, of which waited for: 28 -> 36; matrix products, arithmetic and copies ran while one was open for 38% -> 18% of each run, Pallas kernels for 0% -> 6%
where the time goes in v2:
time: 824 us; the launch traced here: 813 us
  waiting for transfers between devices  334 us (41%)
  starting transfers between devices  167 us (20%)
  matrix products  96.7 us (12%)
  local copies, waits for them, and re-layouts  90.4 us (11%)
  Pallas kernels  63.7 us (8%)
  other arithmetic  38.7 us (5%)
  between operations  15.8 us (2%)
    ppermute x78, waiting for transfers between devices, shift(): lax.ppermute(values, axis, [(j, (j + step) % size) for j in range(size)])  276 us
    ppermute x78, starting transfers between devices, shift(): lax.ppermute(values, axis, [(j, (j + step) % size) for j in range(size)])  114 us
    dot_general x24, matrix products, dot(): lax.dot_general(left, right, (((left_dim,), (right_dim,)), ((), ())), pre...  96.7 us
    pallas_call x12, Pallas kernels, call(): pl.pallas_call(kernel, out_shape=out_shape, in_specs=[pl.BlockSpec(memory...  63.7 us
    all_to_all x2, waiting for transfers between devices, to_experts(): got = lax.all_to_all(sent, every, split_axis=0, concat_axis=0, tiled=True)  32.6 us
    all_to_all x2, starting transfers between devices, to_experts(): got = lax.all_to_all(sent, every, split_axis=0, concat_axis=0, tiled=True)  26.5 us
    all_to_all x2, waiting for transfers between devices, return_rows(): got = lax.all_to_all(sent, every, split_axis=0, concat_axis=0, tiled=True)  20.5 us
    all_to_all x2, starting transfers between devices, return_rows(): got = lax.all_to_all(sent, every, split_axis=0, concat_axis=0, tiled=True)  17.1 us
  transfers between devices with their start and end apart: 85, of which 36 were waited for; matrix products, arithmetic and copies ran while one was open for 18% of the time, Pallas kernels for 6%

profile of v2, /device:TPU:1, one launch (start us, length us, event | category | flops | bytes accessed | tf_op | source)
XLA Modules:
  0.0 812.8 jit_solution(9690856440722182811)
XLA Ops:
  66.9 22.3 %collective-permute-done.9.refs_1_ = bf16[32,4416]{1,0:T(8,128)(2,1)S(1)} collective-permute-done((bf16[32,4416]{1,0:T(8,128)(2,1)S(1)}, bf16[32,4416]{1,0:T(8,128)(2,1)S(1)}, u32[]{:S(2)}, u32[]{:S(2)}) %collective-permute-start.9) | collective-permute-done | bytes 282656 | tf_op jit(solution)/shard_map/ppermute | solution.py:31
  89.2 7.1 collective-permute-done.10.refs_2_
  120.1 13.9 %collective-permute-done.18 = bf16[4,32,4416]{2,1,0:T(8,128)(2,1)} collective-permute-done((bf16[4,32,4416]{2,1,0:T(8,128)(2,1)S(1)}, bf16[4,32,4416]{2,1,0:T(8,128)(2,1)}, u32[]{:S(2)}, u32[]{:S(2)}) %collective-permute-start.18) | collective-permute-done | bytes 1130528 | tf_op jit(solution)/shard_map/ppermute | solution.py:31
  145.4 17.6 %collective-permute-done.23 = bf16[4,32,4416]{2,1,0:T(8,128)(2,1)S(1)} collective-permute-done((bf16[4,32,4416]{2,1,0:T(8,128)(2,1)S(1)}, bf16[4,32,4416]{2,1,0:T(8,128)(2,1)S(1)}, u32[]{:S(2)}, u32[]{:S(2)}) %collective-permute-start.23) | collective-permute-done | bytes 1130528 | tf_op jit(solution)/shard_map/ppermute | solution.py:31
  171.9 12.3 %collective-permute-done.26 = bf16[4,32,4416]{2,1,0:T(8,128)(2,1)S(1)} collective-permute-done((bf16[4,32,4416]{2,1,0:T(8,128)(2,1)}, bf16[4,32,4416]{2,1,0:T(8,128)(2,1)S(1)}, u32[]{:S(2)}, u32[]{:S(2)}) %collective-permute-start.26) | collective-permute-done | bytes 1130528 | tf_op jit(solution)/shard_map/ppermute | solution.py:31
  198.3 16.8 %all-to-all-start = ((bf16[64,16,2048]{2,1,0:T(8,128)(2,1)}), bf16[64,16,2048]{2,1,0:T(8,128)(2,1)}, u32[]{:S(2)}, u32[]{:S(2)}) async-start(bf16[64,16,2048]{2,1,0:T(8,128)(2,1)} %bitcast.239), calls=%async_computation | async-start | bytes 8388608 | tf_op jit(solution)/shard_map/all_to_all | solution.py:472
  232.4 7.3 shard_map.301
  245.5 20.8 %all-to-all-done = bf16[64,16,2048]{2,1,0:T(8,128)(2,1)} async-done(((bf16[64,16,2048]{2,1,0:T(8,128)(2,1)}), bf16[64,16,2048]{2,1,0:T(8,128)(2,1)}, u32[]{:S(2)}, u32[]{:S(2)}) %all-to-all-start) | async-done | bytes 4194336 | tf_op jit(solution)/shard_map/all_to_all | solution.py:472
  303.5 10.4 %collective-permute-done.36 = bf16[128,2048]{1,0:T(8,128)(2,1)} collective-permute-done((bf16[128,2048]{1,0:T(8,128)(2,1)}, bf16[128,2048]{1,0:T(8,128)(2,1)}, u32[]{:S(2)}, u32[]{:S(2)}) %collective-permute-start.36) | collective-permute-done | bytes 524320 | tf_op jit(solution)/shard_map/ppermute | solution.py:31
  321.3 9.7 %all-to-all-start.1 = ((bf16[64,16,2048]{2,1,0:T(8,128)(2,1)}), bf16[64,16,2048]{2,1,0:T(8,128)(2,1)}, u32[]{:S(2)}, u32[]{:S(2)}) async-start(bf16[64,16,2048]{2,1,0:T(8,128)(2,1)} %bitcast.240), calls=%async_computation.1 | async-start | bytes 8388608 | tf_op jit(solution)/shard_map/all_to_all | solution.py:472
  331.0 7.8 fusion.13
  357.1 10.1 %shard_map.304 = bf16[8,4,2,32,2112]{4,3,2,1,0:T(8,128)(2,1)} custom-call(s32[4]{0:T(128)} %pad_add_fusion.1.at, bf16[128,2048]{1,0:T(8,128)(2,1)} %copy-done.9, bf16[128,2048]{1,0:T(8,128)(2,1)} %collective-permute-done.38.other, bf16[256,1408]{1,0:T(8,128)(2,1)} %copy-done.16, bf16[128,2048]{1,0:T(8,128)(2,1)} %cot.1, ...), custom_call_target="tpu_custom_call" | custom-call | flops 2200000000 | bytes 11829248 | tf_op jit(solution)/shard_map/pallas_call | solution.py:142
  370.4 11.8 %all-to-all-done.1 = bf16[64,16,2048]{2,1,0:T(8,128)(2,1)} async-done(((bf16[64,16,2048]{2,1,0:T(8,128)(2,1)}), bf16[64,16,2048]{2,1,0:T(8,128)(2,1)}, u32[]{:S(2)}, u32[]{:S(2)}) %all-to-all-start.1) | async-done | bytes 4194336 | tf_op jit(solution)/shard_map/all_to_all | solution.py:472
  411.7 9.8 %all-to-all-start.2 = ((bf16[64,16,2048]{2,1,0:T(8,128)(2,1)}), bf16[64,16,2048]{2,1,0:T(8,128)(2,1)}, u32[]{:S(2)}, u32[]{:S(2)}) async-start(bf16[64,16,2048]{2,1,0:T(8,128)(2,1)} %bitcast.241), calls=%async_computation.2 | async-start | bytes 8388608 | tf_op jit(solution)/shard_map/all_to_all | solution.py:477
  430.7 7.2 convolution_bitcast_fusion.2
  437.9 7.2 convolution_bitcast_fusion.1
  445.1 7.1 convolution_bitcast_fusion
  452.2 20.5 %all-to-all-done.2 = bf16[64,16,2048]{2,1,0:T(8,128)(2,1)} async-done(((bf16[64,16,2048]{2,1,0:T(8,128)(2,1)}), bf16[64,16,2048]{2,1,0:T(8,128)(2,1)}, u32[]{:S(2)}, u32[]{:S(2)}) %all-to-all-start.2) | async-done | bytes 4194336 | tf_op jit(solution)/shard_map/all_to_all | solution.py:477
  479.4 11.4 %collective-permute-done.41 = bf16[128,2048]{1,0:T(8,128)(2,1)S(1)} collective-permute-done((bf16[128,2048]{1,0:T(8,128)(2,1)S(1)}, bf16[128,2048]{1,0:T(8,128)(2,1)S(1)}, u32[]{:S(2)}, u32[]{:S(2)}) %collective-permute-start.41) | collective-permute-done | bytes 524320 | tf_op jit(solution)/shard_map/ppermute | solution.py:31
  507.4 6.9 shard_map.306
  520.6 8.2 %collective-permute-done.47.b1 = bf16[128,1024]{1,0:T(8,128)(2,1)} collective-permute-done((bf16[128,1024]{1,0:T(8,128)(2,1)}, bf16[128,1024]{1,0:T(8,128)(2,1)}, u32[]{:S(2)}, u32[]{:S(2)}) %collective-permute-start.47) | collective-permute-done | bytes 262176 | tf_op jit(solution)/shard_map/ppermute | solution.py:31
  528.8 10.1 %collective-permute-done.48.b2 = bf16[128,1024]{1,0:T(8,128)(2,1)} collective-permute-done((bf16[128,1024]{1,0:T(8,128)(2,1)}, bf16[128,1024]{1,0:T(8,128)(2,1)}, u32[]{:S(2)}, u32[]{:S(2)}) %collective-permute-start.48) | collective-permute-done | bytes 262176 | tf_op jit(solution)/shard_map/ppermute | solution.py:31
  538.9 8.4 %shard_map.307 = (bf16[256,1408]{1,0:T(8,128)(2,1)}, bf16[256,1024]{1,0:T(8,128)(2,1)}, f32[128,2048]{1,0:T(8,128)}, bf16[128,2048]{1,0:T(8,128)(2,1)}) custom-call(s32[4]{0:T(128)} %pad_add_fusion.1.at, bf16[128,1024]{1,0:T(8,128)(2,1)} %get-tuple-element.103.b0, bf16[128,1024]{1,0:T(8,128)(2,1)} %collective-permute-done.47.b1, ...), custom_call_target="tpu_custom_call" | custom-call | flops 1800000000 | bytes 11599872 | tf_op jit(solution)/shard_map/pallas_call | solution.py:142
  553.2 9.3 %shard_map.308 = (bf16[4,32,2304]{2,1,0:T(8,128)(2,1)}, bf16[4,32,2304]{2,1,0:T(8,128)(2,1)}, bf16[4,32,2304]{2,1,0:T(8,128)(2,1)}, bf16[4,32,2304]{2,1,0:T(8,12...) custom-call(s32[4]{0:T(128)} %pad_add_fusion.1.at, ...), custom_call_target="tpu_custom_call" | custom-call | flops 2200000000 | bytes 14090240 | tf_op jit(solution)/shard_map/pallas_call | solution.py:142
  565.8 7.2 all-to-all-start.3
  578.4 49.1 %collective-permute-done.59 = bf16[4,32,2304]{2,1,0:T(8,128)(2,1)} collective-permute-done((bf16[4,32,2304]{2,1,0:T(8,128)(2,1)}, bf16[4,32,2304]{2,1,0:T(8,128)(2,1)}, u32[]{:S(2)}, u32[]{:S(2)}) %collective-permute-start.59) | collective-permute-done | bytes 589856 | tf_op jit(solution)/shard_map/ppermute | solution.py:31
  629.6 26.3 %collective-permute-done.73 = bf16[4,32,2304]{2,1,0:T(8,128)(2,1)S(1)} collective-permute-done((bf16[4,32,2304]{2,1,0:T(8,128)(2,1)}, bf16[4,32,2304]{2,1,0:T(8,128)(2,1)S(1)}, u32[]{:S(2)}, u32[]{:S(2)}) %collective-permute-start.73) | collective-permute-done | bytes 589856 | tf_op jit(solution)/shard_map/ppermute | solution.py:31
  657.6 24.8 %collective-permute-done.53 = bf16[4,32,2304]{2,1,0:T(8,128)(2,1)S(1)} collective-permute-done((bf16[4,32,2304]{2,1,0:T(8,128)(2,1)S(1)}, bf16[4,32,2304]{2,1,0:T(8,128)(2,1)S(1)}, u32[]{:S(2)}, u32[]{:S(2)}) %collective-permute-start.53) | collective-permute-done | bytes 589856 | tf_op jit(solution)/shard_map/ppermute | solution.py:31
  683.7 7.2 collective-permute-start.74
  690.8 16.5 %collective-permute-done.60 = bf16[4,32,2304]{2,1,0:T(8,128)(2,1)S(1)} collective-permute-done((bf16[4,32,2304]{2,1,0:T(8,128)(2,1)S(1)}, bf16[4,32,2304]{2,1,0:T(8,128)(2,1)S(1)}, u32[]{:S(2)}, u32[]{:S(2)}) %collective-permute-start.60) | collective-permute-done | bytes 589856 | tf_op jit(solution)/shard_map/ppermute | solution.py:31
  747.8 8.0 collective-permute-start.78
  778.0 8.7 %collective-permute-done.43 = bf16[128,2048]{1,0:T(8,128)(2,1)} collective-permute-done((bf16[128,2048]{1,0:T(8,128)(2,1)S(1)}, bf16[128,2048]{1,0:T(8,128)(2,1)}, u32[]{:S(2)}, u32[]{:S(2)}) %collective-permute-start.43) | collective-permute-done | bytes 524320 | tf_op jit(solution)/shard_map/ppermute | solution.py:31
  (506 shorter events, 375.2 us)
Async XLA Ops:
  36.6 29.6 %collective-permute-start.12 = (bf16[32,4416]{1,0:T(8,128)(2,1)}, bf16[32,4416]{1,0:T(8,128)(2,1)}, u32[]{:S(2)}, u32[]{:S(2)}) collective-permute-start(bf16[32,4416]{1,0:T(8,128)(2,1)} %get-tuple-element.168), channel_id=1, source_target_pairs={{0,24},{8,16},{16,8},{24,0},{1,25},{9,17},{17,9},{25,1},{2,26},{10... | collective-permute-start | bytes 847880 | tf_op jit(solution)/shard_map/ppermute | solution.py:35
  55.2 58.8 %collective-permute-start.16 = (bf16[4,32,4416]{2,1,0:T(8,128)(2,1)S(1)}, bf16[4,32,4416]{2,1,0:T(8,128)(2,1)S(1)}, u32[]{:S(2)}, u32[]{:S(2)}) collective-permute-start(bf16[4,32,4416]{2,1,0:T(8,128)(2,1)S(1)} %copy-done.10), channel_id=1, source_target_pairs={{0,2},{2,4},{4,6},{6,0},{1,3},{3,5},{5,7},{7,1},{8,10},{10,12},{12... | collective-permute-start | bytes 3391496 | tf_op jit(solution)/shard_map/ppermute | solution.py:31
  56.6 32.5 %collective-permute-start.9 = (bf16[32,4416]{1,0:T(8,128)(2,1)S(1)}, bf16[32,4416]{1,0:T(8,128)(2,1)S(1)}, u32[]{:S(2)}, u32[]{:S(2)}) collective-permute-start(bf16[32,4416]{1,0:T(8,128)(2,1)S(1)} %collective-permute-done.8.refs_0_), channel_id=1, source_target_pairs={{0,2},{2,4},{4,6},{6,0},{1,3},{3,5},{5,7},{7,1},{8,10},{10,12},{12... | collective-permute-start | bytes 847880 | tf_op jit(solution)/shard_map/ppermute | solution.py:31
  58.0 38.3 %collective-permute-start.10 = (bf16[32,4416]{1,0:T(8,128)(2,1)S(1)}, bf16[32,4416]{1,0:T(8,128)(2,1)S(1)}, u32[]{:S(2)}, u32[]{:S(2)}) collective-permute-start(bf16[32,4416]{1,0:T(8,128)(2,1)S(1)} %collective-permute-done.8.refs_0_), channel_id=1, source_target_pairs={{0,4},{2,6},{4,0},{6,2},{1,5},{3,7},{5,1},{7,3},{8,12},{10,14},{12... | collective-permute-start | bytes 847880 | tf_op jit(solution)/shard_map/ppermute | solution.py:31
  59.4 37.0 %collective-permute-start.11 = (bf16[32,4416]{1,0:T(8,128)(2,1)S(1)}, bf16[32,4416]{1,0:T(8,128)(2,1)S(1)}, u32[]{:S(2)}, u32[]{:S(2)}) collective-permute-start(bf16[32,4416]{1,0:T(8,128)(2,1)S(1)} %collective-permute-done.8.refs_0_), channel_id=1, source_target_pairs={{0,6},{2,0},{4,2},{6,4},{1,7},{3,1},{5,3},{7,5},{8,14},{10,8},{12,... | collective-permute-start | bytes 847880 | tf_op jit(solution)/shard_map/ppermute | solution.py:31
  66.2 51.5 %collective-permute-start.17 = (bf16[4,32,4416]{2,1,0:T(8,128)(2,1)S(1)}, bf16[4,32,4416]{2,1,0:T(8,128)(2,1)}, u32[]{:S(2)}, u32[]{:S(2)}) collective-permute-start(bf16[4,32,4416]{2,1,0:T(8,128)(2,1)S(1)} %copy-done.10), channel_id=1, source_target_pairs={{0,6},{2,0},{4,2},{6,4},{1,7},{3,1},{5,3},{7,5},{8,14},{10,8},{12,... | collective-permute-start | bytes 3391496 | tf_op jit(solution)/shard_map/ppermute | solution.py:31
  104.7 29.3 %collective-permute-start.18 = (bf16[4,32,4416]{2,1,0:T(8,128)(2,1)S(1)}, bf16[4,32,4416]{2,1,0:T(8,128)(2,1)}, u32[]{:S(2)}, u32[]{:S(2)}) collective-permute-start(bf16[4,32,4416]{2,1,0:T(8,128)(2,1)S(1)} %copy-done.11), channel_id=1, source_target_pairs={{0,2},{2,4},{4,6},{6,0},{1,3},{3,5},{5,7},{7,1},{8,10},{10,12},{12... | collective-permute-start | bytes 3391496 | tf_op jit(solution)/shard_map/ppermute | solution.py:31
  109.2 29.8 %collective-permute-start.20 = (bf16[4,32,4416]{2,1,0:T(8,128)(2,1)}, bf16[4,32,4416]{2,1,0:T(8,128)(2,1)}, u32[]{:S(2)}, u32[]{:S(2)}) collective-permute-start(bf16[4,32,4416]{2,1,0:T(8,128)(2,1)} %shard_map.299), channel_id=1, source_target_pairs={{0,32},{32,64},{64,96},{96,0},{1,33},{33,65},{65,97},{97,1},{2,34}... | collective-permute-start | bytes 3391496 | tf_op jit(solution)/shard_map/ppermute | solution.py:31
  114.0 30.0 %collective-permute-start.21 = (bf16[4,32,4416]{2,1,0:T(8,128)(2,1)S(1)}, bf16[4,32,4416]{2,1,0:T(8,128)(2,1)S(1)}, u32[]{:S(2)}, u32[]{:S(2)}) collective-permute-start(bf16[4,32,4416]{2,1,0:T(8,128)(2,1)S(1)} %copy-done.12), channel_id=1, source_target_pairs={{0,96},{32,0},{64,32},{96,64},{1,97},{33,1},{65,33},{97,65},{2,98}... | collective-permute-start | bytes 3391496 | tf_op jit(solution)/shard_map/ppermute | solution.py:31
  117.8 49.7 %collective-permute-start.22 = (bf16[4,32,4416]{2,1,0:T(8,128)(2,1)S(1)}, bf16[4,32,4416]{2,1,0:T(8,128)(2,1)S(1)}, u32[]{:S(2)}, u32[]{:S(2)}) collective-permute-start(bf16[4,32,4416]{2,1,0:T(8,128)(2,1)S(1)} %copy-done.13), channel_id=1, source_target_pairs={{0,32},{32,64},{64,96},{96,0},{1,33},{33,65},{65,97},{97,1},{2,34}... | collective-permute-start | bytes 3391496 | tf_op jit(solution)/shard_map/ppermute | solution.py:31
  134.0 29.0 %collective-permute-start.23 = (bf16[4,32,4416]{2,1,0:T(8,128)(2,1)S(1)}, bf16[4,32,4416]{2,1,0:T(8,128)(2,1)S(1)}, u32[]{:S(2)}, u32[]{:S(2)}) collective-permute-start(bf16[4,32,4416]{2,1,0:T(8,128)(2,1)S(1)} %copy-done.13), channel_id=1, source_target_pairs={{0,96},{32,0},{64,32},{96,64},{1,97},{33,1},{65,33},{97,65},{2,98}... | collective-permute-start | bytes 3391496 | tf_op jit(solution)/shard_map/ppermute | solution.py:31
  136.3 33.3 %collective-permute-start.24 = (bf16[4,32,4416]{2,1,0:T(8,128)(2,1)S(1)}, bf16[4,32,4416]{2,1,0:T(8,128)(2,1)S(1)}, u32[]{:S(2)}, u32[]{:S(2)}) collective-permute-start(bf16[4,32,4416]{2,1,0:T(8,128)(2,1)S(1)} %collective-permute-done.16), channel_id=1, source_target_pairs={{0,2},{2,4},{4,6},{6,0},{1,3},{3,5},{5,7},{7,1},{8,10},{10,12},{12... | collective-permute-start | bytes 3391496 | tf_op jit(solution)/shard_map/ppermute | solution.py:31
  139.0 31.8 %collective-permute-start.25 = (bf16[4,32,4416]{2,1,0:T(8,128)(2,1)}, bf16[4,32,4416]{2,1,0:T(8,128)(2,1)S(1)}, u32[]{:S(2)}, u32[]{:S(2)}) collective-permute-start(bf16[4,32,4416]{2,1,0:T(8,128)(2,1)} %collective-permute-done.19), channel_id=1, source_target_pairs={{0,6},{2,0},{4,2},{6,4},{1,7},{3,1},{5,3},{7,5},{8,14},{10,8},{12,... | collective-permute-start | bytes 3391496 | tf_op jit(solution)/shard_map/ppermute | solution.py:31
  143.9 40.2 %collective-permute-start.26 = (bf16[4,32,4416]{2,1,0:T(8,128)(2,1)}, bf16[4,32,4416]{2,1,0:T(8,128)(2,1)S(1)}, u32[]{:S(2)}, u32[]{:S(2)}) collective-permute-start(bf16[4,32,4416]{2,1,0:T(8,128)(2,1)} %collective-permute-done.20), channel_id=1, source_target_pairs={{0,32},{32,64},{64,96},{96,0},{1,33},{33,65},{65,97},{97,1},{2,34}... | collective-permute-start | bytes 3391496 | tf_op jit(solution)/shard_map/ppermute | solution.py:31
  198.3 68.0 %all-to-all-start = ((bf16[64,16,2048]{2,1,0:T(8,128)(2,1)}), bf16[64,16,2048]{2,1,0:T(8,128)(2,1)}, u32[]{:S(2)}, u32[]{:S(2)}) async-start(bf16[64,16,2048]{2,1,0:T(8,128)(2,1)} %bitcast.239), calls=%async_computation | async-start | bytes 8388608 | tf_op jit(solution)/shard_map/all_to_all | solution.py:472
  239.7 30.7 %collective-permute-start.29 = (bf16[128,1024]{1,0:T(8,128)(2,1)}, bf16[128,1024]{1,0:T(8,128)(2,1)S(1)}, u32[]{:S(2)}, u32[]{:S(2)}) collective-permute-start(bf16[128,1024]{1,0:T(8,128)(2,1)} %get-tuple-element.80), channel_id=1, source_target_pairs={{0,2},{2,4},{4,6},{6,0},{1,3},{3,5},{5,7},{7,1},{8,10},{10,12},{12... | collective-permute-start | bytes 786440 | tf_op jit(solution)/shard_map/ppermute | solution.py:31
  241.0 34.1 %collective-permute-start.30 = (bf16[128,1024]{1,0:T(8,128)(2,1)}, bf16[128,1024]{1,0:T(8,128)(2,1)S(1)}, u32[]{:S(2)}, u32[]{:S(2)}) collective-permute-start(bf16[128,1024]{1,0:T(8,128)(2,1)} %get-tuple-element.81), channel_id=1, source_target_pairs={{0,4},{2,6},{4,0},{6,2},{1,5},{3,7},{5,1},{7,3},{8,12},{10,14},{12... | collective-permute-start | bytes 786440 | tf_op jit(solution)/shard_map/ppermute | solution.py:31
  243.4 32.0 %collective-permute-start.31 = (bf16[128,1024]{1,0:T(8,128)(2,1)}, bf16[128,1024]{1,0:T(8,128)(2,1)}, u32[]{:S(2)}, u32[]{:S(2)}) collective-permute-start(bf16[128,1024]{1,0:T(8,128)(2,1)} %get-tuple-element.82), channel_id=1, source_target_pairs={{0,6},{2,0},{4,2},{6,4},{1,7},{3,1},{5,3},{7,5},{8,14},{10,8},{12,... | collective-permute-start | bytes 786440 | tf_op jit(solution)/shard_map/ppermute | solution.py:31
  301.6 41.9 %collective-permute-start.37 = (bf16[128,2048]{1,0:T(8,128)(2,1)}, bf16[128,2048]{1,0:T(8,128)(2,1)}, u32[]{:S(2)}, u32[]{:S(2)}) collective-permute-start(bf16[128,2048]{1,0:T(8,128)(2,1)} %cot.1), channel_id=1, source_target_pairs={{0,8},{8,0},{1,9},{9,1},{2,10},{10,2},{3,11},{11,3},{4,12},{12,4},... | collective-permute-start | bytes 1572872 | tf_op jit(solution)/shard_map/ppermute | solution.py:31
  321.3 60.8 %all-to-all-start.1 = ((bf16[64,16,2048]{2,1,0:T(8,128)(2,1)}), bf16[64,16,2048]{2,1,0:T(8,128)(2,1)}, u32[]{:S(2)}, u32[]{:S(2)}) async-start(bf16[64,16,2048]{2,1,0:T(8,128)(2,1)} %bitcast.240), calls=%async_computation.1 | async-start | bytes 8388608 | tf_op jit(solution)/shard_map/all_to_all | solution.py:472
  411.7 61.0 %all-to-all-start.2 = ((bf16[64,16,2048]{2,1,0:T(8,128)(2,1)}), bf16[64,16,2048]{2,1,0:T(8,128)(2,1)}, u32[]{:S(2)}, u32[]{:S(2)}) async-start(bf16[64,16,2048]{2,1,0:T(8,128)(2,1)} %bitcast.241), calls=%async_computation.2 | async-start | bytes 8388608 | tf_op jit(solution)/shard_map/all_to_all | solution.py:477
  421.5 369.8 %reduce-scatter.2.cloned.1.call-start = ((), (), s32[]{:S(2)}) async-start(), calls=%async_computation.6 | async-start | bytes 9191424 | tf_op jit(solution)/shard_map/reduce_scatter | solution.py:579
  547.4 29.8 %collective-permute-start.50 = (bf16[128,2048]{1,0:T(8,128)(2,1)}, bf16[128,2048]{1,0:T(8,128)(2,1)}, u32[]{:S(2)}, u32[]{:S(2)}) collective-permute-start(bf16[128,2048]{1,0:T(8,128)(2,1)} %get-tuple-element.110), channel_id=1, source_target_pairs={{0,8},{8,0},{1,9},{9,1},{2,10},{10,2},{3,11},{11,3},{4,12},{12,4},... | collective-permute-start | bytes 1572872 | tf_op jit(solution)/shard_map/ppermute | solution.py:31
  562.4 65.0 %collective-permute-start.59 = (bf16[4,32,2304]{2,1,0:T(8,128)(2,1)}, bf16[4,32,2304]{2,1,0:T(8,128)(2,1)}, u32[]{:S(2)}, u32[]{:S(2)}) collective-permute-start(bf16[4,32,2304]{2,1,0:T(8,128)(2,1)} %get-tuple-element.124), channel_id=1, source_target_pairs={{0,6},{2,0},{4,2},{6,4},{1,7},{3,1},{5,3},{7,5},{8,14},{10,8},{12,... | collective-permute-start | bytes 1769480 | tf_op jit(solution)/shard_map/ppermute | solution.py:31
  565.8 202.5 %all-to-all-start.3 = ((bf16[64,16,2048]{2,1,0:T(8,128)(2,1)}), bf16[64,16,2048]{2,1,0:T(8,128)(2,1)}, u32[]{:S(2)}, u32[]{:S(2)}) async-start(bf16[64,16,2048]{2,1,0:T(8,128)(2,1)} %bitcast.242), calls=%async_computation.3 | async-start | bytes 8388608 | tf_op jit(solution)/shard_map/all_to_all | solution.py:477
  573.1 110.6 %collective-permute-start.58 = (bf16[4,32,2304]{2,1,0:T(8,128)(2,1)}, bf16[4,32,2304]{2,1,0:T(8,128)(2,1)S(1)}, u32[]{:S(2)}, u32[]{:S(2)}) collective-permute-start(bf16[4,32,2304]{2,1,0:T(8,128)(2,1)} %get-tuple-element.122), channel_id=1, source_target_pairs={{0,2},{2,4},{4,6},{6,0},{1,3},{3,5},{5,7},{7,1},{8,10},{10,12},{12... | collective-permute-start | bytes 1769480 | tf_op jit(solution)/shard_map/ppermute | solution.py:31
  574.5 81.4 %collective-permute-start.73 = (bf16[4,32,2304]{2,1,0:T(8,128)(2,1)}, bf16[4,32,2304]{2,1,0:T(8,128)(2,1)S(1)}, u32[]{:S(2)}, u32[]{:S(2)}) collective-permute-start(bf16[4,32,2304]{2,1,0:T(8,128)(2,1)} %get-tuple-element.132), channel_id=1, source_target_pairs={{0,96},{32,0},{64,32},{96,64},{1,97},{33,1},{65,33},{97,65},{2,98}... | collective-permute-start | bytes 1769480 | tf_op jit(solution)/shard_map/ppermute | solution.py:31
  577.2 131.8 %collective-permute-start.72 = (bf16[4,32,2304]{2,1,0:T(8,128)(2,1)}, bf16[4,32,2304]{2,1,0:T(8,128)(2,1)S(1)}, u32[]{:S(2)}, u32[]{:S(2)}) collective-permute-start(bf16[4,32,2304]{2,1,0:T(8,128)(2,1)} %get-tuple-element.130), channel_id=1, source_target_pairs={{0,32},{32,64},{64,96},{96,0},{1,33},{33,65},{65,97},{97,1},{2,34}... | collective-permute-start | bytes 1769480 | tf_op jit(solution)/shard_map/ppermute | solution.py:31
  577.2 78.9 %collective-permute-start.66 = (bf16[4,32,2304]{2,1,0:T(8,128)(2,1)}, bf16[4,32,2304]{2,1,0:T(8,128)(2,1)S(1)}, u32[]{:S(2)}, u32[]{:S(2)}) collective-permute-start(bf16[4,32,2304]{2,1,0:T(8,128)(2,1)} %get-tuple-element.128), channel_id=1, source_target_pairs={{0,32},{32,64},{64,96},{96,0},{1,33},{33,65},{65,97},{97,1},{2,34}... | collective-permute-start | bytes 1769480 | tf_op jit(solution)/shard_map/ppermute | solution.py:31
  627.5 90.3 %collective-permute-start.65 = (bf16[4,32,2304]{2,1,0:T(8,128)(2,1)}, bf16[4,32,2304]{2,1,0:T(8,128)(2,1)S(1)}, u32[]{:S(2)}, u32[]{:S(2)}) collective-permute-start(bf16[4,32,2304]{2,1,0:T(8,128)(2,1)} %get-tuple-element.126), channel_id=1, source_target_pairs={{0,96},{32,0},{64,32},{96,64},{1,97},{33,1},{65,33},{97,65},{2,98}... | collective-permute-start | bytes 1769480 | tf_op jit(solution)/shard_map/ppermute | solution.py:31
  682.6 45.9 %collective-permute-start.52 = (bf16[4,32,2304]{2,1,0:T(8,128)(2,1)S(1)}, bf16[4,32,2304]{2,1,0:T(8,128)(2,1)S(1)}, u32[]{:S(2)}, u32[]{:S(2)}) collective-permute-start(bf16[4,32,2304]{2,1,0:T(8,128)(2,1)S(1)} %copy-done.76), channel_id=1, source_target_pairs={{0,6},{2,0},{4,2},{6,4},{1,7},{3,1},{5,3},{7,5},{8,14},{10,8},{12,... | collective-permute-start | bytes 1769480 | tf_op jit(solution)/shard_map/ppermute | solution.py:31
  683.7 30.4 %collective-permute-start.74 = (bf16[4,32,2304]{2,1,0:T(8,128)(2,1)S(1)}, bf16[4,32,2304]{2,1,0:T(8,128)(2,1)S(1)}, u32[]{:S(2)}, u32[]{:S(2)}) collective-permute-start(bf16[4,32,2304]{2,1,0:T(8,128)(2,1)S(1)} %add_convert_fusion.2), channel_id=1, source_target_pairs={{0,96},{32,0},{64,32},{96,64},{1,97},{33,1},{65,33},{97,65},{2,98}... | collective-permute-start | bytes 1769480 | tf_op jit(solution)/shard_map/ppermute | solution.py:31
  (136 other events, 2677.6 us)
Sparse Core Ops, SparseCore 0:
  505.2 217.2 reduce-scatter.1

commit v3 on v2

--- a/solution.py
+++ b/solution.py
@@ -43,40 +43,115 @@
     return jnp.stack([jnp.where(index == 0, own, other), jnp.where(index == 0, other, own)])
 
 
-def gather_rows(halves, at):
-    x, z, core, y = (lax.axis_index(name) for name in ("x", "z", "c", "y"))
-    lanes = halves.shape[-1]
-    keep, send = pick(halves, core), pick(halves, 1 - core)
+def pack_kernel(
+    at, query, down, up, out, gate, upper, lower, router, attn_gain, latent_gain, ffn_gain, *refs
+):
+    keep, send, *quarters, packs, shared_packs = refs
+    scale = attn_gain[...].astype(F32)
+    lat_scale = latent_gain[...].astype(F32)
+    heads = query[...].astype(F32) * scale
+    lows = down[...].astype(F32) * scale
+    rotated = lows[:, 512:]
+    ups = up[...].astype(F32) * lat_scale
+    outs, gates, uppers, lowers = (ref[...].astype(F32) for ref in (out, gate, upper, lower))
+    for half in range(2):
+        first = half * 4 * HEAD
+        plain = [heads[:, first + i * HEAD : first + i * HEAD + NOPE] for i in range(4)]
+        turned = []
+        for pair in range(2):
+            for side in range(2):
+                for i in (2 * pair, 2 * pair + 1):
+                    start = first + i * HEAD + NOPE + 32 * side
+                    turned.append(heads[:, start : start + 32])
+        blocks = plain + [jnp.concatenate(turned, axis=1), lows[:, :512]]
+        blocks.append(
+            jnp.concatenate([rotated[:, :32], rotated[:, :32], rotated[:, 32:], rotated[:, 32:]], axis=1)
+        )
+        blocks.append(outs[:, half * 512 : half * 512 + 512])
+        start = half * 1024
+        blocks.append(
+            jnp.concatenate([ups[:, start + j * 256 : start + j * 256 + 256] for j in range(4)], axis=0)
+        )
+        gain = jnp.broadcast_to(ffn_gain[...].astype(F32), (32, 64))
+        blocks.append(jnp.concatenate([router[...].astype(F32), gain], axis=1))
+        for side in range(2):
+            index = half * 2 + side
+            span = slice(index * 352, index * 352 + 352)
+            parts = [gates[:, span], uppers[:, span], jnp.zeros((32, 64), F32)]
+            parts += [lowers[:, span], jnp.zeros((32, 32), F32)]
+            shared_packs[index] = jnp.concatenate(parts, axis=1).astype(BF16)
+        at_lane = 0
+        for block in blocks:
+            size = block.shape[1]
+            packs[half, :, at_lane : at_lane + size] = block.astype(BF16)
+            at_lane += size
+    keep[...] = packs[at[2]]
+    send[...] = packs[1 - at[2]]
+    core, side = at[2], at[1]
+    places = (core * 2 + side, (1 - core) * 2 + side, core * 2 + 1 - side, (1 - core) * 2 + 1 - side)
+    for ref, place in zip(quarters, places, strict=True):
+        ref[...] = shared_packs[place]
+
+
+LANES = 2304
+QUARTER = 1152
+DOWN = 768
+
+
+def quad_exchange(parts):
+    z, core = lax.axis_index("z"), lax.axis_index("c")
+    stay, across, beside, corner = parts
+    across, beside, corner = shift(across, "c", 1), shift(beside, "z", 1), diagonal(corner)
+    return in_order(in_order(stay, across, core), in_order(beside, corner, core), z)
+
+
+def quad_blocks(own):
+    beside = shift(own, "z", 1)
+    return [own, shift(own, "c", 1), beside, shift(beside, "c", 1)]
+
+
+def quad_sum(own, across, beside, corner):
+    own = own + shift(across, "c", 1).astype(F32)
+    beside = beside + shift(corner, "c", 1).astype(F32)
+    return own + shift(beside.astype(BF16), "z", 1).astype(F32)
+
+
+def gather_rows(keep, send, at):
     across, beside, corner = shift(send, "c", 1), shift(keep, "z", 1), diagonal(send)
-    final = jnp.zeros((4, 2, 2, 4, 32, lanes), halves.dtype)
-
-    def put_one(buffer, piece, level, place):
-        start = (0, level, core, place % 4, 0, 0)
-        return lax.dynamic_update_slice(buffer, piece.reshape(4, 1, 1, 1, 32, lanes), start)
-
-    def put_two(buffer, piece, level, place):
-        start = (place % 4, level, 1 - core, 0, 0, 0)
-        return lax.dynamic_update_slice(buffer, piece.reshape(1, 1, 1, 4, 32, lanes), start)
-
     first = [line_up(at, 0, keep, "x"), line_up(at, 0, beside, "x")]
     second = [line_up(at, 3, across, "y"), line_up(at, 3, corner, "y")]
-    levels = (z, 1 - z)
-    for put, lines, axis, place in ((put_one, first, "y", y), (put_two, second, "x", x)):
-        for line, level in zip(lines, levels, strict=True):
-            final = put(final, line, level, place)
-    near = {}
-    for name, lines, axis in (("one", first, "y"), ("two", second, "x")):
-        near[name] = [(shift(line, axis, 1), shift(line, axis, -1)) for line in lines]
-    far = {}
-    for name, axis in (("one", "y"), ("two", "x")):
-        far[name] = (shift(near[name][0][0], axis, 1), shift(near[name][1][1], axis, -1))
-    for name, put, place in (("one", put_one, y), ("two", put_two, x)):
-        for (left, right), level in zip(near[name], levels, strict=True):
-            final = put(put(final, left, level, place + 3), right, level, place + 1)
-    for name, put, place in (("one", put_one, y), ("two", put_two, x)):
-        for piece, level in zip(far[name], levels, strict=True):
-            final = put(final, piece, level, place + 2)
-    return final.reshape(-1, lanes)
+    near = [
+        [(shift(line, axis, 1), shift(line, axis, -1)) for line in lines]
+        for lines, axis in ((first, "y"), (second, "x"))
+    ]
+    far = [
+        (shift(pair[0][0], axis, 1), shift(pair[1][1], axis, -1))
+        for pair, axis in zip(near, ("y", "x"), strict=True)
+    ]
+    pieces = []
+    for lines, pair, last in zip((first, second), near, far, strict=True):
+        for level in range(2):
+            pieces += [lines[level], pair[level][0], pair[level][1], last[level]]
+    return pieces
+
+
+PLACES = (0, 3, 1, 2)
+
+
+def fetch(at, pieces, lane, target, sems):
+    size = target.shape[-1]
+    copies = []
+    for index, piece in enumerate(pieces):
+        level = at[1] if index % 8 < 4 else 1 - at[1]
+        step = PLACES[index % 4]
+        if index < 8:
+            place = target.at[:, level, at[2], lax.rem(at[3] + step, 4)]
+        else:
+            place = target.at[lax.rem(at[0] + step, 4), level, 1 - at[2]]
+        copies.append(pltpu.make_async_copy(piece.at[:, :, pl.ds(lane, size)], place, sems.at[index]))
+    for copy in copies:
+        copy.start()
+    return copies
 
 
 def line_kernel(index, at, *refs):
@@ -91,33 +166,59 @@
     )
 
 
-def ring_sum(parts, axis):
+def add_low(*values):
+    return sum(value.astype(F32) for value in values).astype(BF16)
+
+
+def ring_kernel(index, at, a0, a1, a2, b0, b1, b2, o0, o1, o2, o3, low, high):
+    low[...] = (a0[...].astype(F32) + a1[...].astype(F32) + a2[...].astype(F32)).astype(BF16)
+    high[...] = (b0[...].astype(F32) + b1[...].astype(F32) + b2[...].astype(F32)).astype(BF16)
+    for step, out in enumerate((o0, o1, o2, o3)):
+        place = lax.rem(at[index] + step, 4)
+        out[0] = low[place]
+        out[1] = high[place]
+
+
+def ring_sum(parts, axis, at, index):
     low = shift(parts[2][0], axis, 1)
     high = shift(parts[2][1], axis, -1)
     right_high = shift(parts[1][1], axis, 1)
     left_low = shift(parts[3][0], axis, -1)
     right_low = shift(add_low(parts[1][0], low), axis, 1)
     left_high = shift(add_low(parts[3][1], high), axis, -1)
-    return [add_low(parts[0][0], left_low, right_low), add_low(parts[0][1], right_high, left_high)]
-
-
-def add_low(*values):
-    return sum(value.astype(F32) for value in values).astype(BF16)
-
-
-def direct_sum(line, axis):
-    me = lax.axis_index(axis)
-    got = [shift(pick(line, (me + step) % 4), axis, step) for step in (1, 2, 3)]
-    return add_low(pick(line, me), *got)
-
-
-def scatter_rows(one, two):
-    one = [direct_sum(line, "x") for line in ring_sum(one, "y")]
-    two = [direct_sum(line, "y") for line in ring_sum(two, "x")]
-    beside, across, corner = shift(one[1], "z", 1), shift(two[0], "c", 1), diagonal(two[1])
-    own = one[0].astype(F32) + beside.astype(F32)
-    other = across.astype(F32) + corner.astype(F32)
-    return in_order(own, other, lax.axis_index("c"))
+    shape = parts[0][0].shape
+    return call(
+        functools.partial(ring_kernel, index),
+        [(2,) + shape[1:]] * 4,
+        [BF16] * 4,
+        at,
+        parts[0][0],
+        left_low,
+        right_low,
+        parts[0][1],
+        right_high,
+        left_high,
+        scratch=[pltpu.VMEM(shape, BF16)] * 2,
+        many=True,
+    )
+
+
+def sum_kernel(at, p0, p1, p2, p3, low, high):
+    for level, out in enumerate((low, high)):
+        total = p0[level].astype(F32) + p1[level].astype(F32)
+        out[...] = (total + p2[level].astype(F32) + p3[level].astype(F32)).astype(BF16)
+
+
+def direct_sum(pieces, axis, at):
+    got = [pieces[0]] + [shift(pieces[step], axis, step) for step in (1, 2, 3)]
+    shape = pieces[0].shape[1:]
+    return call(sum_kernel, [shape] * 2, [BF16] * 2, at, *got, many=True)
+
+
+def scatter_rows(one, two, at):
+    one, two = ring_sum(one, "y", at, 0), ring_sum(two, "x", at, 3)
+    one, two = direct_sum(one, "x", at), direct_sum(two, "y", at)
+    return one[0], shift(one[1], "z", 1), shift(two[0], "c", 1), diagonal(two[1])
 
 
 def to_ring(pieces):
@@ -133,7 +234,7 @@
     return own + shift(other, "c", 1).astype(F32)
 
 
-def call(kernel, shapes, dtypes, at, *operands, scratch=(), flops=1_000_000, many=False):
+def call(kernel, shapes, dtypes, at, *operands, scratch=(), flops=1_000_000, many=False, far=0, out_far=False):
     if not many:
         shapes, dtypes = [shapes], [dtypes]
     out_shape = [jax.ShapeDtypeStruct(s, d) for s, d in zip(shapes, dtypes, strict=True)]
@@ -143,8 +244,9 @@
         kernel,
         out_shape=out_shape,
         in_specs=[pl.BlockSpec(memory_space=pltpu.SMEM)]
-        + [pl.BlockSpec(memory_space=pltpu.VMEM)] * len(operands),
-        out_specs=[pl.BlockSpec(memory_space=pltpu.VMEM)] * len(out_shape),
+        + [pl.BlockSpec(memory_space=pl.ANY)] * far
+        + [pl.BlockSpec(memory_space=pltpu.VMEM)] * (len(operands) - far),
+        out_specs=[pl.BlockSpec(memory_space=pl.ANY if out_far else pltpu.VMEM)] * len(out_shape),
         scratch_shapes=scratch,
         compiler_params=pltpu.CompilerParams(vmem_limit_bytes=56 * 1024 * 1024),
         cost_estimate=pl.CostEstimate(flops=flops, bytes_accessed=moved, transcendentals=0),
@@ -182,14 +284,21 @@
     return values * cosine + pltpu.roll(values, 64, 1) * sine
 
 
-def project_kernel(
-    at, own, other, weights, up, cosine, sine, m0, m1, m2, m3, normed, low, plain, inverse, query, keys, key
-):
+def project_kernel(at, *refs):
+    pieces = refs[:16]
+    own, other, cosine, sine, m0, m1, m2, m3, normed, low, plain, inverse = refs[16:28]
+    weights, out_weights, up, tail, query, keys, key, raw, sems = refs[28:]
+    copies = fetch(at, pieces, 0, weights, sems.at[0])
+    later = fetch(at, pieces, 1920, raw, sems.at[1])
+    last = fetch(at, pieces, 1408, out_weights, sems.at[2])
+    last += fetch(at, pieces, 2176, tail, sems.at[3])
     for index, block in enumerate((own, other)):
         values = block[...].astype(F32)
         scale = lax.rsqrt(jnp.mean(values * values, axis=1, keepdims=True) + EPS)
         normed[index * 128 : index * 128 + 128] = (values * scale).astype(BF16)
-    lin = dot(normed[...], weights[...])
+    for copy in copies:
+        copy.wait()
+    lin = dot(normed[...], weights[...].reshape(2048, 1408))
     cos, sin = cosine[...], sine[...]
     query[:, :512] = lin[:, :512].astype(BF16)
     for pair in range(2):
@@ -202,6 +311,12 @@
     plain[...] = latent
     low[...] = latent.astype(BF16)
     inverse[...] = jnp.broadcast_to(scale, inverse.shape)
+    for copy in later:
+        copy.wait()
+    ups = raw[...].astype(F32).reshape(64, 4, 8, 256)
+    for head in range(4):
+        span = slice(head * 256, head * 256 + 256)
+        up[:, span] = ups[:, head].reshape(512, 256).astype(BF16)
     keys[...] = dot(low[...], up[...]).astype(BF16)
     for step, out in enumerate((m0, m1, m2, m3)):
         block, pair = owner(at, ahead(at, step))
@@ -210,6 +325,8 @@
         out[:, QR:KV] = query[rows, lanes_at(pair, 128, 512)]
         out[:, KV:KR] = keys[rows, lanes_at(pair, 512)]
         out[:, KR:] = key[rows, :]
+    for copy in last:
+        copy.wait()
 
 
 def head_lanes(rows, head):
@@ -336,36 +453,125 @@
     other[...] = dot(lin_grad[128:], weights[...], 1, 1).astype(BF16)
 
 
-def grads_kernel(at, normed, lin_grad, own, other, attended, up, tail, *refs):
-    one, two, rows = refs[:8], refs[8:16], refs[16]
+def grads_kernel(at, normed, lin_grad, own, other, attended, low, kv_grad, tail, *refs):
+    one, two, rows, ups = refs[:8], refs[8:16], refs[16], refs[17]
+    for head in range(4):
+        span = slice(head * 256, head * 256 + 256)
+        ups[:, head] = dot(low[...], kv_grad[:, span], 0, 0).reshape(64, 8, 256)
     for step in range(4):
         column = lax.rem(at[0] + step, 4)
         for side in range(2):
             level = at[1] if side == 0 else 1 - at[1]
-            start = pl.multiple_of((column * 2 + level) * 256, 256)
-            span = pl.ds(start, 256)
+            chunk = column * 2 + level
+            span = pl.ds(pl.multiple_of(chunk * 256, 256), 256)
             part = dot(normed[:, span], lin_grad[...], 0, 0).astype(BF16)
             rows[:, :, :1408] = part.reshape(8, 32, 1408)
             part = dot(own[:, span], attended[:128], 0, 0) + dot(other[:, span], attended[128:], 0, 0)
             rows[:, :, 1408:1920] = part.astype(BF16).reshape(8, 32, 512)
-            rows[:, :, 1920:2176] = up[span, :].reshape(8, 32, 256)
+            rows[:, :, 1920:2176] = ups[pl.ds(chunk * 8, 8)].reshape(8, 32, 256).astype(BF16)
             rows[:, :, 2176:] = tail[span, :].reshape(8, 32, 128)
             for place in range(4):
                 one[place * 2 + side][column] = rows[at[2] * 4 + ahead(at, place)]
             two[step * 2 + side][...] = rows[pl.ds((1 - at[2]) * 4, 4)]
 
 
-def shared_grads_kernel(at, own, other, lin_grad, cot, cot_other, act, out):
+def shared_kernel(at, gathered, *refs):
+    ffn_blocks, cot_blocks, outs, backs, grads = refs[:4], refs[4:8], refs[8:12], refs[12:16], refs[16]
+    weights, ffn, cot, lin_grad, act, sems = refs[17:]
+    copies = []
+    for z in range(2):
+        for core in range(2):
+            copies.append(
+                pltpu.make_async_copy(
+                    gathered.at[:, :, z, core], weights.at[:, z, core], sems.at[2 * z + core]
+                )
+            )
+    for copy in copies:
+        copy.start()
+    for i in range(4):
+        ffn[i * 128 : i * 128 + 128] = ffn_blocks[i][...]
+        cot[i * 128 : i * 128 + 128] = cot_blocks[i][...]
+    for copy in copies:
+        copy.wait()
+    gate_up = weights[:, :, :, :, :, :704].reshape(2048, 704)
+    down = weights[:, :, :, :, :, DOWN : DOWN + 352].reshape(2048, 352)
+    lin = dot(ffn[...], gate_up)
+    act_grad = dot(cot[...], down)
+    up_lin = lin[:, 352:]
+    silu, slope = silu_parts(lin[:, :352])
+    act[...] = (silu * up_lin).astype(BF16)
+    both = jnp.concatenate([act_grad * up_lin * slope, act_grad * silu], axis=1)
+    lin_grad[...] = both.astype(BF16)
+    back = dot(lin_grad[...], gate_up, 1, 1)
+    out = dot(act[...], down, 1, 1)
+    for i in range(4):
+        span = slice(i * 128, i * 128 + 128)
+        backs[i][...] = back[span].astype(backs[i].dtype)
+        outs[i][...] = out[span].astype(outs[i].dtype)
     for block in range(8):
         span = slice(block * 256, block * 256 + 256)
-        part = dot(own[:, span], lin_grad[:128], 0, 0) + dot(other[:, span], lin_grad[128:], 0, 0)
-        part = part.astype(BF16).reshape(2, 4, 32, 1408)
+        part = dot(ffn[:, span], lin_grad[...], 0, 0).astype(BF16).reshape(2, 4, 32, 704)
+        low = dot(cot[:, span], act[...], 0, 0).astype(BF16).reshape(2, 4, 32, 352)
         for core in range(2):
-            out[block, :, core, :, :1408] = part[core]
-        part = dot(cot[:, span], act[:128], 0, 0) + dot(cot_other[:, span], act[128:], 0, 0)
-        part = part.astype(BF16).reshape(2, 4, 32, 704)
-        for core in range(2):
-            out[block, :, core, :, 1408:] = part[core]
+            grads[block // 2, :, block % 2, core, :, :704] = part[core]
+            grads[block // 2, :, block % 2, core, :, DOWN : DOWN + 352] = low[core]
+            grads[block // 2, :, block % 2, core, :, 704:DOWN] = jnp.zeros((4, 32, 64), BF16)
+            grads[block // 2, :, block % 2, core, :, DOWN + 352 :] = jnp.zeros((4, 32, 32), BF16)
+
+
+def finish_kernel(at, p0, p1, p2, p3, query, down, up, attn_gain, latent_gain, *outs):
+    query_out, up_out, out_out, small, ffn_gain_out = outs
+    own = p0[...].astype(F32) + p1[...].astype(F32)
+    other = p2[...].astype(F32) + p3[...].astype(F32)
+    first = at[2] == 0
+    halves = [jnp.where(first, own, other), jnp.where(first, other, own)]
+    heads, lifts = [], []
+    for half in halves:
+        for head in range(4):
+            pair, place = head // 2, head % 2
+            heads.append(half[:, head * 128 : head * 128 + 128])
+            for side in range(2):
+                start = 512 + pair * 128 + side * 64 + place * 32
+                heads.append(half[:, start : start + 32])
+        lifts += [half[8 * j : 8 * j + 8, 1920:2176] for j in range(4)]
+    grads = jnp.concatenate(heads, axis=1)
+    query_out[...] = grads * attn_gain[...].astype(F32)
+    part = jnp.sum(grads * query[...].astype(F32), axis=1, keepdims=True)
+    lift = jnp.concatenate(lifts, axis=1)
+    up_out[...] = lift * latent_gain[...].astype(F32)
+    lift_part = jnp.sum(lift * up[...].astype(F32), axis=1, keepdims=True)
+    out_out[:, :512] = halves[0][:, 1408:1920]
+    out_out[:, 512:] = halves[1][:, 1408:1920]
+    both = own + other
+    small[:, :512] = both[:, 768:1280]
+    turned = jnp.concatenate(
+        [
+            both[:, 1280:1312] + both[:, 1312:1344],
+            both[:, 1344:1376] + both[:, 1376:1408],
+            both[:, 2176:2240],
+        ],
+        axis=1,
+    )
+    small[:, 512:640] = turned
+    part += jnp.sum(down[:, :512].astype(F32) * both[:, 768:1280], axis=1, keepdims=True)
+    part += jnp.sum(down[:, 512:].astype(F32) * turned[:, :64], axis=1, keepdims=True)
+    small[:, 640:768] = jnp.broadcast_to(part, (32, 128))
+    small[:, 768:] = jnp.zeros((32, 128), F32)
+    small[:8, 768:] = jnp.broadcast_to(lift_part, (8, 128))
+    ffn_gain_out[...] = both[:, 2240:2241]
+
+
+def shared_finish_kernel(at, stay, across, beside, corner, gate, up, down):
+    core, side = at[2] == 0, at[1] == 0
+    own = [ref[...].astype(F32) for ref in (stay, beside)]
+    other = [ref[...].astype(F32) for ref in (across, corner)]
+    own = [jnp.where(side, own[0], own[1]), jnp.where(side, own[1], own[0])]
+    other = [jnp.where(side, other[0], other[1]), jnp.where(side, other[1], other[0])]
+    parts = [jnp.where(core, a, b) for a, b in zip(own, other, strict=True)]
+    parts += [jnp.where(core, b, a) for a, b in zip(own, other, strict=True)]
+    gate[...] = jnp.concatenate([part[:, :352] for part in parts], axis=1)
+    up[...] = jnp.concatenate([part[:, 352:704] for part in parts], axis=1)
+    down[...] = jnp.concatenate([part[:, DOWN : DOWN + 352] for part in parts], axis=1)
 
 
 def doc_positions(doc_row):
@@ -418,44 +624,28 @@
     capacity = 16
     every = ("x", "z", "c", "y")
 
-    gain_col = attn_gain.astype(F32)[:, None]
-    heads = query_weight.reshape(32, 2, 2, 2, HEAD)
-    query_plain = heads[..., :NOPE].reshape(32, 2, 512)
-    query_turn = heads[..., NOPE:].reshape(32, 2, 2, 2, 2, 32).transpose(0, 1, 2, 4, 3, 5)
-    query_pack = jnp.concatenate([query_plain, query_turn.reshape(32, 2, 256)], axis=2)
-    query_pack = query_pack.transpose(1, 0, 2)
-    down_pack = jnp.concatenate(
-        [latent_down[:, :544], latent_down[:, 512:], latent_down[:, 544:]], axis=1
-    )
-    up_pack = latent_up.reshape(8, 2, 4, 256).transpose(1, 0, 2, 3)
-    up_scaled = (up_pack.astype(F32) * latent_gain.astype(F32)[None, :, None, None]).astype(BF16)
-    shared_pack = jnp.concatenate(
-        [
-            shared_gate.reshape(32, 2, 704),
-            shared_up.reshape(32, 2, 704),
-            shared_down.reshape(2, 704, 32).transpose(2, 0, 1),
-        ],
-        axis=2,
-    )
-    both = jnp.concatenate([router, ffn_gain[:, None]], axis=1)
-    pack = jnp.concatenate(
-        [
-            (query_pack.astype(F32) * gain_col).astype(BF16),
-            jnp.broadcast_to((down_pack.astype(F32) * gain_col).astype(BF16), (2, 32, 640)),
-            output_weight.reshape(2, 512, 32).transpose(0, 2, 1),
-            up_scaled.reshape(2, 32, 256),
-            shared_pack.transpose(1, 0, 2),
-            jnp.broadcast_to(jnp.pad(both, ((0, 0), (0, 63))), (2, 32, 128)),
-        ],
-        axis=2,
-    )
-    weights = gather_rows(pack, at)
-    in_all = weights[:, :1408]
-    out_all = weights[:, 1408:1920]
-    up_all = weights[:, 1920:2176].reshape(LATENT, 1024)
-    gate_up_all = weights[:, 2176:3584]
-    down_all = weights[:, 3584:4288]
-    router_all = weights[:, 4288:4352]
+    keep, send, *quarters = call(
+        pack_kernel,
+        [(32, LANES)] * 2 + [(32, QUARTER)] * 4,
+        [BF16] * 6,
+        at,
+        query_weight,
+        latent_down,
+        latent_up,
+        output_weight.T,
+        shared_gate,
+        shared_up,
+        shared_down.T,
+        router,
+        attn_gain[:, None],
+        latent_gain[:, None],
+        ffn_gain[:, None],
+        scratch=[pltpu.VMEM((2, 32, LANES), BF16), pltpu.VMEM((4, 32, QUARTER), BF16)],
+        many=True,
+    )
+    pieces = gather_rows(keep, send, at)
+    shared_rows = quad_exchange(quarters).reshape(128, QUARTER)
+    cot_four = quad_blocks(cotangent)
 
     named = jnp.any(
         routes.T[None, :, :] == jnp.arange(experts_count, dtype=jnp.int32)[:, None, None], axis=1
@@ -467,18 +657,10 @@
     ).astype(BF16)
     slots = slots.reshape(experts_count * capacity, rows)
 
-    def to_experts(values):
-        sent = dot(slots, values).astype(BF16).reshape(experts_count, capacity, width)
-        got = lax.all_to_all(sent, every, split_axis=0, concat_axis=0, tiled=True)
-        return got.reshape(-1, width)
-
-    def return_rows(values):
+    def exchange_rows(values):
         sent = values.reshape(experts_count, capacity, width)
         got = lax.all_to_all(sent, every, split_axis=0, concat_axis=0, tiled=True)
         return got.reshape(-1, width)
-
-    cot_sent, in_all = lax.optimization_barrier((cotangent, in_all))
-    expert_cot = to_experts(cot_sent)
 
     docs = jnp.concatenate([documents, shift(documents, "c", 1)])
     positions = jax.vmap(doc_positions)(docs)
@@ -492,29 +674,46 @@
     doc_row, doc_col = doc[None, :], doc[:, None]
 
     tokens_other = shift(tokens_in, "c", 1)
+    cot_sent = dot(slots, cotangent).astype(BF16)
+    cot_sent, pieces, shared_rows, cot_four, cosine, sine, doc_row, doc_col, tokens_other = (
+        lax.optimization_barrier(
+            (cot_sent, pieces, shared_rows, cot_four, cosine, sine, doc_row, doc_col, tokens_other)
+        )
+    )
+    expert_cot = exchange_rows(cot_sent)
+    shared_all = lax.all_gather(shared_rows, ("x", "y"), axis=0, tiled=True)
+    shared_all = shared_all.reshape(4, 4, 2, 2, 32, QUARTER)
     sent = [(rows, MSG)] * 4
     two = 2 * rows
-    *sent, normed_low, latent_low, latent_normed, latent_inverse = call(
+    six = (4, 2, 2, 4, 32)
+    outs = call(
         project_kernel,
-        sent + [(two, width), (two, LATENT), (two, LATENT), (two, 128)],
-        [BF16] * 6 + [F32, F32],
-        at,
+        sent
+        + [(two, width), (two, LATENT), (two, LATENT), (two, 128)]
+        + [six + (1408,), six + (512,), (LATENT, 1024), six + (128,)],
+        [BF16] * 6 + [F32, F32] + [BF16] * 4,
+        at,
+        *pieces,
         tokens_in,
         tokens_other,
-        in_all,
-        up_all,
         cosine,
         sine,
         scratch=[
             pltpu.VMEM((two, 768), BF16),
             pltpu.VMEM((two, 1024), BF16),
             pltpu.VMEM((two, 128), BF16),
+            pltpu.VMEM(six + (256,), BF16),
+            pltpu.SemaphoreType.DMA((4, 16)),
         ],
         flops=1_800_000_000,
         many=True,
-    )
+        far=16,
+    )
+    sent, normed_low, latent_low, latent_normed, latent_inverse = outs[:4], *outs[4:8]
+    in_all, out_all = outs[8].reshape(width, 1408), outs[9].reshape(width, 512)
+    up_all, tail_all = outs[10], outs[11].reshape(width, 128)
     received = to_ring(sent)
-    received[0], expert_cot = lax.optimization_barrier((received[0], expert_cot))
+    received, expert_cot = lax.optimization_barrier((received, expert_cot))
     msg, *mixed = call(
         forward_kernel,
         [(4, rows, MSG)] + [(rows, 256)] * 4,
@@ -540,50 +739,58 @@
     tokens_f = tokens_in.astype(F32)
     resid = tokens_f + half_sum(core_sum(out_own, out_other))
 
-    pointer = jnp.broadcast_to(jnp.arange(64)[None, :] == 0, (8, 64)).astype(BF16)
-    gain_two = dot(pointer, weights[:, 4352:], 1, 1)[:1]
+    pointer = jnp.broadcast_to(jnp.arange(128)[None, :] == 64, (8, 128)).astype(BF16)
+    gain_two = dot(pointer, tail_all, 1, 1)[:1]
+    router_all = tail_all[:, :64]
     inverse_two = rms(resid)
     normed_two = resid * inverse_two
     ffn_in = (normed_two * gain_two).astype(BF16)
-    expert_rows = to_experts(ffn_in)
-
-    ffn_other = shift(ffn_in, "c", 1)
-    cot_other = shift(cotangent, "c", 1)
-    ffn_two = jnp.concatenate([ffn_in, ffn_other])
-    cot_two = jnp.concatenate([cotangent, cot_other])
-    shared_lin = dot(ffn_two, gate_up_all)
-    shared_up_lin = shared_lin[:, 704:]
-    shared_silu, shared_slope = silu_parts(shared_lin[:, :704])
-    shared_act = (shared_silu * shared_up_lin).astype(BF16)
-    shared_dact = dot(cot_two, down_all)
-    shared_dlin = jnp.concatenate(
-        [shared_dact * shared_up_lin * shared_slope, shared_dact * shared_silu], axis=1
-    ).astype(BF16)
-    shared_out = dot(shared_act, down_all, 1, 1)
-    shared_out = core_sum(shared_out[:rows], shared_out[rows:].astype(BF16))
-    shared_back = dot(shared_dlin, gate_up_all, 1, 1)
-    shared_back = core_sum(shared_back[:rows], shared_back[rows:].astype(BF16))
-    shared_grads = call(
-        shared_grads_kernel,
-        (8, 4, 2, 32, 2112),
-        BF16,
-        at,
-        ffn_in,
-        ffn_other,
-        shared_dlin,
-        cotangent,
-        cot_other,
-        shared_act,
-        flops=2_200_000_000,
-    )
+    ffn_sent = dot(slots, ffn_in).astype(BF16)
+    ffn_four, ffn_sent = lax.optimization_barrier((quad_blocks(ffn_in), ffn_sent))
+    expert_rows = exchange_rows(ffn_sent)
+
+    *shared_parts, shared_grads = call(
+        shared_kernel,
+        [(rows, width)] * 8 + [(4, 4, 2, 2, 32, QUARTER)],
+        [F32, BF16, F32, BF16] * 2 + [BF16],
+        at,
+        shared_all,
+        *ffn_four,
+        *cot_four,
+        scratch=[
+            pltpu.VMEM((4, 2, 2, 4, 32, QUARTER), BF16),
+            pltpu.VMEM((4 * rows, width), BF16),
+            pltpu.VMEM((4 * rows, width), BF16),
+            pltpu.VMEM((4 * rows, 704), BF16),
+            pltpu.VMEM((4 * rows, 352), BF16),
+            pltpu.SemaphoreType.DMA((4,)),
+        ],
+        flops=7_000_000_000,
+        many=True,
+        far=1,
+    )
+    shared_back = quad_sum(*shared_parts[4:])
     shared_sum = lax.psum_scatter(
-        shared_grads.reshape(width, -1), ("x", "z", "y"), scatter_dimension=0, tiled=True
-    ).reshape(2, 32, -1)
-
+        shared_grads.reshape(width, QUARTER), ("x", "y"), scatter_dimension=0, tiled=True
+    ).reshape(2, 2, 32, QUARTER)
+    own_rows, far_rows = pick(shared_sum, at[1]), pick(shared_sum, 1 - at[1])
+    stay, beside = pick(own_rows, core), shift(pick(far_rows, core), "z", 1)
+    across, corner = shift(pick(own_rows, 1 - core), "c", 1), diagonal(pick(far_rows, 1 - core))
+    shared_gate_grad, shared_up_grad, shared_down_grad = call(
+        shared_finish_kernel,
+        [(32, 1408)] * 3,
+        [F32] * 3,
+        at,
+        stay,
+        across,
+        beside,
+        corner,
+        many=True,
+    )
     gate_w, up_w, down_w = expert_gate[0], expert_up[0], expert_down[0]
     plain_grad = dot(expert_cot, down_w, 1, 1)
-    expert_rows, shared_back, shared_out, plain_grad, shared_grads = lax.optimization_barrier(
-        (expert_rows, shared_back, shared_out, plain_grad, shared_grads)
+    expert_rows, plain_grad, shared_parts, shared_grads = lax.optimization_barrier(
+        (expert_rows, plain_grad, shared_parts, shared_grads)
     )
     probs = jax.nn.softmax(dot(expert_rows, router_all), axis=1)
     mine = (jnp.arange(experts_count, dtype=jnp.int32) == expert)[None, :].astype(F32)
@@ -601,15 +808,15 @@
     row_grad = (
         dot(gate_grad, gate_w, 1, 1) + dot(up_grad, up_w, 1, 1) + dot(logit_grad, router_all, 1, 1)
     ).astype(BF16)
-    back_rows = return_rows(row_grad)
+    back_rows = exchange_rows(row_grad)
     piece = dot(act_low, down_w).astype(BF16)
     expert_down_grad = dot(act_low, expert_cot, 0, 0)[None]
     expert_gate_grad = dot(expert_rows, gate_grad, 0, 0)[None]
     expert_up_grad = dot(expert_rows, up_grad, 0, 0)[None]
     router_grad = dot(expert_rows, logit_grad, 0, 0)
-    back_rows, piece, expert_down_grad, expert_gate_grad, expert_up_grad, router_grad = (
+    back_rows, piece, expert_down_grad, expert_gate_grad, expert_up_grad, router_grad, shared_back = (
         lax.optimization_barrier(
-            (back_rows, piece, expert_down_grad, expert_gate_grad, expert_up_grad, router_grad)
+            (back_rows, piece, expert_down_grad, expert_gate_grad, expert_up_grad, router_grad, shared_back)
         )
     )
     routed_back = dot(slots, back_rows, 0, 0)
@@ -634,7 +841,9 @@
         many=True,
     )
     heads_got = to_ring(heads_grad)
-    piece, heads_got[0] = lax.optimization_barrier((piece, heads_got[0]))
+    heads_got, shared_gate_grad, shared_up_grad, shared_down_grad = lax.optimization_barrier(
+        (heads_got, shared_gate_grad, shared_up_grad, shared_down_grad)
+    )
     back = call(
         backward_kernel,
         [(rows, MSG)] * 4,
@@ -653,12 +862,14 @@
         flops=1_500_000_000,
         many=True,
     )
+    returned, piece = lax.optimization_barrier((to_ring(back), piece))
+    piece_rows = exchange_rows(piece)
     lin_grad, kv_grad, in_own, in_other = call(
         return_kernel,
         [(two, 1408), (two, 1024), (rows, width), (rows, width)],
         [BF16, BF16, F32, BF16],
         at,
-        *to_ring(back),
+        *returned,
         in_all,
         up_all,
         cosine,
@@ -669,9 +880,8 @@
         flops=1_800_000_000,
         many=True,
     )
-    up_part = dot(latent_low, kv_grad, 0, 0).astype(BF16).reshape(width, 256)
     tail = jnp.concatenate([router_grad, ffn_gain_part], axis=1).astype(BF16)
-    pieces = call(
+    blocks = call(
         grads_kernel,
         [(4, 32, 2304)] * 16,
         [BF16] * 16,
@@ -681,71 +891,55 @@
         resid_low,
         resid_other,
         attended,
-        up_part,
+        latent_low,
+        kv_grad,
         tail,
-        scratch=[pltpu.VMEM((8, 32, 2304), BF16)],
+        scratch=[pltpu.VMEM((8, 32, 2304), BF16), pltpu.VMEM((64, 4, 8, 256), F32)],
         flops=2_200_000_000,
         many=True,
     )
-    pairs = [pieces[2 * i : 2 * i + 2] for i in range(8)]
-    attn_sum = scatter_rows(pairs[:4], pairs[4:])
+    blocks = list(blocks)
+    blocks[4], blocks[5], blocks[12], blocks[13], piece_rows = lax.optimization_barrier(
+        (blocks[4], blocks[5], blocks[12], blocks[13], piece_rows)
+    )
+    pairs = [blocks[2 * i : 2 * i + 2] for i in range(8)]
+    attn_sum = scatter_rows(pairs[:4], pairs[4:], at)
 
     attn_in_grad = half_sum(core_sum(in_own, in_other))
     inverse_one = rms(tokens_f)
     input_grad = resid_grad + norm_back(attn_in_grad, tokens_f * inverse_one, inverse_one)
-    routed_out = dot(slots, return_rows(piece), 0, 0)
+    routed_out = dot(slots, piece_rows, 0, 0)
+    shared_out = quad_sum(*shared_parts[:4])
     layer_out = (resid + half_sum(shared_out + routed_out)).astype(BF16)
 
-    shared_sum = lax.all_to_all(shared_sum, "c", split_axis=0, concat_axis=0, tiled=True)
-    shared_sum = shared_sum.astype(F32)
-    query_sum = attn_sum[..., :768]
-    up_sum = attn_sum[..., 1920:2176]
-    down_sum = attn_sum[0, :, 768:1408] + attn_sum[1, :, 768:1408]
-    down_sum = jnp.concatenate(
-        [
-            down_sum[:, :512],
-            down_sum[:, 512:544] + down_sum[:, 544:576],
-            down_sum[:, 576:608] + down_sum[:, 608:],
-        ],
-        axis=1,
-    )
-    attn_gain_part = jnp.sum(query_pack.astype(F32) * query_sum, axis=(0, 2)) + jnp.sum(
-        latent_down.astype(F32) * down_sum, axis=1
-    )
-    latent_gain_part = jnp.sum(up_pack.reshape(2, 32, 256).astype(F32) * up_sum, axis=(0, 2))
-    tail_sum = attn_sum[0, :, 2176:] + attn_sum[1, :, 2176:]
-    small = jnp.concatenate(
-        [down_sum, tail_sum[:, :64], attn_gain_part[:, None], latent_gain_part[:, None]], axis=1
+    query_out, up_out, out_out, small, ffn_gain_grad = call(
+        finish_kernel,
+        [(32, 1536), (8, 2048), (32, 1024), (32, 896), (32, 1)],
+        [F32] * 5,
+        at,
+        *attn_sum,
+        query_weight,
+        latent_down,
+        latent_up,
+        attn_gain[:, None],
+        latent_gain[:, None],
+        many=True,
     )
     small = small + shift(small, "t", 1)
-    attn_gain_grad = small[:, 640]
-    latent_gain_grad = jnp.sum(small[:, 641].reshape(8, 4), axis=1)
-    latent_down_grad = gain_col * small[:, :576]
-    router_out = small[:, 576:640]
-    query_plain = query_sum[..., :512].reshape(2, 32, 2, 2, NOPE)
-    query_turn = query_sum[..., 512:].reshape(2, 32, 2, 2, 2, 32).transpose(0, 1, 2, 4, 3, 5)
-    query_turn = query_turn.reshape(2, 32, 2, 2, ROPE)
-    query_out = jnp.concatenate([query_plain, query_turn], axis=4).transpose(1, 0, 2, 3, 4)
-    query_out = gain_col * query_out.reshape(32, 2 * 4 * HEAD)
-    up_out = up_sum.reshape(2, 8, 4, 256).transpose(1, 0, 2, 3).reshape(8, 2048)
-    up_out = latent_gain.astype(F32)[:, None] * up_out
-    out_out = attn_sum[..., 1408:1920].transpose(0, 2, 1).reshape(1024, 32)
-    ffn_gain_grad = tail_sum[:, 64]
-    shared_rows = shared_sum.transpose(1, 0, 2)
     return (
         layer_out,
         input_grad,
-        attn_gain_grad,
+        small[:, 640],
         query_out,
-        latent_down_grad,
-        latent_gain_grad,
+        attn_gain.astype(F32)[:, None] * small[:, :576],
+        small[:8, 768],
         up_out,
-        out_out,
-        ffn_gain_grad,
-        router_out,
-        shared_rows[..., :704].reshape(32, 1408),
-        shared_rows[..., 704:1408].reshape(32, 1408),
-        shared_sum[..., 1408:2112].transpose(0, 2, 1).reshape(1408, 32),
+        out_out.T,
+        ffn_gain_grad[:, 0],
+        small[:, 576:640],
+        shared_gate_grad,
+        shared_up_grad,
+        shared_down_grad.T,
         expert_gate_grad,
         expert_up_grad,
         expert_down_grad,

time: 824 us -> 680 us (0.83)
  waiting for transfers between devices: 334 us -> 262 us
  local copies, waits for them, and re-layouts: 90.4 us -> 23.5 us
  Pallas kernels: 63.7 us -> 91.7 us
  matrix products: 96.7 us -> 78.9 us
  other arithmetic: 38.7 us -> 30.3 us
    ppermute x78 -> x84, waiting for transfers between devices: 276 us -> 179 us  [shift(): lax.ppermute(values, axis, [(j, (j + step) % size) for j in range(size)])]
    pallas_call x12 -> x19, Pallas kernels: 63.7 us -> 91.7 us  [call(): pl.pallas_call(kernel, out_shape=out_shape, in_specs=[pl.BlockSpec(memory...]
    dynamic_update_slice x16 -> x0, local copies, waits for them, and re-layouts: 26.7 us -> none  [the longest x8 14 us: put_one(): lax.dynamic_update_slice(buffer, piece.reshape(4, 1, 1, 1, 32, lanes), st...]
    all_to_all x4, waiting for transfers between devices: 53.1 us -> 78.6 us  [exchange_rows(): got = lax.all_to_all(sent, every, split_axis=0, concat_axis=0, tiled=True)]
    slice x17 -> x4, local copies, waits for them, and re-layouts: 20.9 us -> 2.71 us  [the longest x1 5.51 us: shards(): in_all = weights[:, :1408]]
    dot_general x24 -> x19, matrix products: 96.7 us -> 78.9 us  [dot(): lax.dot_general(left, right, (((left_dim,), (right_dim,)), ((), ())), pre...]
    reshape x27 -> x1, local copies, waits for them, and re-layouts: 16.8 us -> 0.02 us  [the longest x1 2.48 us: shards(): up_all = weights[:, 1920:2176].reshape(LATENT, 1024)]
    ppermute x78 -> x84, starting transfers between devices: 114 us -> 128 us  [shift(): lax.ppermute(values, axis, [(j, (j + step) % size) for j in range(size)])]
  transfers between devices with their start and end apart: 85 -> 94, of which waited for: 36 -> 33; matrix products, arithmetic and copies ran while one was open for 18% -> 17% of each run, Pallas kernels for 6% -> 12%
where the time goes in v3:
time: 680 us; the launch traced here: 670 us
  waiting for transfers between devices  262 us (39%)
  starting transfers between devices  168 us (25%)
  Pallas kernels  91.7 us (13%)
  matrix products  78.9 us (12%)
  other arithmetic  30.3 us (4%)
  local copies, waits for them, and re-layouts  23.5 us (3%)
  between operations  15.1 us (2%)
    ppermute x84, waiting for transfers between devices, shift(): lax.ppermute(values, axis, [(j, (j + step) % size) for j in range(size)])  179 us
    ppermute x84, starting transfers between devices, shift(): lax.ppermute(values, axis, [(j, (j + step) % size) for j in range(size)])  128 us
    pallas_call x19, Pallas kernels, call(): pl.pallas_call(kernel, out_shape=out_shape, in_specs=[pl.BlockSpec(memory...  91.7 us
    dot_general x19, matrix products, dot(): lax.dot_general(left, right, (((left_dim,), (right_dim,)), ((), ())), pre...  78.9 us
    all_to_all x4, waiting for transfers between devices, exchange_rows(): got = lax.all_to_all(sent, every, split_axis=0, concat_axis=0, tiled=True)  78.6 us
    all_to_all x4, starting transfers between devices, exchange_rows(): got = lax.all_to_all(sent, every, split_axis=0, concat_axis=0, tiled=True)  35.7 us
  transfers between devices with their start and end apart: 94, of which 33 were waited for; matrix products, arithmetic and copies ran while one was open for 17% of the time, Pallas kernels for 12%

profile of v3, /device:TPU:1, one launch (start us, length us, event | category | flops | bytes accessed | tf_op | source)
XLA Modules:
  0.0 670.0 jit_solution(8778331551818506174)
XLA Ops:
  56.9 6.3 collective-permute-start.34
  90.5 10.0 %collective-permute-done.24.refs_13_ = bf16[4,32,2304]{2,1,0:T(8,128)(2,1)} collective-permute-done((bf16[4,32,2304]{2,1,0:T(8,128)(2,1)}, bf16[4,32,2304]{2,1,0:T(8,128)(2,1)}, u32[]{:S(2)}, u32[]{:S(2)}) %collective-permute-start.24) | collective-permute-done | bytes 589856 | tf_op jit(solution)/shard_map/ppermute | solution.py:31
  104.9 9.1 %collective-permute-done.19.refs_11_ = bf16[4,32,2304]{2,1,0:T(8,128)(2,1)} collective-permute-done((bf16[4,32,2304]{2,1,0:T(8,128)(2,1)}, bf16[4,32,2304]{2,1,0:T(8,128)(2,1)}, u32[]{:S(2)}, u32[]{:S(2)}) %collective-permute-start.19) | collective-permute-done | bytes 589856 | tf_op jit(solution)/shard_map/ppermute | solution.py:31
  114.0 8.8 %all-to-all-start = ((bf16[64,16,2048]{2,1,0:T(8,128)(2,1)}), bf16[64,16,2048]{2,1,0:T(8,128)(2,1)}, u32[]{:S(2)}, u32[]{:S(2)}) async-start(bf16[64,16,2048]{2,1,0:T(8,128)(2,1)} %bitcast.110), calls=%async_computation | async-start | bytes 8388608 | tf_op jit(solution)/shard_map/all_to_all | solution.py:662
  124.3 11.8 %shard_map.302 = (bf16[128,1024]{1,0:T(8,128)(2,1)}, bf16[128,1024]{1,0:T(8,128)(2,1)}, bf16[128,1024]{1,0:T(8,128)(2,1)}, bf16[128,1024]{1,0:T(8,128)(2,1)}, bf...) custom-call(s32[4]{0:T(128)} %pad_add_fusion.1.at, ...), custom_call_target="tpu_custom_call" | custom-call | flops 1800000000 | bytes 23199744 | tf_op jit(solution)/shard_map/pallas_call | solution.py:243
  142.0 40.1 %collective-permute-done.35.m1 = bf16[128,1024]{1,0:T(8,128)(2,1)S(1)} collective-permute-done((bf16[128,1024]{1,0:T(8,128)(2,1)}, bf16[128,1024]{1,0:T(8,128)(2,1)S(1)}, u32[]{:S(2)}, u32[]{:S(2)}) %collective-permute-start.35) | collective-permute-done | bytes 262176 | tf_op jit(solution)/shard_map/ppermute | solution.py:31
  216.0 11.6 %collective-permute-done.42 = bf16[128,2048]{1,0:T(8,128)(2,1)S(1)} collective-permute-done((bf16[128,2048]{1,0:T(8,128)(2,1)S(1)}, bf16[128,2048]{1,0:T(8,128)(2,1)S(1)}, u32[]{:S(2)}, u32[]{:S(2)}) %collective-permute-start.42) | collective-permute-done | bytes 524320 | tf_op jit(solution)/shard_map/ppermute | solution.py:31
  232.7 9.5 %collective-permute-done.44.refs_2_ = bf16[128,2048]{1,0:T(8,128)(2,1)S(1)} collective-permute-done((bf16[128,2048]{1,0:T(8,128)(2,1)S(1)}, bf16[128,2048]{1,0:T(8,128)(2,1)S(1)}, u32[]{:S(2)}, u32[]{:S(2)}) %collective-permute-start.44) | collective-permute-done | bytes 524320 | tf_op jit(solution)/shard_map/ppermute | solution.py:31
  249.0 7.9 %all-to-all-start.1 = ((bf16[64,16,2048]{2,1,0:T(8,128)(2,1)}), bf16[64,16,2048]{2,1,0:T(8,128)(2,1)}, u32[]{:S(2)}, u32[]{:S(2)}) async-start(bf16[64,16,2048]{2,1,0:T(8,128)(2,1)} %bitcast.111), calls=%async_computation.1 | async-start | bytes 8388608 | tf_op jit(solution)/shard_map/all_to_all | solution.py:662
  257.1 16.1 %shard_map.305 = (f32[128,2048]{1,0:T(8,128)}, bf16[128,2048]{1,0:T(8,128)(2,1)}, f32[128,2048]{1,0:T(8,128)}, bf16[128,2048]{1,0:T(8,128)(2,1)}, f32[128,2048]{...) custom-call(s32[4]{0:T(128)} %pad_add_fusion.1.at, ...), custom_call_target="tpu_custom_call" | custom-call | flops 7000000000 | bytes 19922944 | tf_op jit(solution)/shard_map/pallas_call | solution.py:243
  273.8 6.9 %fusion.9 = f32[1024,704]{0,1:T(8,128)} fusion(bf16[1024,2048]{1,0:T(8,128)(2,1)} %bitcast.21, bf16[1,704,2048]{2,1,0:T(8,128)(2,1)S(1)} %copy-done.63), kind=kOutput, calls=%fused_computation.16 | convolution fusion | flops 2952790016 | bytes 9961472 | tf_op jit(solution)/shard_map/dot_general | solution.py:24
  284.3 26.3 %all-to-all-done.1 = bf16[64,16,2048]{2,1,0:T(8,128)(2,1)} async-done(((bf16[64,16,2048]{2,1,0:T(8,128)(2,1)}), bf16[64,16,2048]{2,1,0:T(8,128)(2,1)}, u32[]{:S(2)}, u32[]{:S(2)}) %all-to-all-start.1) | async-done | bytes 4194336 | tf_op jit(solution)/shard_map/all_to_all | solution.py:662
  314.5 5.7 fusion.2
  320.4 7.9 %multiply_reduce_fusion = (f32[1024]{0:T(1024)S(1)}, bf16[1024,704]{0,1:T(8,128)(2,1)S(1)}, bf16[1024,704]{0,1:T(8,128)(2,1)}, bf16[1024,704]{0,1:T(8,128)(2,1)S(1)}) fusion(f32[1024,704]{0,1:T(8,128)S(1)} %copy-done.81, f32[1024,704]{0,1:T(8,128)S(1)} %fusion.2, f32[1024]{0:T(1024)S(1)} %multiply_reduce_fusion.3, bf16[1024,2048]{1,0:T(8,128)(2,1)} %bitcast.26, ...), kind=kOutput, calls=%fused_computation.19 | convolution fusion | flops 2966486016 | bytes 17178624 | tf_op jit(solution)/shard_map/dot_general | solution.py:24
  338.7 11.1 %all-to-all-start.2 = ((bf16[64,16,2048]{2,1,0:T(8,128)(2,1)}), bf16[64,16,2048]{2,1,0:T(8,128)(2,1)}, u32[]{:S(2)}, u32[]{:S(2)}) async-start(bf16[64,16,2048]{2,1,0:T(8,128)(2,1)} %bitcast.112), calls=%async_computation.2 | async-start | bytes 8388608 | tf_op jit(solution)/shard_map/all_to_all | solution.py:662
  360.8 7.2 %convolution_bitcast_fusion.2 = f32[1,704,2048]{2,1,0:T(8,128)} fusion(bf16[1024,704]{0,1:T(8,128)(2,1)S(1)} %copy-done.82, bf16[1024,2048]{1,0:T(8,128)(2,1)} %bitcast.21), kind=kOutput, calls=%fused_computation.6 | convolution fusion | flops 2952790016 | bytes 11403264 | tf_op jit(solution)/shard_map/dot_general | solution.py:24
  368.0 7.2 %convolution_bitcast_fusion.1 = f32[1,2048,704]{1,2,0:T(8,128)} fusion(bf16[1024,704]{0,1:T(8,128)(2,1)S(1)} %copy-done.80, bf16[1024,2048]{1,0:T(8,128)(2,1)} %bitcast.26), kind=kOutput, calls=%fused_computation.5 | convolution fusion | flops 2952790016 | bytes 11403264 | tf_op jit(solution)/shard_map/dot_general | solution.py:24
  375.2 7.1 %convolution_bitcast_fusion = f32[1,2048,704]{1,2,0:T(8,128)} fusion(bf16[1024,704]{0,1:T(8,128)(2,1)S(1)} %copy-done.78, bf16[1024,2048]{1,0:T(8,128)(2,1)} %bitcast.26), kind=kOutput, calls=%fused_computation.4 | convolution fusion | flops 2952790016 | bytes 11403264 | tf_op jit(solution)/shard_map/dot_general | solution.py:24
  382.3 23.1 %all-to-all-done.2 = bf16[64,16,2048]{2,1,0:T(8,128)(2,1)} async-done(((bf16[64,16,2048]{2,1,0:T(8,128)(2,1)}), bf16[64,16,2048]{2,1,0:T(8,128)(2,1)}, u32[]{:S(2)}, u32[]{:S(2)}) %all-to-all-start.2) | async-done | bytes 4194336 | tf_op jit(solution)/shard_map/all_to_all | solution.py:662
  412.3 12.4 %collective-permute-done.52 = bf16[128,2048]{1,0:T(8,128)(2,1)S(1)} collective-permute-done((bf16[128,2048]{1,0:T(8,128)(2,1)S(1)}, bf16[128,2048]{1,0:T(8,128)(2,1)S(1)}, u32[]{:S(2)}, u32[]{:S(2)}) %collective-permute-start.52) | collective-permute-done | bytes 524320 | tf_op jit(solution)/shard_map/ppermute | solution.py:31
  441.5 6.9 %shard_map.308 = (bf16[128,1024]{1,0:T(8,128)(2,1)}, bf16[128,1024]{1,0:T(8,128)(2,1)}, bf16[128,1024]{1,0:T(8,128)(2,1)}, bf16[128,1024]{1,0:T(8,128)(2,1)}) custom-call(s32[4]{0:T(128)} %pad_add_fusion.1.at, bf16[4,128,1024]{2,1,0:T(8,128)(2,1)} %get-tuple-element.235.msg_ref, bf16[128,256]{1,0:T(8,128)(2,1)} %get-tuple-element.247.g0, ...), custom_call_target="tpu_custom_call" | custom-call | flops 1500000000 | bytes 2363392 | tf_op jit(solution)/shard_map/pallas_call | solution.py:243
  456.7 6.8 %collective-permute-done.61.b2 = bf16[128,1024]{1,0:T(8,128)(2,1)S(1)} collective-permute-done((bf16[128,1024]{1,0:T(8,128)(2,1)}, bf16[128,1024]{1,0:T(8,128)(2,1)S(1)}, u32[]{:S(2)}, u32[]{:S(2)}) %collective-permute-start.61) | collective-permute-done | bytes 262176 | tf_op jit(solution)/shard_map/ppermute | solution.py:31
  464.4 7.9 %all-to-all-start.3 = ((bf16[64,16,2048]{2,1,0:T(8,128)(2,1)}), bf16[64,16,2048]{2,1,0:T(8,128)(2,1)}, u32[]{:S(2)}, u32[]{:S(2)}) async-start(bf16[64,16,2048]{2,1,0:T(8,128)(2,1)} %bitcast.120), calls=%async_computation.4 | async-start | bytes 8388608 | tf_op jit(solution)/shard_map/all_to_all | solution.py:662
  475.4 8.4 %shard_map.309 = (bf16[256,1408]{1,0:T(8,128)(2,1)}, bf16[256,1024]{1,0:T(8,128)(2,1)}, f32[128,2048]{1,0:T(8,128)}, bf16[128,2048]{1,0:T(8,128)(2,1)}) custom-call(s32[4]{0:T(128)} %pad_add_fusion.1.at, bf16[128,1024]{1,0:T(8,128)(2,1)} %get-tuple-element.256.b0, bf16[128,1024]{1,0:T(8,128)(2,1)} %copy-done.38, bf16[128,1024]{1,0:T(8,128)(2,1)} %copy-done.39, ...), custom_call_target="tpu_custom_call" | custom-call | flops 1800000000 | bytes 11599872 | tf_op jit(solution)/shard_map/pallas_call | solution.py:243
  484.7 9.6 %shard_map.310 = (bf16[4,32,2304]{2,1,0:T(8,128)(2,1)}, bf16[4,32,2304]{2,1,0:T(8,128)(2,1)}, bf16[4,32,2304]{2,1,0:T(8,128)(2,1)}, bf16[4,32,2304]{2,1,0:T(8,12...) custom-call(s32[4]{0:T(128)} %pad_add_fusion.1.at, ...), custom_call_target="tpu_custom_call" | custom-call | flops 2200000000 | bytes 13828096 | tf_op jit(solution)/shard_map/pallas_call | solution.py:243
  494.3 29.1 %all-to-all-done.3 = bf16[64,16,2048]{2,1,0:T(8,128)(2,1)} async-done(((bf16[64,16,2048]{2,1,0:T(8,128)(2,1)}), bf16[64,16,2048]{2,1,0:T(8,128)(2,1)}, u32[]{:S(2)}, u32[]{:S(2)}) %all-to-all-start.3) | async-done | bytes 4194336 | tf_op jit(solution)/shard_map/all_to_all | solution.py:662
  530.3 8.6 %collective-permute-done.67 = bf16[4,32,2304]{2,1,0:T(8,128)(2,1)S(1)} collective-permute-done((bf16[4,32,2304]{2,1,0:T(8,128)(2,1)}, bf16[4,32,2304]{2,1,0:T(8,128)(2,1)S(1)}, u32[]{:S(2)}, u32[]{:S(2)}) %collective-permute-start.67) | collective-permute-done | bytes 589856 | tf_op jit(solution)/shard_map/ppermute | solution.py:31
  539.1 14.5 %collective-permute-done.70 = bf16[4,32,2304]{2,1,0:T(8,128)(2,1)S(1)} collective-permute-done((bf16[4,32,2304]{2,1,0:T(8,128)(2,1)S(1)}, bf16[4,32,2304]{2,1,0:T(8,128)(2,1)S(1)}, u32[]{:S(2)}, u32[]{:S(2)}) %collective-permute-start.70) | collective-permute-done | bytes 589856 | tf_op jit(solution)/shard_map/ppermute | solution.py:31
  556.9 10.3 %collective-permute-done.77 = bf16[4,32,2304]{2,1,0:T(8,128)(2,1)S(1)} collective-permute-done((bf16[4,32,2304]{2,1,0:T(8,128)(2,1)S(1)}, bf16[4,32,2304]{2,1,0:T(8,128)(2,1)S(1)}, u32[]{:S(2)}, u32[]{:S(2)}) %collective-permute-start.77) | collective-permute-done | bytes 589856 | tf_op jit(solution)/shard_map/ppermute | solution.py:31
  574.4 9.8 %collective-permute-done.80 = bf16[4,32,2304]{2,1,0:T(8,128)(2,1)S(1)} collective-permute-done((bf16[4,32,2304]{2,1,0:T(8,128)(2,1)S(1)}, bf16[4,32,2304]{2,1,0:T(8,128)(2,1)S(1)}, u32[]{:S(2)}, u32[]{:S(2)}) %collective-permute-start.80) | collective-permute-done | bytes 589856 | tf_op jit(solution)/shard_map/ppermute | solution.py:31
  588.9 6.5 collective-permute-done.71.b2
  632.8 9.5 %collective-permute-start.85 = (bf16[32,2304]{1,0:T(8,128)(2,1)}, bf16[32,2304]{1,0:T(8,128)(2,1)S(1)}, u32[]{:S(2)}, u32[]{:S(2)}) collective-permute-start(bf16[32,2304]{1,0:T(8,128)(2,1)} %get-tuple-element.303), channel_id=1, source_target_pairs={{0,8},{8,0},{1,9},{9,1},{2,10},{10,2},{3,11},{11,3},{4,12},{12,4},... | collective-permute-start | bytes 442376 | tf_op jit(solution)/shard_map/ppermute | solution.py:31
  (428 shorter events, 280.6 us)
Async XLA Ops:
  27.7 29.2 %collective-permute-start.30 = (bf16[128,2048]{1,0:T(8,128)(2,1)}, bf16[128,2048]{1,0:T(8,128)(2,1)}, u32[]{:S(2)}, u32[]{:S(2)}) collective-permute-start(bf16[128,2048]{1,0:T(8,128)(2,1)} %refs_4_), channel_id=1, source_target_pairs={{0,8},{8,0},{1,9},{9,1},{2,10},{10,2},{3,11},{11,3},{4,12},{12,4},... | collective-permute-start | bytes 1572872 | tf_op jit(solution)/shard_map/ppermute | solution.py:31
  51.1 22.7 %collective-permute-start.3 = (bf16[4,32,2304]{2,1,0:T(8,128)(2,1)}, bf16[4,32,2304]{2,1,0:T(8,128)(2,1)}, u32[]{:S(2)}, u32[]{:S(2)}) collective-permute-start(bf16[4,32,2304]{2,1,0:T(8,128)(2,1)} %shard_map.298.refs_0_), channel_id=1, source_target_pairs={{0,2},{2,4},{4,6},{6,0},{1,3},{3,5},{5,7},{7,1},{8,10},{10,12},{12... | collective-permute-start | bytes 1769480 | tf_op jit(solution)/shard_map/ppermute | solution.py:31
  51.5 24.6 %collective-permute-start.4 = (bf16[4,32,2304]{2,1,0:T(8,128)(2,1)}, bf16[4,32,2304]{2,1,0:T(8,128)(2,1)}, u32[]{:S(2)}, u32[]{:S(2)}) collective-permute-start(bf16[4,32,2304]{2,1,0:T(8,128)(2,1)} %shard_map.298.refs_0_), channel_id=1, source_target_pairs={{0,6},{2,0},{4,2},{6,4},{1,7},{3,1},{5,3},{7,5},{8,14},{10,8},{12,... | collective-permute-start | bytes 1769480 | tf_op jit(solution)/shard_map/ppermute | solution.py:31
  53.7 22.3 %collective-permute-start.10 = (bf16[4,32,2304]{2,1,0:T(8,128)(2,1)}, bf16[4,32,2304]{2,1,0:T(8,128)(2,1)}, u32[]{:S(2)}, u32[]{:S(2)}) collective-permute-start(bf16[4,32,2304]{2,1,0:T(8,128)(2,1)} %shard_map.299.refs_4_), channel_id=1, source_target_pairs={{0,2},{2,4},{4,6},{6,0},{1,3},{3,5},{5,7},{7,1},{8,10},{10,12},{12... | collective-permute-start | bytes 1769480 | tf_op jit(solution)/shard_map/ppermute | solution.py:31
  76.0 24.4 %collective-permute-start.24 = (bf16[4,32,2304]{2,1,0:T(8,128)(2,1)}, bf16[4,32,2304]{2,1,0:T(8,128)(2,1)}, u32[]{:S(2)}, u32[]{:S(2)}) collective-permute-start(bf16[4,32,2304]{2,1,0:T(8,128)(2,1)} %shard_map.301.refs_12_), channel_id=1, source_target_pairs={{0,32},{32,64},{64,96},{96,0},{1,33},{33,65},{65,97},{97,1},{2,34}... | collective-permute-start | bytes 1769480 | tf_op jit(solution)/shard_map/ppermute | solution.py:31
  76.0 24.4 %collective-permute-start.25 = (bf16[4,32,2304]{2,1,0:T(8,128)(2,1)}, bf16[4,32,2304]{2,1,0:T(8,128)(2,1)}, u32[]{:S(2)}, u32[]{:S(2)}) collective-permute-start(bf16[4,32,2304]{2,1,0:T(8,128)(2,1)} %shard_map.301.refs_12_), channel_id=1, source_target_pairs={{0,96},{32,0},{64,32},{96,64},{1,97},{33,1},{65,33},{97,65},{2,98}... | collective-permute-start | bytes 1769480 | tf_op jit(solution)/shard_map/ppermute | solution.py:31
  83.4 21.4 %collective-permute-start.32 = (bf16[128,2048]{1,0:T(8,128)(2,1)}, bf16[128,2048]{1,0:T(8,128)(2,1)}, u32[]{:S(2)}, u32[]{:S(2)}) collective-permute-start(bf16[128,2048]{1,0:T(8,128)(2,1)} %copy-done.68), channel_id=1, source_target_pairs={{0,8},{8,0},{1,9},{9,1},{2,10},{10,2},{3,11},{11,3},{4,12},{12,4},... | collective-permute-start | bytes 1572872 | tf_op jit(solution)/shard_map/ppermute | solution.py:31
  87.8 17.1 %collective-permute-start.5 = (bf16[4,32,2304]{2,1,0:T(8,128)(2,1)}, bf16[4,32,2304]{2,1,0:T(8,128)(2,1)}, u32[]{:S(2)}, u32[]{:S(2)}) collective-permute-start(bf16[4,32,2304]{2,1,0:T(8,128)(2,1)} %collective-permute-done.3.refs_1_), channel_id=1, source_target_pairs={{0,2},{2,4},{4,6},{6,0},{1,3},{3,5},{5,7},{7,1},{8,10},{10,12},{12... | collective-permute-start | bytes 1769480 | tf_op jit(solution)/shard_map/ppermute | solution.py:31
  87.8 17.1 %collective-permute-start.12 = (bf16[4,32,2304]{2,1,0:T(8,128)(2,1)}, bf16[4,32,2304]{2,1,0:T(8,128)(2,1)}, u32[]{:S(2)}, u32[]{:S(2)}) collective-permute-start(bf16[4,32,2304]{2,1,0:T(8,128)(2,1)} %collective-permute-done.11.refs_6_), channel_id=1, source_target_pairs={{0,6},{2,0},{4,2},{6,4},{1,7},{3,1},{5,3},{7,5},{8,14},{10,8},{12,... | collective-permute-start | bytes 1769480 | tf_op jit(solution)/shard_map/ppermute | solution.py:31
  114.0 73.6 %all-to-all-start = ((bf16[64,16,2048]{2,1,0:T(8,128)(2,1)}), bf16[64,16,2048]{2,1,0:T(8,128)(2,1)}, u32[]{:S(2)}, u32[]{:S(2)}) async-start(bf16[64,16,2048]{2,1,0:T(8,128)(2,1)} %bitcast.110), calls=%async_computation | async-start | bytes 8388608 | tf_op jit(solution)/shard_map/all_to_all | solution.py:662
  122.8 134.2 %all-gather.2.cloned.1.call-start = ((), (), s32[]{:S(2)}) async-start(), calls=%async_computation.5 | async-start | bytes 5013504 | tf_op jit(solution)/shard_map/all_gather | solution.py:684
  136.2 46.0 %collective-permute-start.35 = (bf16[128,1024]{1,0:T(8,128)(2,1)}, bf16[128,1024]{1,0:T(8,128)(2,1)S(1)}, u32[]{:S(2)}, u32[]{:S(2)}) collective-permute-start(bf16[128,1024]{1,0:T(8,128)(2,1)} %get-tuple-element.192), channel_id=1, source_target_pairs={{0,2},{2,4},{4,6},{6,0},{1,3},{3,5},{5,7},{7,1},{8,10},{10,12},{12... | collective-permute-start | bytes 786440 | tf_op jit(solution)/shard_map/ppermute | solution.py:31
  137.6 49.5 %collective-permute-start.36 = (bf16[128,1024]{1,0:T(8,128)(2,1)}, bf16[128,1024]{1,0:T(8,128)(2,1)S(1)}, u32[]{:S(2)}, u32[]{:S(2)}) collective-permute-start(bf16[128,1024]{1,0:T(8,128)(2,1)} %get-tuple-element.193), channel_id=1, source_target_pairs={{0,4},{2,6},{4,0},{6,2},{1,5},{3,7},{5,1},{7,3},{8,12},{10,14},{12... | collective-permute-start | bytes 786440 | tf_op jit(solution)/shard_map/ppermute | solution.py:31
  140.0 47.6 %collective-permute-start.37 = (bf16[128,1024]{1,0:T(8,128)(2,1)}, bf16[128,1024]{1,0:T(8,128)(2,1)}, u32[]{:S(2)}, u32[]{:S(2)}) collective-permute-start(bf16[128,1024]{1,0:T(8,128)(2,1)} %get-tuple-element.194), channel_id=1, source_target_pairs={{0,6},{2,0},{4,2},{6,4},{1,7},{3,1},{5,3},{7,5},{8,14},{10,8},{12,... | collective-permute-start | bytes 786440 | tf_op jit(solution)/shard_map/ppermute | solution.py:31
  249.0 61.6 %all-to-all-start.1 = ((bf16[64,16,2048]{2,1,0:T(8,128)(2,1)}), bf16[64,16,2048]{2,1,0:T(8,128)(2,1)}, u32[]{:S(2)}, u32[]{:S(2)}) async-start(bf16[64,16,2048]{2,1,0:T(8,128)(2,1)} %bitcast.111), calls=%async_computation.1 | async-start | bytes 8388608 | tf_op jit(solution)/shard_map/all_to_all | solution.py:662
  256.9 169.0 %reduce-scatter.2.cloned.1.call-start = ((), (), s32[]{:S(2)}) async-start(), calls=%async_computation.6 | async-start | bytes 5013504 | tf_op jit(solution)/shard_map/reduce_scatter | solution.py:773
  280.7 69.1 %collective-permute-start.49 = (bf16[128,2048]{1,0:T(8,128)(2,1)}, bf16[128,2048]{1,0:T(8,128)(2,1)}, u32[]{:S(2)}, u32[]{:S(2)}) collective-permute-start(bf16[128,2048]{1,0:T(8,128)(2,1)} %get-tuple-element.226), channel_id=1, source_target_pairs={{0,8},{8,0},{1,9},{9,1},{2,10},{10,2},{3,11},{11,3},{4,12},{12,4},... | collective-permute-start | bytes 1572872 | tf_op jit(solution)/shard_map/ppermute | solution.py:31
  282.9 66.9 %collective-permute-start.51 = (bf16[128,2048]{1,0:T(8,128)(2,1)}, bf16[128,2048]{1,0:T(8,128)(2,1)}, u32[]{:S(2)}, u32[]{:S(2)}) collective-permute-start(bf16[128,2048]{1,0:T(8,128)(2,1)} %add_convert_fusion.9), channel_id=1, source_target_pairs={{0,16},{16,0},{1,17},{17,1},{2,18},{18,2},{3,19},{19,3},{4,20},{20... | collective-permute-start | bytes 1572872 | tf_op jit(solution)/shard_map/ppermute | solution.py:31
  338.7 66.8 %all-to-all-start.2 = ((bf16[64,16,2048]{2,1,0:T(8,128)(2,1)}), bf16[64,16,2048]{2,1,0:T(8,128)(2,1)}, u32[]{:S(2)}, u32[]{:S(2)}) async-start(bf16[64,16,2048]{2,1,0:T(8,128)(2,1)} %bitcast.112), calls=%async_computation.2 | async-start | bytes 8388608 | tf_op jit(solution)/shard_map/all_to_all | solution.py:662
  464.4 59.1 %all-to-all-start.3 = ((bf16[64,16,2048]{2,1,0:T(8,128)(2,1)}), bf16[64,16,2048]{2,1,0:T(8,128)(2,1)}, u32[]{:S(2)}, u32[]{:S(2)}) async-start(bf16[64,16,2048]{2,1,0:T(8,128)(2,1)} %bitcast.120), calls=%async_computation.4 | async-start | bytes 8388608 | tf_op jit(solution)/shard_map/all_to_all | solution.py:662
  472.9 52.7 %collective-permute-start.47 = (bf16[128,2048]{1,0:T(8,128)(2,1)}, bf16[128,2048]{1,0:T(8,128)(2,1)}, u32[]{:S(2)}, u32[]{:S(2)}) collective-permute-start(bf16[128,2048]{1,0:T(8,128)(2,1)} %get-tuple-element.233), channel_id=1, source_target_pairs={{0,8},{8,0},{1,9},{9,1},{2,10},{10,2},{3,11},{11,3},{4,12},{12,4},... | collective-permute-start | bytes 1572872 | tf_op jit(solution)/shard_map/ppermute | solution.py:31
  473.4 99.4 %collective-permute-start.46 = (bf16[128,2048]{1,0:T(8,128)(2,1)}, bf16[128,2048]{1,0:T(8,128)(2,1)}, u32[]{:S(2)}, u32[]{:S(2)}) collective-permute-start(bf16[128,2048]{1,0:T(8,128)(2,1)} %get-tuple-element.231), channel_id=1, source_target_pairs={{0,8},{8,0},{1,9},{9,1},{2,10},{10,2},{3,11},{11,3},{4,12},{12,4},... | collective-permute-start | bytes 1572872 | tf_op jit(solution)/shard_map/ppermute | solution.py:31
  483.8 45.3 %collective-permute-start.64 = (bf16[128,2048]{1,0:T(8,128)(2,1)}, bf16[128,2048]{1,0:T(8,128)(2,1)}, u32[]{:S(2)}, u32[]{:S(2)}) collective-permute-start(bf16[128,2048]{1,0:T(8,128)(2,1)} %get-tuple-element.276), channel_id=1, source_target_pairs={{0,8},{8,0},{1,9},{9,1},{2,10},{10,2},{3,11},{11,3},{4,12},{12,4},... | collective-permute-start | bytes 1572872 | tf_op jit(solution)/shard_map/ppermute | solution.py:31
  527.5 79.2 %collective-permute-start.48 = (bf16[128,2048]{1,0:T(8,128)(2,1)}, bf16[128,2048]{1,0:T(8,128)(2,1)}, u32[]{:S(2)}, u32[]{:S(2)}) collective-permute-start(bf16[128,2048]{1,0:T(8,128)(2,1)} %add_convert_fusion.10), channel_id=1, source_target_pairs={{0,16},{16,0},{1,17},{17,1},{2,18},{18,2},{3,19},{19,3},{4,20},{20... | collective-permute-start | bytes 1572872 | tf_op jit(solution)/shard_map/ppermute | solution.py:31
  527.5 46.5 %collective-permute-start.66 = (bf16[4,32,2304]{2,1,0:T(8,128)(2,1)}, bf16[4,32,2304]{2,1,0:T(8,128)(2,1)S(1)}, u32[]{:S(2)}, u32[]{:S(2)}) collective-permute-start(bf16[4,32,2304]{2,1,0:T(8,128)(2,1)} %get-tuple-element.278), channel_id=1, source_target_pairs={{0,6},{2,0},{4,2},{6,4},{1,7},{3,1},{5,3},{7,5},{8,14},{10,8},{12,... | collective-permute-start | bytes 1769480 | tf_op jit(solution)/shard_map/ppermute | solution.py:31
  529.1 45.2 %collective-permute-start.69 = (bf16[4,32,2304]{2,1,0:T(8,128)(2,1)}, bf16[4,32,2304]{2,1,0:T(8,128)(2,1)S(1)}, u32[]{:S(2)}, u32[]{:S(2)}) collective-permute-start(bf16[4,32,2304]{2,1,0:T(8,128)(2,1)} %get-tuple-element.282), channel_id=1, source_target_pairs={{0,2},{2,4},{4,6},{6,0},{1,3},{3,5},{5,7},{7,1},{8,10},{10,12},{12... | collective-permute-start | bytes 1769480 | tf_op jit(solution)/shard_map/ppermute | solution.py:31
  572.8 36.9 %collective-permute-start.76 = (bf16[4,32,2304]{2,1,0:T(8,128)(2,1)}, bf16[4,32,2304]{2,1,0:T(8,128)(2,1)S(1)}, u32[]{:S(2)}, u32[]{:S(2)}) collective-permute-start(bf16[4,32,2304]{2,1,0:T(8,128)(2,1)} %get-tuple-element.292), channel_id=1, source_target_pairs={{0,96},{32,0},{64,32},{96,64},{1,97},{33,1},{65,33},{97,65},{2,98}... | collective-permute-start | bytes 1769480 | tf_op jit(solution)/shard_map/ppermute | solution.py:31
  574.1 35.7 %collective-permute-start.79 = (bf16[4,32,2304]{2,1,0:T(8,128)(2,1)}, bf16[4,32,2304]{2,1,0:T(8,128)(2,1)S(1)}, u32[]{:S(2)}, u32[]{:S(2)}) collective-permute-start(bf16[4,32,2304]{2,1,0:T(8,128)(2,1)} %get-tuple-element.296), channel_id=1, source_target_pairs={{0,32},{32,64},{64,96},{96,0},{1,33},{33,65},{65,97},{97,1},{2,34}... | collective-permute-start | bytes 1769480 | tf_op jit(solution)/shard_map/ppermute | solution.py:31
  588.5 24.8 %collective-permute-start.78 = (bf16[4,32,2304]{2,1,0:T(8,128)(2,1)S(1)}, bf16[4,32,2304]{2,1,0:T(8,128)(2,1)S(1)}, u32[]{:S(2)}, u32[]{:S(2)}) collective-permute-start(bf16[4,32,2304]{2,1,0:T(8,128)(2,1)S(1)} %add_convert_fusion.2), channel_id=1, source_target_pairs={{0,32},{32,64},{64,96},{96,0},{1,33},{33,65},{65,97},{97,1},{2,34}... | collective-permute-start | bytes 1769480 | tf_op jit(solution)/shard_map/ppermute | solution.py:31
  596.2 17.3 %collective-permute-start.81 = (bf16[4,32,2304]{2,1,0:T(8,128)(2,1)S(1)}, bf16[4,32,2304]{2,1,0:T(8,128)(2,1)}, u32[]{:S(2)}, u32[]{:S(2)}) collective-permute-start(bf16[4,32,2304]{2,1,0:T(8,128)(2,1)S(1)} %add_convert_fusion.1), channel_id=1, source_target_pairs={{0,96},{32,0},{64,32},{96,64},{1,97},{33,1},{65,33},{97,65},{2,98}... | collective-permute-start | bytes 1769480 | tf_op jit(solution)/shard_map/ppermute | solution.py:31
  613.3 41.9 %collective-permute-start.63 = (bf16[128,2048]{1,0:T(8,128)(2,1)S(1)}, bf16[128,2048]{1,0:T(8,128)(2,1)S(1)}, u32[]{:S(2)}, u32[]{:S(2)}) collective-permute-start(bf16[128,2048]{1,0:T(8,128)(2,1)S(1)} %add_convert_fusion.7), channel_id=1, source_target_pairs={{0,1},{1,0},{2,3},{3,2},{4,5},{5,4},{6,7},{7,6},{8,9},{9,8},{10,11... | collective-permute-start | bytes 1572872 | tf_op jit(solution)/shard_map/ppermute | solution.py:31
  625.6 18.7 %collective-permute-start.75 = (bf16[32,2304]{1,0:T(8,128)(2,1)}, bf16[32,2304]{1,0:T(8,128)(2,1)S(1)}, u32[]{:S(2)}, u32[]{:S(2)}) collective-permute-start(bf16[32,2304]{1,0:T(8,128)(2,1)} %get-tuple-element.290), channel_id=1, source_target_pairs={{0,16},{16,0},{1,17},{17,1},{2,18},{18,2},{3,19},{19,3},{4,20},{20... | collective-permute-start | bytes 442376 | tf_op jit(solution)/shard_map/ppermute | solution.py:31
  (145 other events, 1970.5 us)
Sparse Core Ops, SparseCore 0:
  125.8 92.3 all-gather.1
  280.9 118.9 reduce-scatter.1
